TPU v7x, 1024 devices: a whole 8x8x8 slice. The times are simulated.
1024 devices in a mesh: seg: 64 (over x, z), curve: 16 (over y, core).
Axes of the slice: x: 8, y: 8, z: 8, core: 2. Of those that a mesh axis runs over, the one named last changes fastest.
Arguments:
- state: float32 [2048, 5, 16, 256], P(('seg', 'curve')), as said below
- new_slot: int32 [2048], P(('seg', 'curve')), may hold values from 0 to 2047, as said below
- neighbours: int32 [2048, 6], P(('seg', 'curve')), may hold values from 0 to 2047, as said below
Outputs:
- new_state: float32 [2048, 5, 16, 256], P(('seg', 'curve'))
Inputs may be any that keep to these rules, and one draw needn't show every extreme that they name: `state`: densities and pressures are positive in every cell. Each box keeps its segment (32 consecutive indices, in the old and in the new order). The 2 consecutive boxes of a device go as 1 boxes to each of exactly 2 devices of its segment (possibly itself) and none to the others; new_slot is a permutation, so every device receives exactly 2 boxes. A periodic grid of boxes; each face's neighbour names the box back across the opposite face. The -z and +z neighbours of a box are owned by its own device; its -x and +x neighbours by its own device or by the device at the same curve place of the segment before (for -x) or after (for +x), cyclically; its -y and +y neighbours lie on other devices of its own segment, all 2 boxes of a device having their -y neighbours on one device and their +y neighbours on another.
All inputs are finite; a program needn't handle non-finite values.
Results may differ from a plain program's by a relative error of at most 0.00002.
Values sent between devices are 32-bit elements; how exact they have to be, the bound alone decides.
No kernel may reach another device: no remote copies, remote signals or barrier semaphores. Data moves between devices by JAX's collectives and lax.ppermute only.
A program may use at most 32 MiB of HBM per device.

v0:
```python
import jax
import jax.numpy as jnp
from jax import lax
from jax.sharding import PartitionSpec as P

gamma_ratio = 1.4
courant = 0.3


def padded(value, sides, width):
    for axis, dim in sides:
        size, length = (lax.axis_size(axis), value.shape[dim])
        up = [(i, (i + 1) % size) for i in range(size)]
        down = [(j, i) for i, j in up]
        last = lax.slice_in_dim(value, length - width, length, axis=dim)
        first = lax.slice_in_dim(value, 0, width, axis=dim)
        before = lax.ppermute(last, axis, up)
        after = lax.ppermute(first, axis, down)
        value = jnp.concatenate([before, value, after], axis=dim)
    return value


def euler_flux(conserved, axis_num):
    density = conserved[0]
    moment = conserved[1:4]
    velocity = moment[axis_num] / density
    kinetic = (
        0.5 * (moment[0] * moment[0] + moment[1] * moment[1] + moment[2] * moment[2]) / density
    )
    pressure = (gamma_ratio - 1.0) * (conserved[4] - kinetic)
    sound_speed = jnp.sqrt(gamma_ratio * pressure / density)
    pieces = [moment[axis_num]]
    for index in range(3):
        product_term = moment[index] * velocity
        if index == axis_num:
            product_term = product_term + pressure
        pieces.append(product_term)
    pieces.append((conserved[4] + pressure) * velocity)
    return (jnp.stack(pieces), jnp.abs(velocity) + sound_speed)


def wave_speed(cube_state):
    density = cube_state[0]
    moment = cube_state[1:4]
    kinetic = (
        0.5 * (moment[0] * moment[0] + moment[1] * moment[1] + moment[2] * moment[2]) / density
    )
    pressure = (gamma_ratio - 1.0) * (cube_state[4] - kinetic)
    sound_speed = jnp.sqrt(gamma_ratio * pressure / density)
    largest = jnp.maximum(jnp.maximum(jnp.abs(moment[0]), jnp.abs(moment[1])), jnp.abs(moment[2]))
    return jnp.max(largest / density + sound_speed)


def rusanov(left, right, axis_num):
    flux_left, speed_left = euler_flux(left, axis_num)
    flux_right, speed_right = euler_flux(right, axis_num)
    fastest = jnp.maximum(speed_left, speed_right)
    return 0.5 * (flux_left + flux_right) - 0.5 * fastest[None] * (right - left)


def advance(box_flat, ghosts, step_size):
    edge = box_flat.shape[1]
    plane_cells = box_flat.shape[2]
    flat_pos = jnp.arange(plane_cells, dtype=jnp.int32)[None, None, :]
    lower_x = ghosts[0][:, None, :]
    upper_x = ghosts[1][:, None, :]
    extended = jnp.concatenate([lower_x, box_flat, upper_x], axis=1)
    fluxes = rusanov(extended[:, : edge + 1], extended[:, 1:], 0)
    change = fluxes[:, 1:] - fluxes[:, :edge]
    for axis_num in (1, 2):
        stride = edge if axis_num == 1 else 1
        low_plane = ghosts[2 * axis_num].reshape(5, edge, edge)
        high_plane = ghosts[2 * axis_num + 1].reshape(5, edge, edge)
        if axis_num == 1:
            low_full = jnp.tile(low_plane, (1, 1, edge))
            high_full = jnp.tile(high_plane, (1, 1, edge))
            along = flat_pos // edge
        else:
            low_full = jnp.repeat(low_plane, edge, axis=2)
            high_full = jnp.repeat(high_plane, edge, axis=2)
            along = flat_pos % edge
        right = jnp.where(along == edge - 1, high_full, jnp.roll(box_flat, -stride, axis=2))
        upper_flux = rusanov(box_flat, right, axis_num)
        edge_flux = rusanov(low_full, box_flat, axis_num)
        lower_flux = jnp.where(along == 0, edge_flux, jnp.roll(upper_flux, stride, axis=2))
        change = change + (upper_flux - lower_flux)
    return box_flat - step_size * change


def faces_of(box_flat):
    edge = box_flat.shape[1]
    plane_cells = box_flat.shape[2]
    pieces = [
        box_flat[:, 0],
        box_flat[:, -1],
        box_flat[:, :, 0:edge],
        box_flat[:, :, plane_cells - edge :],
        box_flat[:, :, 0::edge],
        box_flat[:, :, edge - 1 :: edge],
    ]
    return jnp.stack([piece.reshape(5, plane_cells) for piece in pieces])


def local(state, new_slot, neighbours):
    own_count = state.shape[0]
    plane_cells = state.shape[3]
    curve_count = lax.axis_size("curve")
    seg_boxes = own_count * curve_count
    seg_id = lax.axis_index("seg")
    curve_id = lax.axis_index("curve")
    first_id = (seg_id * curve_count + curve_id) * own_count
    per_peer = max(1, own_count // curve_count)
    slot_count = curve_count * per_peer
    local_fastest = jnp.max(jax.vmap(wave_speed)(state))
    fastest = lax.pmax(local_fastest, ("seg", "curve"))
    step_size = courant / fastest
    target_dev = new_slot // own_count % curve_count
    positions = jnp.arange(own_count, dtype=jnp.int32)
    earlier = (target_dev[:, None] == target_dev[None, :]) & (
        positions[:, None] > positions[None, :]
    )
    order_rank = jnp.sum(earlier.astype(jnp.int32), axis=1)
    target_row = target_dev * per_peer + order_rank
    slots = jnp.arange(slot_count, dtype=jnp.int32)
    matches = target_row[None, :] == slots[:, None]
    present = jnp.any(matches, axis=1)
    chosen = jnp.sum(jnp.where(matches, positions[None, :], 0), axis=1)
    outgoing = jnp.take(state, chosen, axis=0)
    outgoing_ids = jnp.where(present, jnp.take(new_slot, chosen), -1)
    arrived, arrived_ids = (
        lax.all_to_all(outgoing, "curve", split_axis=0, concat_axis=0, tiled=True),
        lax.all_to_all(outgoing_ids, "curve", split_axis=0, concat_axis=0, tiled=True),
    )
    wanted = first_id + positions
    placed = arrived_ids[None, :] == wanted[:, None]
    source_row = jnp.sum(jnp.where(placed, slots[None, :], 0), axis=1)
    moved = jnp.take(arrived, source_row, axis=0)
    new_faces = jax.vmap(faces_of)(moved)
    sides = jnp.stack([new_faces[:, 0], new_faces[:, 1]])
    widened = padded(sides, (("seg", 0),), 1)
    edge_flat = jnp.stack([widened[0], widened[3]]).reshape(2 * own_count, 5, plane_cells)
    face_index = jnp.arange(6, dtype=jnp.int32)[None, :]
    opposite = jnp.bitwise_xor(face_index, 1)
    other_seg = neighbours // seg_boxes
    local_index = neighbours % seg_boxes
    owner = local_index // own_count
    owner_slot = local_index % own_count
    inside = other_seg == seg_id
    edge_row = face_index % 2 * own_count + owner_slot
    edge_ghost = jnp.take(edge_flat, edge_row, axis=0)
    own_table = lax.all_gather(new_faces, "curve", axis=0, tiled=True)
    box_row = owner * own_count + owner_slot
    own_flat = own_table.reshape(seg_boxes * 6, 5, plane_cells)
    own_ghost = jnp.take(own_flat, box_row * 6 + opposite, axis=0)
    ghosts = jnp.where(inside[:, :, None, None], own_ghost, edge_ghost)
    result = jax.vmap(advance, in_axes=(0, 0, None))(moved, ghosts, step_size)
    return result


def solution(mesh):
    placed = (P(("seg", "curve"), None, None, None), P(("seg", "curve")), P(("seg", "curve"), None))
    return jax.shard_map(
        local,
        mesh=mesh,
        in_specs=placed,
        out_specs=P(("seg", "curve"), None, None, None),
        check_vma=False,
    )
```

profile of v0, /device:TPU:1, one launch (start us, length us, event | category | flops | bytes accessed | tf_op | source)
XLA Modules:
  0.0 216.5 jit_solution(14595023146161858177)
XLA Ops:
  0.0 0.7 and_select_fusion.8
  0.9 0.7 fusion.148
  1.7 1.4 fusion.147
  3.1 1.3 bitcast_select_fusion
  4.4 0.7 copy.320
  5.0 17.4 %all-to-all-start = ((s32[16,1,1]{2,1,0:T(1,128)}), s32[16,1,1]{2,1,0:T(1,128)S(1)}, u32[]{:S(2)}, u32[]{:S(2)}) async-start(s32[16,1,1]{2,1,0:T(1,128)} %copy.320), calls=%async_computation | async-start | bytes 16384 | tf_op jit(solution)/shard_map/all_to_all | solution.py:132
  22.5 1.5 gather_fusion
  24.0 1.2 broadcast_select_fusion
  25.3 4.2 %all-to-all-done = s32[16,1,1]{2,1,0:T(1,128)S(1)} async-done(((s32[16,1,1]{2,1,0:T(1,128)}), s32[16,1,1]{2,1,0:T(1,128)S(1)}, u32[]{:S(2)}, u32[]{:S(2)}) %all-to-all-start) | async-done | bytes 96 | tf_op jit(solution)/shard_map/all_to_all | solution.py:132
  29.4 4.2 %all-to-all-start.1 = ((f32[16,5,16,256]{3,2,1,0:T(8,128)}), f32[16,5,16,256]{3,2,1,0:T(8,128)S(1)}, u32[]{:S(2)}, u32[]{:S(2)}) async-start(f32[16,5,16,256]{3,2,1,0:T(8,128)} %broadcast_select_fusion), calls=%async_computation.1 | async-start | bytes 2621440 | tf_op jit(solution)/shard_map/all_to_all | solution.py:131
  33.6 0.6 fusion.123
  34.2 139.8 %pmax.7 = f32[]{:T(128)} all-reduce(f32[]{:T(128)} %fusion.123), channel_id=1, replica_groups=mesh['seg'=64,'curve'=16] {'seg','curve'}, use_global_device_ids=true, to_apply=%region_5.6 | all-reduce | flops 1 | bytes 8 | tf_op jit(solution)/shard_map/pmax | solution.py:115
  176.0 0.6 gather_fusion.1
  177.3 0.5 slice.178
  178.4 20.1 %all_gather.3 = f32[32,6,5,256]{3,1,2,0:T(8,128)S(1)} all-gather(f32[2,6,5,256]{3,1,2,0:T(8,128)S(1)} %bitcast.834), channel_id=1, replica_groups=mesh['seg'=64,'curve'=16] {'curve'}, dimensions={0}, use_global_device_ids=true | all-gather | bytes 1044480 | tf_op jit(solution)/shard_map/all_gather | solution.py:151
  198.7 2.1 collective-permute-start
  200.8 6.5 %collective-permute-start.1 = (f32[1,2,5,256]{3,0,2,1:T(1,128)S(1)}, f32[1,2,5,256]{3,0,2,1:T(1,128)S(1)}, u32[]{:S(2)}, u32[]{:S(2)}) collective-permute-start(f32[1,2,5,256]{3,0,2,1:T(1,128)S(1)} %get-tuple-element.54), channel_id=1, source_target_pairs={{16,0},{32,16},{48,32},{64,48},{80,64},{96,80},{112,96},{128,112},... | collective-permute-start | bytes 30728 | tf_op jit(solution)/shard_map/ppermute | solution.py:18
  208.4 0.6 gather_fusion.2
  209.0 0.6 gather_fusion.3
  210.4 0.6 reshape.1472
  211.3 0.6 tile.25
  212.0 0.6 tile.22
  213.3 0.6 reshape.1471
  215.6 0.9 fusion.8
  (117 shorter events, 7.4 us)
Async XLA Ops:
  5.0 24.4 %all-to-all-start = ((s32[16,1,1]{2,1,0:T(1,128)}), s32[16,1,1]{2,1,0:T(1,128)S(1)}, u32[]{:S(2)}, u32[]{:S(2)}) async-start(s32[16,1,1]{2,1,0:T(1,128)} %copy.320), calls=%async_computation | async-start | bytes 16384 | tf_op jit(solution)/shard_map/all_to_all | solution.py:132
  25.3 8.3 %copy-start = (f32[2,5,16,256]{3,2,1,0:T(8,128)S(1)}, f32[2,5,16,256]{3,2,1,0:T(8,128)}, u32[]{:S(2)}) copy-start(f32[2,5,16,256]{3,2,1,0:T(8,128)} %param.3) | copy-start | bytes 491524
  25.3 148.8 %copy-start.2 = (s32[2,6]{1,0:T(2,128)S(1)}, s32[2,6]{1,0:T(2,128)}, u32[]{:S(2)}) copy-start(s32[2,6]{1,0:T(2,128)} %param.5) | copy-start | bytes 148
  29.4 146.6 %all-to-all-start.1 = ((f32[16,5,16,256]{3,2,1,0:T(8,128)}), f32[16,5,16,256]{3,2,1,0:T(8,128)S(1)}, u32[]{:S(2)}, u32[]{:S(2)}) async-start(f32[16,5,16,256]{3,2,1,0:T(8,128)} %broadcast_select_fusion), calls=%async_computation.1 | async-start | bytes 2621440 | tf_op jit(solution)/shard_map/all_to_all | solution.py:131
  176.7 31.3 %copy-start.1 = (f32[2,5,16,256]{3,2,1,0:T(8,128)}, f32[2,5,16,256]{3,2,1,0:T(8,128)S(1)}, u32[]{:S(2)}) copy-start(f32[2,5,16,256]{3,2,1,0:T(8,128)S(1)} %broadcast_select_fusion.1) | copy-start | bytes 491524
  198.7 10.3 %collective-permute-start = (f32[1,2,5,256]{3,0,2,1:T(1,128)S(1)}, f32[1,2,5,256]{3,0,2,1:T(1,128)S(1)}, u32[]{:S(2)}, u32[]{:S(2)}) collective-permute-start(f32[1,2,5,256]{3,0,2,1:T(1,128)S(1)} %get-tuple-element.53), channel_id=1, source_target_pairs={{0,16},{16,32},{32,48},{48,64},{64,80},{80,96},{96,112},{112,128},... | collective-permute-start | bytes 30728 | tf_op jit(solution)/shard_map/ppermute | solution.py:17
  200.8 8.2 %collective-permute-start.1 = (f32[1,2,5,256]{3,0,2,1:T(1,128)S(1)}, f32[1,2,5,256]{3,0,2,1:T(1,128)S(1)}, u32[]{:S(2)}, u32[]{:S(2)}) collective-permute-start(f32[1,2,5,256]{3,0,2,1:T(1,128)S(1)} %get-tuple-element.54), channel_id=1, source_target_pairs={{16,0},{32,16},{48,32},{64,48},{80,64},{96,80},{112,96},{128,112},... | collective-permute-start | bytes 30728 | tf_op jit(solution)/shard_map/ppermute | solution.py:18
  212.9 1.0 slice-start
where the time goes:
time: 217 us; the launch traced here: 216 us
  blocking collectives  160 us (74%)
  starting transfers between devices  30.2 us (14%)
  local copies, waits for them, and re-layouts  12 us (6%)
  other arithmetic  8.76 us (4%)
  waiting for transfers between devices  4.17 us (2%)
    pmax x1, blocking collectives, local(): fastest = lax.pmax(local_fastest, ('seg', 'curve'))  140 us
    all_gather x1, blocking collectives, local(): own_table = lax.all_gather(new_faces, 'curve', axis=0, tiled=True)  20.1 us
    all_to_all x1, starting transfers between devices, local(): lax.all_to_all(outgoing_ids, 'curve', split_axis=0, concat_axis=0, tiled=...  17.4 us
    ppermute x1, starting transfers between devices, padded(): after = lax.ppermute(first, axis, down)  6.46 us
  transfers between devices with their start and end apart: 4, of which 1 were waited for; matrix products, arithmetic and copies ran while one was open for 3% of the time, Pallas kernels for 0%

commit v1 on v0

v1 whole, which is shorter than its diff:
```python
import jax
import jax.numpy as jnp
from jax import lax
from jax.experimental import pallas as pl
from jax.experimental.pallas import tpu as pltpu
from jax.sharding import PartitionSpec as P

gamma_ratio = 1.4
courant = 0.3

LANES = 128
ROWS = 10
SLOT = 24

vmem = pl.BlockSpec(memory_space=pltpu.VMEM)
smem = pl.BlockSpec(memory_space=pltpu.SMEM)


def lane_index(shape):
    return lax.broadcasted_iota(jnp.int32, shape, len(shape) - 1)


def primitives(cell):
    inverse = 1.0 / cell[0]
    velocity = [cell[1 + d] * inverse for d in range(3)]
    kinetic = 0.5 * (cell[1] * velocity[0] + cell[2] * velocity[1] + cell[3] * velocity[2])
    pressure = (gamma_ratio - 1.0) * (cell[4] - kinetic)
    sound = jnp.sqrt(gamma_ratio * pressure * inverse)
    return velocity, pressure, sound


def side(cell, axis_num):
    velocity, pressure, sound = primitives(cell)
    along = velocity[axis_num]
    flux = [cell[1 + axis_num]]
    for d in range(3):
        term = cell[1 + d] * along
        flux.append(term + pressure if d == axis_num else term)
    flux.append((cell[4] + pressure) * along)
    return flux, jnp.abs(along) + sound


def axis_change(cell, speed, below, above, axis_num):
    flux_below, speed_below = side(below, axis_num)
    flux_above, speed_above = side(above, axis_num)
    speed_below = jnp.maximum(speed, speed_below)
    speed_above = jnp.maximum(speed, speed_above)
    return [
        0.5 * (flux_above[v] - flux_below[v])
        - 0.5 * (speed_above * (above[v] - cell[v]) - speed_below * (cell[v] - below[v]))
        for v in range(5)
    ]


def pack_kernel(slot_ref, near_ref, state_ref, out_ref):
    count = out_ref.shape[0] // SLOT
    boxes = 2 * count
    best = None
    for box in range(2):
        cell = [state_ref[box, v] for v in range(5)]
        for v in range(5):
            for half in range(2):
                row = ROWS * box + 2 * v + half
                out_ref[pl.ds(row, count, stride=SLOT), :] = cell[v][:, LANES * half : LANES * (half + 1)]
        velocity, _, sound = primitives(cell)
        largest = jnp.maximum(jnp.maximum(jnp.abs(velocity[0]), jnp.abs(velocity[1])), jnp.abs(velocity[2]))
        speed = largest + sound
        best = speed if best is None else jnp.maximum(best, speed)
    best = jnp.max(jnp.max(best, axis=0, keepdims=True), axis=1, keepdims=True)

    def place(index):
        local = lax.rem(index, boxes)
        return lax.rem(local, 2) * count + lax.div(local, 2)

    values = [place(slot_ref[0]), place(slot_ref[1])]
    for box in range(2):
        values += [place(near_ref[box, 2]), place(near_ref[box, 3])]
    lane = lane_index((count, LANES))
    header = jnp.where(lane == 6, jnp.broadcast_to(best, lane.shape), 0.0)
    for position, value in enumerate(values):
        header = jnp.where(lane == position, value.astype(jnp.float32), header)
    out_ref[pl.ds(20, count, stride=SLOT), :] = header
    for row in range(21, SLOT):
        out_ref[pl.ds(row, count, stride=SLOT), :] = jnp.zeros((count, LANES), jnp.float32)


def exact_dot(left, right, contract):
    return lax.dot_general(
        left,
        right,
        ((contract, (0,)), ((), ())),
        precision=lax.Precision.HIGHEST,
        preferred_element_type=jnp.float32,
    )


def route_kernel(in_ref, out_ref, best_ref):
    count = in_ref.shape[0] // SLOT
    boxes = 2 * count
    header = in_ref[pl.ds(20, count, stride=SLOT), :]
    lane = lane_index((count, LANES))
    lane_f = lane.astype(jnp.float32)
    best = jnp.max(jnp.where(lane == 6, header, 0.0), axis=0, keepdims=True)
    best = jnp.max(best, axis=1, keepdims=True)
    best_ref[...] = jnp.broadcast_to(best.reshape(1, 1, 1), best_ref.shape)

    def one_hot(first, second):
        rows = [
            jnp.where(lane_f == jnp.broadcast_to(header[:, j : j + 1], lane_f.shape), 1.0, 0.0) for j in (first, second)
        ]
        return jnp.concatenate(rows, axis=0)[:, :boxes]

    columns = []
    for row in range(ROWS):
        columns.append(
            jnp.concatenate(
                [in_ref[pl.ds(ROWS * box + row, count, stride=SLOT), :] for box in range(2)], axis=0
            )
        )
    lane2 = lane_index((boxes, LANES))
    last = jnp.zeros((boxes, LANES), jnp.float32)
    first = jnp.zeros((boxes, LANES), jnp.float32)
    for v in range(5):
        mine = (lane2 >= 16 * v) & (lane2 < 16 * (v + 1))
        last = jnp.where(mine, pltpu.roll(columns[2 * v + 1], 16 * (v + 1), 1), last)
        first = jnp.where(mine, pltpu.roll(columns[2 * v], 16 * v, 1) if v else columns[0], first)
    everything = jnp.concatenate(columns + [last, first], axis=1)
    placed = exact_dot(one_hot(0, 1), everything, (0,))
    below = exact_dot(one_hot(2, 4), placed[:, ROWS * LANES : (ROWS + 1) * LANES], (1,))
    above = exact_dot(one_hot(3, 5), placed[:, (ROWS + 1) * LANES :], (1,))
    for box in range(2):
        rows = slice(count * box, count * (box + 1))
        for row in range(ROWS):
            out_ref[pl.ds(ROWS * box + row, count, stride=SLOT), :] = placed[rows, LANES * row : LANES * (row + 1)]
        out_ref[pl.ds(20 + box, count, stride=SLOT), :] = below[rows]
        out_ref[pl.ds(22 + box, count, stride=SLOT), :] = above[rows]


def load_cells(in_ref):
    count = in_ref.shape[0] // SLOT
    return [
        jnp.stack(
            [
                in_ref[pl.ds(ROWS * box + 2 * v + half, count, stride=SLOT), :]
                for box in range(2)
                for half in range(2)
            ]
        )
        for v in range(5)
    ]


def plane_kernel(near_ref, in_ref, out_ref):
    count = in_ref.shape[0] // SLOT
    cell = load_cells(in_ref)
    velocity, _, sound = primitives(cell)
    lane = lane_index(cell[0].shape)

    ghost_low = [in_ref[pl.ds(20 + box, count, stride=SLOT), :] for box in range(2)]
    ghost_high = [in_ref[pl.ds(22 + box, count, stride=SLOT), :] for box in range(2)]
    below, above = [], []
    for v in range(5):
        low = [pltpu.roll(g, LANES - 16 * v, 1) if v else g for g in ghost_low]
        high = [pltpu.roll(g, 112 - 16 * v, 1) for g in ghost_high]
        rolled = pltpu.roll(cell[v], 16, 2)
        edge = jnp.stack([low[0], rolled[0], low[1], rolled[2]])
        below.append(jnp.where(lane < 16, edge, rolled))
        rolled = pltpu.roll(cell[v], LANES - 16, 2)
        edge = jnp.stack([rolled[1], high[0], rolled[3], high[1]])
        above.append(jnp.where(lane >= LANES - 16, edge, rolled))
    change = axis_change(cell, jnp.abs(velocity[1]) + sound, below, above, 1)

    deep = lane & 15
    below, above = [], []
    slots = [[lax.rem(near_ref[box, face], 2) for box in range(2)] for face in (4, 5)]
    for v in range(5):
        wrapped = pltpu.roll(cell[v], LANES - 15, 2)
        edge = jnp.concatenate([jnp.where(slots[0][box] == 0, wrapped[0:2], wrapped[2:4]) for box in range(2)], axis=0)
        below.append(jnp.where(deep == 0, edge, pltpu.roll(cell[v], 1, 2)))
        wrapped = pltpu.roll(cell[v], 15, 2)
        edge = jnp.concatenate([jnp.where(slots[1][box] == 0, wrapped[0:2], wrapped[2:4]) for box in range(2)], axis=0)
        above.append(jnp.where(deep == 15, edge, pltpu.roll(cell[v], LANES - 1, 2)))
    more = axis_change(cell, jnp.abs(velocity[2]) + sound, below, above, 2)
    for v in range(5):
        out_ref[v] = change[v] + more[v]


def final_kernel(near_ref, in_ref, change_ref, before_ref, after_ref, best_ref, out_ref):
    count = in_ref.shape[0] // SLOT
    boxes = 2 * count
    cell = load_cells(in_ref)
    velocity, _, sound = primitives(cell)
    segment = lax.axis_index("seg")
    own_first = in_ref[0:SLOT, :]
    own_last = in_ref[SLOT * (count - 1) : SLOT * count, :]

    def ghost(face, own, other):
        chosen = []
        for box in range(2):
            index = near_ref[box, face]
            inside = lax.div(index, boxes) == segment
            rows = jnp.where(inside, own, other)
            chosen.append(jnp.where(lax.rem(index, 2) == 0, rows[0:ROWS], rows[ROWS : 2 * ROWS]))
        return chosen

    low = ghost(0, own_last, before_ref[...])
    high = ghost(1, own_first, after_ref[...])
    layer = lax.broadcasted_iota(jnp.int32, cell[0].shape, 1)
    below, above = [], []
    for v in range(5):

        def spread(rows):
            return jnp.stack([rows[box][2 * v + half : 2 * v + half + 1] for box in range(2) for half in range(2)])

        below.append(jnp.where(layer == 0, spread(low), pltpu.roll(cell[v], 1, 1)))
        above.append(jnp.where(layer == count - 1, spread(high), pltpu.roll(cell[v], count - 1, 1)))
    change = axis_change(cell, jnp.abs(velocity[0]) + sound, below, above, 0)

    best = jnp.max(best_ref[...], axis=0)
    step = courant / best
    for v in range(5):
        result = cell[v] - step[None] * (change[v] + change_ref[v])
        for box in range(2):
            for half in range(2):
                out_ref[box, v, :, LANES * half : LANES * (half + 1)] = result[2 * box + half]


def local(state, new_slot, neighbours):
    count = lax.axis_size("curve")
    segs = lax.axis_size("seg")
    f32 = jnp.float32
    rows = SLOT * count
    sent = pl.pallas_call(
        pack_kernel,
        out_shape=jax.ShapeDtypeStruct((rows, LANES), f32),
        in_specs=[smem, smem, vmem],
        out_specs=vmem,
        name="pack",
    )(new_slot, neighbours, state)
    met = lax.all_to_all(sent.reshape(count, SLOT, LANES), "curve", 0, 0, tiled=True)
    routed, best = pl.pallas_call(
        route_kernel,
        out_shape=(jax.ShapeDtypeStruct((rows, LANES), f32), jax.ShapeDtypeStruct((segs, 1, LANES), f32)),
        in_specs=[vmem],
        out_specs=(vmem, vmem),
        name="route",
    )(met.reshape(rows, LANES))
    moved = lax.all_to_all(routed.reshape(count, SLOT, LANES), "curve", 0, 0, tiled=True)
    best = lax.all_to_all(best, "seg", 0, 0, tiled=True)
    up = [(i, (i + 1) % segs) for i in range(segs)]
    down = [(j, i) for i, j in up]
    before = lax.ppermute(moved[count - 1], "seg", up)
    after = lax.ppermute(moved[0], "seg", down)
    moved = moved.reshape(rows, LANES)
    change = pl.pallas_call(
        plane_kernel,
        out_shape=jax.ShapeDtypeStruct((5, 4, count, LANES), f32),
        in_specs=[smem, vmem],
        out_specs=vmem,
        name="planes",
    )(neighbours, moved)
    return pl.pallas_call(
        final_kernel,
        out_shape=jax.ShapeDtypeStruct(state.shape, f32),
        in_specs=[smem, vmem, vmem, vmem, vmem, vmem],
        out_specs=vmem,
        name="finish",
    )(neighbours, moved, change, before, after, best)


def solution(mesh):
    placed = (P(("seg", "curve"), None, None, None), P(("seg", "curve")), P(("seg", "curve"), None))
    return jax.shard_map(
        local,
        mesh=mesh,
        in_specs=placed,
        out_specs=P(("seg", "curve"), None, None, None),
        check_vma=False,
    )
```

time: 217 us -> 76.4 us (0.35)
  blocking collectives: 160 us -> 41.8 us
  local copies, waits for them, and re-layouts: 12 us -> 0.61 us
  other arithmetic: 8.76 us -> 0 us
  starting transfers between devices: 30.2 us -> 21.8 us
  Pallas kernels: 0 us -> 7.93 us
    pmax x1 -> x0, blocking collectives: 140 us -> none  [local(): fastest = lax.pmax(local_fastest, ('seg', 'curve'))]
    all_to_all x0 -> x2, blocking collectives: none -> 41.8 us  [the longest x1 28.5 us: local(): lax.all_to_all(sent.reshape(count, SLOT, LANES), 'curve', 0, 0, tiled=True)]
    all_gather x1 -> x0, blocking collectives: 20.1 us -> none  [local(): own_table = lax.all_gather(new_faces, 'curve', axis=0, tiled=True)]
    all_to_all x2 -> x1, starting transfers between devices: 21.6 us -> 13.4 us  [local(): best = lax.all_to_all(best, 'seg', 0, 0, tiled=True)]
    pallas_call x0 -> x4, Pallas kernels: none -> 7.93 us  [the longest x1 2.19 us: local(): pl.pallas_call(route_kernel, out_shape=(jax.ShapeDtypeStruct((rows, LANES...]
    gather x5 -> x0, local copies, waits for them, and re-layouts: 4.6 us -> none  [the longest x1 1.55 us: local(): outgoing = jnp.take(state, chosen, axis=0)]
    all_to_all x2 -> x1, waiting for transfers between devices: 4.16 us -> 0.19 us  [local(): best = lax.all_to_all(best, 'seg', 0, 0, tiled=True)]
    select_n x9 -> x0, other arithmetic: 3.71 us -> none  [the longest x2 1.27 us: local(): outgoing_ids = jnp.where(present, jnp.take(new_slot, chosen), -1)]
  transfers between devices with their start and end apart: 4 -> 3, of which waited for: 1 -> 2; matrix products, arithmetic and copies ran while one was open for 3% -> 0% of each run, Pallas kernels for 0% -> 3%
where the time goes in v1:
time: 76.4 us; the launch traced here: 75.9 us
  blocking collectives  41.8 us (55%)
  starting transfers between devices  21.8 us (29%)
  Pallas kernels  7.93 us (10%)
  waiting for transfers between devices  3.74 us (5%)
    all_to_all x1, blocking collectives, local(): lax.all_to_all(sent.reshape(count, SLOT, LANES), 'curve', 0, 0, tiled=True)  28.5 us
    all_to_all x1, starting transfers between devices, local(): best = lax.all_to_all(best, 'seg', 0, 0, tiled=True)  13.4 us
    all_to_all x1, blocking collectives, local(): lax.all_to_all(routed.reshape(count, SLOT, LANES), 'curve', 0, 0, tiled=T...  13.2 us
    ppermute x1, starting transfers between devices, local(): after = lax.ppermute(moved[0], 'seg', down)  6.55 us
    ppermute x1, waiting for transfers between devices, local(): before = lax.ppermute(moved[count - 1], 'seg', up)  3.55 us
    pallas_call x1, Pallas kernels, local(): pl.pallas_call(route_kernel, out_shape=(jax.ShapeDtypeStruct((rows, LANES...  2.19 us
    pallas_call x1, Pallas kernels, local(): pl.pallas_call(plane_kernel, out_shape=jax.ShapeDtypeStruct((5, 4, count,...  2.07 us
    pallas_call x1, Pallas kernels, local(): pl.pallas_call(final_kernel, out_shape=jax.ShapeDtypeStruct(state.shape,...  1.94 us
  transfers between devices with their start and end apart: 3, of which 2 were waited for; matrix products, arithmetic and copies ran while one was open for 0% of the time, Pallas kernels for 3%

profile of v1, /device:TPU:1, one launch (start us, length us, event | category | flops | bytes accessed | tf_op | source)
XLA Modules:
  0.0 75.9 jit_solution(11922737454793822624)
XLA Ops:
  0.0 1.7 %pack.1 = f32[384,128]{1,0:T(8,128)} custom-call(s32[2]{0:T(128)} %slot_ref.1, s32[2,6]{1,0:T(2,128)} %near_ref.5, f32[2,5,16,256]{3,2,1,0:T(8,128)} %state_ref.1), custom_call_target="tpu_custom_call" | custom-call | tf_op jit(solution)/shard_map/pack/pallas_call | solution.py:233
  1.7 28.5 %all_to_all.15 = f32[16,24,128]{2,1,0:T(8,128)} all-to-all(f32[16,24,128]{2,1,0:T(8,128)} %bitcast.11), channel_id=1, replica_groups=mesh['seg'=64,'curve'=16] {'curve'}, dimensions={0} | all-to-all | bytes 393216 | tf_op jit(solution)/shard_map/all_to_all | solution.py:240
  30.3 2.2 %route.1 = (f32[384,128]{1,0:T(8,128)}, f32[64,1,128]{2,1,0:T(1,128)}) custom-call(f32[384,128]{1,0:T(8,128)} %bitcast.10), custom_call_target="tpu_custom_call" | custom-call | tf_op jit(solution)/shard_map/route/pallas_call | solution.py:241
  32.4 13.2 %all_to_all.16 = f32[16,24,128]{2,1,0:T(8,128)S(1)} all-to-all(f32[16,24,128]{2,1,0:T(8,128)} %bitcast.12), channel_id=1, replica_groups=mesh['seg'=64,'curve'=16] {'curve'}, dimensions={0} | all-to-all | bytes 393216 | tf_op jit(solution)/shard_map/all_to_all | solution.py:248
  45.7 0.0 copy-start
  45.7 13.4 %all-to-all-start.2 = ((f32[64,1,128]{2,1,0:T(1,128)}), f32[64,1,128]{2,1,0:T(1,128)S(1)}, u32[]{:S(2)}, u32[]{:S(2)}) async-start(f32[64,1,128]{2,1,0:T(1,128)} %get-tuple-element.8), calls=%async_computation.2 | async-start | bytes 65536 | tf_op jit(solution)/shard_map/all_to_all | solution.py:249
  59.0 6.6 %collective-permute-start.1 = (f32[24,128]{1,0:T(8,128)S(1)}, f32[24,128]{1,0:T(8,128)S(1)}, u32[]{:S(2)}, u32[]{:S(2)}) collective-permute-start(f32[24,128]{1,0:T(8,128)S(1)} %get-tuple-element.9), channel_id=1, source_target_pairs={{16,0},{32,16},{48,32},{64,48},{80,64},{96,80},{112,96},{128,112},... | collective-permute-start | bytes 36872 | tf_op jit(solution)/shard_map/ppermute | solution.py:253
  65.6 1.9 %collective-permute-start = (f32[24,128]{1,0:T(8,128)S(1)}, f32[24,128]{1,0:T(8,128)S(1)}, u32[]{:S(2)}, u32[]{:S(2)}) collective-permute-start(f32[24,128]{1,0:T(8,128)S(1)} %get-tuple-element.10), channel_id=1, source_target_pairs={{0,16},{16,32},{32,48},{48,64},{64,80},{80,96},{96,112},{112,128},... | collective-permute-start | bytes 36872 | tf_op jit(solution)/shard_map/ppermute | solution.py:252
  67.5 0.0 copy-done
  67.5 2.1 %planes.1.change_ref = f32[5,4,16,128]{3,2,1,0:T(8,128)} custom-call(s32[2,6]{1,0:T(2,128)} %near_ref.5, f32[384,128]{1,0:T(8,128)} %bitcast.8), custom_call_target="tpu_custom_call" | custom-call | tf_op jit(solution)/shard_map/planes/pallas_call | solution.py:255
  69.6 0.2 all-to-all-done.2.best_ref
  69.8 0.0 copy-start.1
  69.8 0.0 collective-permute-done.1.after_ref
  69.8 0.0 copy-start.2
  69.8 3.6 %collective-permute-done.before_ref = f32[24,128]{1,0:T(8,128)S(1)} collective-permute-done((f32[24,128]{1,0:T(8,128)S(1)}, f32[24,128]{1,0:T(8,128)S(1)}, u32[]{:S(2)}, u32[]{:S(2)}) %collective-permute-start) | collective-permute-done | bytes 12320 | tf_op jit(solution)/shard_map/ppermute | solution.py:252
  73.4 0.0 copy-done.1
  73.4 0.0 copy-done.2
  73.4 0.0 copy-start.3
  73.4 0.6 copy-done.3
  74.0 1.9 %finish.1 = f32[2,5,16,256]{3,2,1,0:T(8,128)} custom-call(s32[2,6]{1,0:T(2,128)} %near_ref.5, f32[384,128]{1,0:T(8,128)} %bitcast.9, f32[5,4,16,128]{3,2,1,0:T(8,128)} %planes.1.change_ref, f32[24,128]{1,0:T(8,128)} %copy-done.3, f32[24,128]{1,0:T(8,128)} %copy-done.2, f32[64,1,128]{2,1,0:T(1,128)} %copy-done.1), custom_call_target="tpu_custom_call" | custom-call | tf_op jit(solution)/shard_map/finish/pallas_call | solution.py:262
  (1 shorter events, 0.0 us)
Async XLA Ops:
  45.7 21.9 %copy-start = (f32[16,24,128]{2,1,0:T(8,128)}, f32[16,24,128]{2,1,0:T(8,128)S(1)}, u32[]{:S(2)}) copy-start(f32[16,24,128]{2,1,0:T(8,128)S(1)} %all_to_all.16) | copy-start | bytes 589828
  45.7 24.1 %all-to-all-start.2 = ((f32[64,1,128]{2,1,0:T(1,128)}), f32[64,1,128]{2,1,0:T(1,128)S(1)}, u32[]{:S(2)}, u32[]{:S(2)}) async-start(f32[64,1,128]{2,1,0:T(1,128)} %get-tuple-element.8), calls=%async_computation.2 | async-start | bytes 65536 | tf_op jit(solution)/shard_map/all_to_all | solution.py:249
  59.0 10.8 %collective-permute-start.1 = (f32[24,128]{1,0:T(8,128)S(1)}, f32[24,128]{1,0:T(8,128)S(1)}, u32[]{:S(2)}, u32[]{:S(2)}) collective-permute-start(f32[24,128]{1,0:T(8,128)S(1)} %get-tuple-element.9), channel_id=1, source_target_pairs={{16,0},{32,16},{48,32},{64,48},{80,64},{96,80},{112,96},{128,112},... | collective-permute-start | bytes 36872 | tf_op jit(solution)/shard_map/ppermute | solution.py:253
  65.6 7.8 %collective-permute-start = (f32[24,128]{1,0:T(8,128)S(1)}, f32[24,128]{1,0:T(8,128)S(1)}, u32[]{:S(2)}, u32[]{:S(2)}) collective-permute-start(f32[24,128]{1,0:T(8,128)S(1)} %get-tuple-element.10), channel_id=1, source_target_pairs={{0,16},{16,32},{32,48},{48,64},{64,80},{80,96},{96,112},{112,128},... | collective-permute-start | bytes 36872 | tf_op jit(solution)/shard_map/ppermute | solution.py:252
  69.8 3.6 %copy-start.1 = (f32[64,1,128]{2,1,0:T(1,128)}, f32[64,1,128]{2,1,0:T(1,128)S(1)}, u32[]{:S(2)}) copy-start(f32[64,1,128]{2,1,0:T(1,128)S(1)} %all-to-all-done.2.best_ref) | copy-start | bytes 98308
  69.8 3.6 %copy-start.2 = (f32[24,128]{1,0:T(8,128)}, f32[24,128]{1,0:T(8,128)S(1)}, u32[]{:S(2)}) copy-start(f32[24,128]{1,0:T(8,128)S(1)} %collective-permute-done.1.after_ref) | copy-start | bytes 36868
  73.4 0.6 copy-start.3

commit v2 on v1

v2 whole, which is shorter than its diff:
```python
import math

import jax
import jax.numpy as jnp
from jax import lax
from jax.experimental import pallas as pl
from jax.experimental.pallas import tpu as pltpu
from jax.sharding import Mesh, PartitionSpec as P

gamma_ratio = 1.4
courant = 0.3

LANES = 128
ROWS = 10
SLOT = 24
WIDE = 48

vmem = pl.BlockSpec(memory_space=pltpu.VMEM)
smem = pl.BlockSpec(memory_space=pltpu.SMEM)
params = pltpu.CompilerParams(vmem_limit_bytes=16 * 2**20)
SEG = ("seg_x", "seg_z")


def lane_index(shape):
    return lax.broadcasted_iota(jnp.int32, shape, len(shape) - 1)


def primitives(cell):
    inverse = 1.0 / cell[0]
    velocity = [cell[1 + d] * inverse for d in range(3)]
    kinetic = 0.5 * (cell[1] * velocity[0] + cell[2] * velocity[1] + cell[3] * velocity[2])
    pressure = (gamma_ratio - 1.0) * (cell[4] - kinetic)
    sound = jnp.sqrt(gamma_ratio * pressure * inverse)
    return velocity, pressure, sound


def side(cell, axis_num):
    velocity, pressure, sound = primitives(cell)
    along = velocity[axis_num]
    flux = [cell[1 + axis_num]]
    for d in range(3):
        term = cell[1 + d] * along
        flux.append(term + pressure if d == axis_num else term)
    flux.append((cell[4] + pressure) * along)
    return flux, jnp.abs(along) + sound


def axis_change(cell, speed, below, above, axis_num):
    flux_below, speed_below = side(below, axis_num)
    flux_above, speed_above = side(above, axis_num)
    speed_below = jnp.maximum(speed, speed_below)
    speed_above = jnp.maximum(speed, speed_above)
    return [
        0.5 * (flux_above[v] - flux_below[v])
        - 0.5 * (speed_above * (above[v] - cell[v]) - speed_below * (cell[v] - below[v]))
        for v in range(5)
    ]


def pack_kernel(slot_ref, near_ref, state_ref, out_ref, pick_ref):
    count = out_ref.shape[0] // SLOT
    boxes = 2 * count
    best = None
    for box in range(2):
        cell = [state_ref[box, v] for v in range(5)]
        for v in range(5):
            for half in range(2):
                row = ROWS * box + 2 * v + half
                out_ref[pl.ds(row, count, stride=SLOT), :] = cell[v][:, LANES * half : LANES * (half + 1)]
        velocity, _, sound = primitives(cell)
        largest = jnp.maximum(jnp.maximum(jnp.abs(velocity[0]), jnp.abs(velocity[1])), jnp.abs(velocity[2]))
        speed = largest + sound
        best = speed if best is None else jnp.maximum(best, speed)
    best = jnp.max(jnp.max(best, axis=0, keepdims=True), axis=1, keepdims=True)

    def place(index):
        local = lax.rem(index, boxes)
        return lax.rem(local, 2) * count + lax.div(local, 2)

    values = [place(slot_ref[0]), place(slot_ref[1])]
    for box in range(2):
        values += [place(near_ref[box, 2]), place(near_ref[box, 3])]
    lane = lane_index((count, LANES))
    header = jnp.where(lane == 6, jnp.broadcast_to(best, lane.shape), 0.0)
    for position, value in enumerate(values):
        header = jnp.where(lane == position, value.astype(jnp.float32), header)
    out_ref[pl.ds(20, count, stride=SLOT), :] = header
    for row in range(21, SLOT):
        out_ref[pl.ds(row, count, stride=SLOT), :] = jnp.zeros((count, LANES), jnp.float32)

    segment = lax.axis_index(SEG)
    lane = lane_index(pick_ref.shape)
    picks = jnp.zeros(pick_ref.shape, jnp.float32)
    for box in range(2):
        for face in (0, 1, 4, 5):
            index = near_ref[box, face]
            value = lax.rem(index, 2)
            if face < 2:
                value = value + jnp.where(lax.div(index, boxes) == segment, 2, 0)
            picks = jnp.where(lane == 6 * box + face, value.astype(jnp.float32), picks)
    pick_ref[...] = picks


def peak_kernel(in_ref, best_ref):
    count = in_ref.shape[0] // SLOT
    header = in_ref[pl.ds(20, count, stride=SLOT), :]
    best = jnp.max(jnp.where(lane_index(header.shape) == 6, header, 0.0), axis=0, keepdims=True)
    best = jnp.max(best, axis=1, keepdims=True)
    best_ref[...] = jnp.broadcast_to(best.reshape(1, 1, 1), best_ref.shape)


def three_parts(value):
    high = value.astype(jnp.bfloat16)
    rest = value - high.astype(jnp.float32)
    middle = rest.astype(jnp.bfloat16)
    low = (rest - middle.astype(jnp.float32)).astype(jnp.bfloat16)
    return jnp.concatenate([high, middle, low], axis=0)


def gather_rows(one_hot, parts):
    chosen = jnp.where(one_hot, 1.0, 0.0).astype(jnp.bfloat16)
    return jnp.dot(jnp.concatenate([chosen] * 3, axis=1), parts, preferred_element_type=jnp.float32)


def route_kernel(in_ref, before_ref, after_ref, out_ref):
    count = in_ref.shape[0] // SLOT
    boxes = 2 * count
    header = in_ref[pl.ds(20, count, stride=SLOT), :]
    lane = lane_index((count, LANES))
    both = jnp.concatenate([header, pltpu.roll(header, LANES - 1, 1)], axis=0)
    target = jnp.broadcast_to(jnp.transpose(both)[0:1, :], (boxes, boxes))
    index = lax.broadcasted_iota(jnp.int32, (boxes, boxes), 0).astype(jnp.float32)

    def beside(first, second):
        rows = jnp.concatenate([header[:, first : first + 1], header[:, second : second + 1]], axis=0)
        return jnp.broadcast_to(rows, (boxes, boxes))

    columns = []
    for row in range(ROWS):
        columns.append(
            jnp.concatenate(
                [in_ref[pl.ds(ROWS * box + row, count, stride=SLOT), :] for box in range(2)], axis=0
            )
        )
    lane2 = lane_index((boxes, LANES))
    last = jnp.zeros((boxes, LANES), jnp.float32)
    first = jnp.zeros((boxes, LANES), jnp.float32)
    for v in range(5):
        mine = (lane2 >= 16 * v) & (lane2 < 16 * (v + 1))
        last = jnp.where(mine, pltpu.roll(columns[2 * v + 1], 16 * (v + 1), 1), last)
        first = jnp.where(mine, pltpu.roll(columns[2 * v], 16 * v, 1) if v else columns[0], first)
    placed = gather_rows(index == target, three_parts(jnp.concatenate(columns, axis=1)))
    below = gather_rows(beside(2, 4) == target, three_parts(last))
    above = gather_rows(beside(3, 5) == target, three_parts(first))
    for box in range(2):
        rows = slice(count * box, count * (box + 1))
        for row in range(ROWS):
            out_ref[pl.ds(ROWS * box + row, count, stride=WIDE), :] = placed[rows, LANES * row : LANES * (row + 1)]
        out_ref[pl.ds(20 + box, count, stride=WIDE), :] = below[rows]
        out_ref[pl.ds(22 + box, count, stride=WIDE), :] = above[rows]

    place = lax.broadcasted_iota(jnp.int32, (count, LANES), 0).astype(jnp.float32)
    marks = jnp.zeros((count, LANES), jnp.float32)
    for side_num, face_ref in enumerate((after_ref, before_ref)):
        face = face_ref[...]
        target = [jnp.broadcast_to(face[20:21, box : box + 1], place.shape) for box in range(2)]
        slot = [jnp.where(t >= count, 1.0, 0.0) for t in target]
        here = [place == target[box] - count * slot[box] for box in range(2)]
        for row in range(ROWS):
            value = jnp.where(here[0], face[row : row + 1], face[ROWS + row : ROWS + row + 1])
            out_ref[pl.ds(24 + ROWS * side_num + row, count, stride=WIDE), :] = value
        mark = jnp.where(here[0], slot[0], jnp.where(here[1], slot[1], -1.0))
        marks = jnp.where(lane == side_num, mark, marks)
    for row in range(44, WIDE):
        out_ref[pl.ds(row, count, stride=WIDE), :] = marks


def advance_kernel(pick_ref, in_ref, best_ref, out_ref):
    count = in_ref.shape[0] // WIDE

    def rows_of(row):
        return in_ref[pl.ds(row, count, stride=WIDE), :]

    def pick(box, face):
        return pick_ref[0:1, 6 * box + face : 6 * box + face + 1]

    cell = [
        jnp.stack([rows_of(ROWS * box + 2 * v + half) for box in range(2) for half in range(2)]) for v in range(5)
    ]
    velocity, _, sound = primitives(cell)
    lane = lane_index(cell[0].shape)

    marks = rows_of(44)
    own = (in_ref[WIDE * (count - 1) : WIDE * (count - 1) + SLOT, :], in_ref[0:SLOT, :])
    ghosts = []
    for face in range(2):
        start = 34 - ROWS * face
        mark = jnp.broadcast_to(marks[:, 1 - face : 2 - face], (count, LANES))
        strips = [rows_of(start + row) for row in range(ROWS)]
        for box in range(2):
            wanted = pick(box, face)
            mine = mark == wanted
            far = [jnp.sum(jnp.where(mine, strip, 0.0), axis=0, keepdims=True) for strip in strips]
            near = jnp.where(wanted == 2.0, own[face][0:ROWS], own[face][ROWS : 2 * ROWS])
            inside = wanted >= 2.0
            ghosts.append([jnp.where(inside, near[row : row + 1], far[row]) for row in range(ROWS)])
    layer = lax.broadcasted_iota(jnp.int32, cell[0].shape, 1)
    below, above = [], []
    for v in range(5):

        def spread(rows):
            return jnp.stack([rows[box][2 * v + half] for box in range(2) for half in range(2)])

        below.append(jnp.where(layer == 0, spread(ghosts[0:2]), pltpu.roll(cell[v], 1, 1)))
        above.append(jnp.where(layer == count - 1, spread(ghosts[2:4]), pltpu.roll(cell[v], count - 1, 1)))
    change = axis_change(cell, jnp.abs(velocity[0]) + sound, below, above, 0)

    ghost_low = [rows_of(20 + box) for box in range(2)]
    ghost_high = [rows_of(22 + box) for box in range(2)]
    below, above = [], []
    for v in range(5):
        low = [pltpu.roll(g, LANES - 16 * v, 1) if v else g for g in ghost_low]
        high = [pltpu.roll(g, 112 - 16 * v, 1) for g in ghost_high]
        rolled = pltpu.roll(cell[v], 16, 2)
        edge = jnp.stack([low[0], rolled[0], low[1], rolled[2]])
        below.append(jnp.where(lane < 16, edge, rolled))
        rolled = pltpu.roll(cell[v], LANES - 16, 2)
        edge = jnp.stack([rolled[1], high[0], rolled[3], high[1]])
        above.append(jnp.where(lane >= LANES - 16, edge, rolled))
    more = axis_change(cell, jnp.abs(velocity[1]) + sound, below, above, 1)
    change = [change[v] + more[v] for v in range(5)]

    deep = lane & 15
    below, above = [], []
    slots = [[pick(box, face) == 0.0 for box in range(2)] for face in (4, 5)]
    for v in range(5):
        wrapped = pltpu.roll(cell[v], LANES - 15, 2)
        edge = jnp.concatenate([jnp.where(slots[0][box], wrapped[0:2], wrapped[2:4]) for box in range(2)], axis=0)
        below.append(jnp.where(deep == 0, edge, pltpu.roll(cell[v], 1, 2)))
        wrapped = pltpu.roll(cell[v], 15, 2)
        edge = jnp.concatenate([jnp.where(slots[1][box], wrapped[0:2], wrapped[2:4]) for box in range(2)], axis=0)
        above.append(jnp.where(deep == 15, edge, pltpu.roll(cell[v], LANES - 1, 2)))
    more = axis_change(cell, jnp.abs(velocity[2]) + sound, below, above, 2)

    step = courant / jnp.max(best_ref[...], axis=0)
    for v in range(5):
        result = cell[v] - step[None] * (change[v] + more[v])
        for box in range(2):
            for half in range(2):
                out_ref[box, v, :, LANES * half : LANES * (half + 1)] = result[2 * box + half]


def local(state, new_slot, neighbours):
    count = lax.axis_size("curve")
    along_x, along_z = (lax.axis_size(axis) for axis in SEG)
    segs = along_x * along_z
    f32 = jnp.float32
    sent, pick = pl.pallas_call(
        pack_kernel,
        out_shape=(jax.ShapeDtypeStruct((SLOT * count, LANES), f32), jax.ShapeDtypeStruct((8, LANES), f32)),
        in_specs=[smem, smem, vmem],
        out_specs=(vmem, vmem),
        compiler_params=params,
        name="pack",
    )(new_slot, neighbours, state)
    up = [(i, (i + 1) % segs) for i in range(segs)]
    down = [(j, i) for i, j in up]
    met = lax.all_to_all(sent.reshape(count, SLOT, LANES), "curve", 0, 0, tiled=True)
    before = lax.ppermute(sent[SLOT * (count - 1) :], SEG, up)
    after = lax.ppermute(sent[:SLOT], SEG, down)
    met = met.reshape(SLOT * count, LANES)
    best = pl.pallas_call(
        peak_kernel,
        out_shape=jax.ShapeDtypeStruct((along_x, 1, LANES), f32),
        in_specs=[vmem],
        out_specs=vmem,
        compiler_params=params,
        name="peak",
    )(met)
    best = lax.all_to_all(best, SEG[0], 0, 0, tiled=True)
    routed = pl.pallas_call(
        route_kernel,
        out_shape=jax.ShapeDtypeStruct((WIDE * count, LANES), f32),
        in_specs=[vmem, vmem, vmem],
        out_specs=vmem,
        compiler_params=params,
        name="route",
    )(met, before, after)
    moved = lax.all_to_all(routed.reshape(count, WIDE, LANES), "curve", 0, 0, tiled=True)
    best = lax.all_gather(best, SEG[1], axis=0, tiled=True)
    return pl.pallas_call(
        advance_kernel,
        out_shape=jax.ShapeDtypeStruct(state.shape, f32),
        in_specs=[vmem, vmem, vmem],
        out_specs=vmem,
        compiler_params=params,
        name="advance",
    )(pick, moved.reshape(WIDE * count, LANES), best)


def solution(mesh):
    segs, count = mesh.devices.shape
    side_x = math.isqrt(segs)
    grid = Mesh(mesh.devices.reshape(side_x, segs // side_x, count), SEG + ("curve",))
    placed = P(SEG + ("curve",))
    return jax.shard_map(
        local, mesh=grid, in_specs=(placed, placed, placed), out_specs=placed, check_vma=False
    )
```

time: 76.4 us -> 81.1 us (1.062)
  the two profiles are of different devices: /device:TPU:1 before, /device:TPU:16 now
where the time goes in v2:
time: 81.1 us; the launch traced here: 80.5 us
  starting transfers between devices  41.1 us (51%)
  blocking collectives  25.3 us (31%)
  waiting for transfers between devices  6.48 us (8%)
  Pallas kernels  4.56 us (6%)
  local copies, waits for them, and re-layouts  2.99 us (4%)
    all_gather x1, blocking collectives, local(): best = lax.all_gather(best, SEG[1], axis=0, tiled=True)  25.3 us
    all_to_all x1, starting transfers between devices, local(): lax.all_to_all(sent.reshape(count, SLOT, LANES), 'curve', 0, 0, tiled=True)  16.3 us
    ppermute x1, starting transfers between devices, local(): after = lax.ppermute(sent[:SLOT], SEG, down)  11.2 us
    all_to_all x1, starting transfers between devices, local(): lax.all_to_all(routed.reshape(count, WIDE, LANES), 'curve', 0, 0, tiled=T...  7.22 us
    all_to_all x1, waiting for transfers between devices, local(): best = lax.all_to_all(best, SEG[0], 0, 0, tiled=True)  4.64 us
    all_to_all x1, starting transfers between devices, local(): best = lax.all_to_all(best, SEG[0], 0, 0, tiled=True)  4.45 us
    unnamed x6, local copies, waits for them, and re-layouts  2.25 us
    ppermute x1, starting transfers between devices, local(): before = lax.ppermute(sent[SLOT * (count - 1):], SEG, up)  1.92 us
  transfers between devices with their start and end apart: 5, of which 2 were waited for; matrix products, arithmetic and copies ran while one was open for 1% of the time, Pallas kernels for 2%

profile of v2, /device:TPU:16, one launch (start us, length us, event | category | flops | bytes accessed | tf_op | source)
XLA Modules:
  0.0 80.5 jit_solution(17793316024771881957)
XLA Ops:
  0.0 0.0 copy-start
  0.0 0.9 %copy-done = f32[2,5,16,256]{3,2,1,0:T(8,128)S(1)} copy-done((f32[2,5,16,256]{3,2,1,0:T(8,128)S(1)}, f32[2,5,16,256]{3,2,1,0:T(8,128)}, u32[]{:S(2)}) %copy-start) | copy-done | bytes 163864
  0.9 0.0 copy-start.1
  0.9 0.7 copy-done.1
  1.6 0.0 copy-start.2
  1.6 0.7 copy-done.2
  2.3 1.4 %pack.1 = (f32[384,128]{1,0:T(8,128)}, f32[8,128]{1,0:T(8,128)S(1)}) custom-call(s32[2]{0:T(128)S(1)} %copy-done.2, s32[2,6]{1,0:T(2,128)S(1)} %copy-done.1, f32[2,5,16,256]{3,2,1,0:T(8,128)S(1)} %copy-done), custom_call_target="tpu_custom_call" | custom-call | tf_op jit(solution)/shard_map/pack/pallas_call | solution.py:258
  3.6 16.3 %all-to-all-start = ((f32[16,24,128]{2,1,0:T(8,128)}), f32[16,24,128]{2,1,0:T(8,128)S(1)}, u32[]{:S(2)}, u32[]{:S(2)}) async-start(f32[16,24,128]{2,1,0:T(8,128)} %bitcast), calls=%async_computation | async-start | bytes 393216 | tf_op jit(solution)/shard_map/all_to_all | solution.py:268
  19.9 0.7 fusion
  20.7 11.2 %collective-permute-start.1 = (f32[24,128]{1,0:T(8,128)S(1)}, f32[24,128]{1,0:T(8,128)S(1)}, u32[]{:S(2)}, u32[]{:S(2)}) collective-permute-start(f32[24,128]{1,0:T(8,128)S(1)} %get-tuple-element.9), channel_id=1, source_target_pairs={{16,0},{32,16},{48,32},{64,48},{80,64},{96,80},{112,96},{128,112},... | collective-permute-start | bytes 36872 | tf_op jit(solution)/shard_map/ppermute | solution.py:270
  31.9 1.9 %collective-permute-start = (f32[24,128]{1,0:T(8,128)S(1)}, f32[24,128]{1,0:T(8,128)S(1)}, u32[]{:S(2)}, u32[]{:S(2)}) collective-permute-start(f32[24,128]{1,0:T(8,128)S(1)} %get-tuple-element.10), channel_id=1, source_target_pairs={{0,16},{16,32},{32,48},{48,64},{64,80},{80,96},{96,112},{112,128},... | collective-permute-start | bytes 36872 | tf_op jit(solution)/shard_map/ppermute | solution.py:269
  33.8 0.0 all-to-all-done
  33.8 0.7 peak.1
  34.5 4.5 %all-to-all-start.2 = ((f32[8,1,128]{2,1,0:T(1,128)}), f32[8,1,128]{2,1,0:T(1,128)S(1)}, u32[]{:S(2)}, u32[]{:S(2)}) async-start(f32[8,1,128]{2,1,0:T(1,128)} %peak.1), calls=%async_computation.2 | async-start | bytes 8192 | tf_op jit(solution)/shard_map/all_to_all | solution.py:280
  39.0 0.0 collective-permute-done.1.after_ref
  39.0 1.8 %collective-permute-done.before_ref = f32[24,128]{1,0:T(8,128)S(1)} collective-permute-done((f32[24,128]{1,0:T(8,128)S(1)}, f32[24,128]{1,0:T(8,128)S(1)}, u32[]{:S(2)}, u32[]{:S(2)}) %collective-permute-start) | collective-permute-done | bytes 12320 | tf_op jit(solution)/shard_map/ppermute | solution.py:269
  40.8 1.1 %route.1 = f32[768,128]{1,0:T(8,128)} custom-call(f32[384,128]{1,0:T(8,128)S(1)} %bitcast.5, f32[24,128]{1,0:T(8,128)S(1)} %collective-permute-done.before_ref, f32[24,128]{1,0:T(8,128)S(1)} %collective-permute-done.1.after_ref), custom_call_target="tpu_custom_call" | custom-call | tf_op jit(solution)/shard_map/route/pallas_call | solution.py:281
  41.9 4.6 %all-to-all-done.2 = f32[8,1,128]{2,1,0:T(1,128)S(1)} async-done(((f32[8,1,128]{2,1,0:T(1,128)}), f32[8,1,128]{2,1,0:T(1,128)S(1)}, u32[]{:S(2)}, u32[]{:S(2)}) %all-to-all-start.2) | async-done | bytes 4128 | tf_op jit(solution)/shard_map/all_to_all | solution.py:280
  46.6 7.2 %all-to-all-start.1 = ((f32[16,48,128]{2,1,0:T(8,128)}), f32[16,48,128]{2,1,0:T(8,128)S(1)}, u32[]{:S(2)}, u32[]{:S(2)}) async-start(f32[16,48,128]{2,1,0:T(8,128)} %bitcast.2), calls=%async_computation.1 | async-start | bytes 786432 | tf_op jit(solution)/shard_map/all_to_all | solution.py:289
  53.8 25.3 %all_gather.3.best_ref = f32[64,1,128]{2,1,0:T(1,128)S(1)} all-gather(f32[8,1,128]{2,1,0:T(1,128)S(1)} %all-to-all-done.2), channel_id=1, replica_groups=mesh['seg_x'=8,'seg_z'=8,'curve'=16] {'seg_z'}, dimensions={0}, use_global_device_ids=true | all-gather | bytes 36864 | tf_op jit(solution)/shard_map/all_gather | solution.py:290
  79.1 0.0 all-to-all-done.1
  79.1 1.4 %advance.1 = f32[2,5,16,256]{3,2,1,0:T(8,128)} custom-call(f32[8,128]{1,0:T(8,128)S(1)} %get-tuple-element.7.pick_ref, f32[768,128]{1,0:T(8,128)S(1)} %bitcast.6, f32[64,1,128]{2,1,0:T(1,128)S(1)} %all_gather.3.best_ref), custom_call_target="tpu_custom_call" | custom-call | tf_op jit(solution)/shard_map/advance/pallas_call | solution.py:291
Async XLA Ops:
  0.0 0.9 %copy-start = (f32[2,5,16,256]{3,2,1,0:T(8,128)S(1)}, f32[2,5,16,256]{3,2,1,0:T(8,128)}, u32[]{:S(2)}) copy-start(f32[2,5,16,256]{3,2,1,0:T(8,128)} %state_ref.1) | copy-start | bytes 491524
  0.9 0.7 copy-start.1
  1.6 0.7 copy-start.2
  3.6 30.2 %all-to-all-start = ((f32[16,24,128]{2,1,0:T(8,128)}), f32[16,24,128]{2,1,0:T(8,128)S(1)}, u32[]{:S(2)}, u32[]{:S(2)}) async-start(f32[16,24,128]{2,1,0:T(8,128)} %bitcast), calls=%async_computation | async-start | bytes 393216 | tf_op jit(solution)/shard_map/all_to_all | solution.py:268
  20.7 18.3 %collective-permute-start.1 = (f32[24,128]{1,0:T(8,128)S(1)}, f32[24,128]{1,0:T(8,128)S(1)}, u32[]{:S(2)}, u32[]{:S(2)}) collective-permute-start(f32[24,128]{1,0:T(8,128)S(1)} %get-tuple-element.9), channel_id=1, source_target_pairs={{16,0},{32,16},{48,32},{64,48},{80,64},{96,80},{112,96},{128,112},... | collective-permute-start | bytes 36872 | tf_op jit(solution)/shard_map/ppermute | solution.py:270
  31.9 8.9 %collective-permute-start = (f32[24,128]{1,0:T(8,128)S(1)}, f32[24,128]{1,0:T(8,128)S(1)}, u32[]{:S(2)}, u32[]{:S(2)}) collective-permute-start(f32[24,128]{1,0:T(8,128)S(1)} %get-tuple-element.10), channel_id=1, source_target_pairs={{0,16},{16,32},{32,48},{48,64},{64,80},{80,96},{96,112},{112,128},... | collective-permute-start | bytes 36872 | tf_op jit(solution)/shard_map/ppermute | solution.py:269
  34.5 12.1 %all-to-all-start.2 = ((f32[8,1,128]{2,1,0:T(1,128)}), f32[8,1,128]{2,1,0:T(1,128)S(1)}, u32[]{:S(2)}, u32[]{:S(2)}) async-start(f32[8,1,128]{2,1,0:T(1,128)} %peak.1), calls=%async_computation.2 | async-start | bytes 8192 | tf_op jit(solution)/shard_map/all_to_all | solution.py:280
  46.6 32.6 %all-to-all-start.1 = ((f32[16,48,128]{2,1,0:T(8,128)}), f32[16,48,128]{2,1,0:T(8,128)S(1)}, u32[]{:S(2)}, u32[]{:S(2)}) async-start(f32[16,48,128]{2,1,0:T(8,128)} %bitcast.2), calls=%async_computation.1 | async-start | bytes 786432 | tf_op jit(solution)/shard_map/all_to_all | solution.py:289

commit v3 on v2

--- a/solution.py
+++ b/solution.py
@@ -1,11 +1,9 @@
-import math
-
 import jax
 import jax.numpy as jnp
 from jax import lax
 from jax.experimental import pallas as pl
 from jax.experimental.pallas import tpu as pltpu
-from jax.sharding import Mesh, PartitionSpec as P
+from jax.sharding import PartitionSpec as P
 
 gamma_ratio = 1.4
 courant = 0.3
@@ -13,12 +11,10 @@
 LANES = 128
 ROWS = 10
 SLOT = 24
-WIDE = 48
 
 vmem = pl.BlockSpec(memory_space=pltpu.VMEM)
-smem = pl.BlockSpec(memory_space=pltpu.SMEM)
+hbm = pl.BlockSpec(memory_space=pltpu.HBM)
 params = pltpu.CompilerParams(vmem_limit_bytes=16 * 2**20)
-SEG = ("seg_x", "seg_z")
 
 
 def lane_index(shape):
@@ -57,7 +53,17 @@
     ]
 
 
-def pack_kernel(slot_ref, near_ref, state_ref, out_ref, pick_ref):
+def pack_kernel(slot_hbm, near_hbm, state_hbm, out_ref, pick_ref, slot_ref, near_ref, state_ref, sems):
+    copies = [
+        pltpu.make_async_copy(source, target, sems.at[i])
+        for i, (source, target) in enumerate(
+            ((state_hbm, state_ref), (slot_hbm, slot_ref), (near_hbm, near_ref))
+        )
+    ]
+    for copy in copies:
+        copy.start()
+    for copy in copies:
+        copy.wait()
     count = out_ref.shape[0] // SLOT
     boxes = 2 * count
     best = None
@@ -88,7 +94,7 @@
     for row in range(21, SLOT):
         out_ref[pl.ds(row, count, stride=SLOT), :] = jnp.zeros((count, LANES), jnp.float32)
 
-    segment = lax.axis_index(SEG)
+    segment = lax.axis_index("seg")
     lane = lane_index(pick_ref.shape)
     picks = jnp.zeros(pick_ref.shape, jnp.float32)
     for box in range(2):
@@ -101,14 +107,6 @@
     pick_ref[...] = picks
 
 
-def peak_kernel(in_ref, best_ref):
-    count = in_ref.shape[0] // SLOT
-    header = in_ref[pl.ds(20, count, stride=SLOT), :]
-    best = jnp.max(jnp.where(lane_index(header.shape) == 6, header, 0.0), axis=0, keepdims=True)
-    best = jnp.max(best, axis=1, keepdims=True)
-    best_ref[...] = jnp.broadcast_to(best.reshape(1, 1, 1), best_ref.shape)
-
-
 def three_parts(value):
     high = value.astype(jnp.bfloat16)
     rest = value - high.astype(jnp.float32)
@@ -122,11 +120,13 @@
     return jnp.dot(jnp.concatenate([chosen] * 3, axis=1), parts, preferred_element_type=jnp.float32)
 
 
-def route_kernel(in_ref, before_ref, after_ref, out_ref):
+def route_kernel(in_ref, out_ref, best_ref):
     count = in_ref.shape[0] // SLOT
     boxes = 2 * count
     header = in_ref[pl.ds(20, count, stride=SLOT), :]
-    lane = lane_index((count, LANES))
+    best = jnp.max(jnp.where(lane_index(header.shape) == 6, header, 0.0), axis=0, keepdims=True)
+    best = jnp.max(best, axis=1, keepdims=True)
+    best_ref[...] = jnp.broadcast_to(best.reshape(1, 1, 1), best_ref.shape)
     both = jnp.concatenate([header, pltpu.roll(header, LANES - 1, 1)], axis=0)
     target = jnp.broadcast_to(jnp.transpose(both)[0:1, :], (boxes, boxes))
     index = lax.broadcasted_iota(jnp.int32, (boxes, boxes), 0).astype(jnp.float32)
@@ -155,31 +155,16 @@
     for box in range(2):
         rows = slice(count * box, count * (box + 1))
         for row in range(ROWS):
-            out_ref[pl.ds(ROWS * box + row, count, stride=WIDE), :] = placed[rows, LANES * row : LANES * (row + 1)]
-        out_ref[pl.ds(20 + box, count, stride=WIDE), :] = below[rows]
-        out_ref[pl.ds(22 + box, count, stride=WIDE), :] = above[rows]
-
-    place = lax.broadcasted_iota(jnp.int32, (count, LANES), 0).astype(jnp.float32)
-    marks = jnp.zeros((count, LANES), jnp.float32)
-    for side_num, face_ref in enumerate((after_ref, before_ref)):
-        face = face_ref[...]
-        target = [jnp.broadcast_to(face[20:21, box : box + 1], place.shape) for box in range(2)]
-        slot = [jnp.where(t >= count, 1.0, 0.0) for t in target]
-        here = [place == target[box] - count * slot[box] for box in range(2)]
-        for row in range(ROWS):
-            value = jnp.where(here[0], face[row : row + 1], face[ROWS + row : ROWS + row + 1])
-            out_ref[pl.ds(24 + ROWS * side_num + row, count, stride=WIDE), :] = value
-        mark = jnp.where(here[0], slot[0], jnp.where(here[1], slot[1], -1.0))
-        marks = jnp.where(lane == side_num, mark, marks)
-    for row in range(44, WIDE):
-        out_ref[pl.ds(row, count, stride=WIDE), :] = marks
-
-
-def advance_kernel(pick_ref, in_ref, best_ref, out_ref):
-    count = in_ref.shape[0] // WIDE
+            out_ref[pl.ds(ROWS * box + row, count, stride=SLOT), :] = placed[rows, LANES * row : LANES * (row + 1)]
+        out_ref[pl.ds(20 + box, count, stride=SLOT), :] = below[rows]
+        out_ref[pl.ds(22 + box, count, stride=SLOT), :] = above[rows]
+
+
+def advance_kernel(pick_ref, in_ref, before_ref, after_ref, best_ref, out_ref):
+    count = in_ref.shape[0] // SLOT
 
     def rows_of(row):
-        return in_ref[pl.ds(row, count, stride=WIDE), :]
+        return in_ref[pl.ds(row, count, stride=SLOT), :]
 
     def pick(box, face):
         return pick_ref[0:1, 6 * box + face : 6 * box + face + 1]
@@ -190,26 +175,21 @@
     velocity, _, sound = primitives(cell)
     lane = lane_index(cell[0].shape)
 
-    marks = rows_of(44)
-    own = (in_ref[WIDE * (count - 1) : WIDE * (count - 1) + SLOT, :], in_ref[0:SLOT, :])
+    own = (in_ref[SLOT * (count - 1) : SLOT * count, :], in_ref[0:SLOT, :])
+    other = (before_ref[...], after_ref[...])
     ghosts = []
     for face in range(2):
-        start = 34 - ROWS * face
-        mark = jnp.broadcast_to(marks[:, 1 - face : 2 - face], (count, LANES))
-        strips = [rows_of(start + row) for row in range(ROWS)]
         for box in range(2):
             wanted = pick(box, face)
-            mine = mark == wanted
-            far = [jnp.sum(jnp.where(mine, strip, 0.0), axis=0, keepdims=True) for strip in strips]
-            near = jnp.where(wanted == 2.0, own[face][0:ROWS], own[face][ROWS : 2 * ROWS])
-            inside = wanted >= 2.0
-            ghosts.append([jnp.where(inside, near[row : row + 1], far[row]) for row in range(ROWS)])
+            rows = jnp.where(wanted >= 2.0, own[face], other[face])
+            first = (wanted == 0.0) | (wanted == 2.0)
+            ghosts.append(jnp.where(first, rows[0:ROWS], rows[ROWS : 2 * ROWS]))
     layer = lax.broadcasted_iota(jnp.int32, cell[0].shape, 1)
     below, above = [], []
     for v in range(5):
 
         def spread(rows):
-            return jnp.stack([rows[box][2 * v + half] for box in range(2) for half in range(2)])
+            return jnp.stack([rows[box][2 * v + half : 2 * v + half + 1] for box in range(2) for half in range(2)])
 
         below.append(jnp.where(layer == 0, spread(ghosts[0:2]), pltpu.roll(cell[v], 1, 1)))
         above.append(jnp.where(layer == count - 1, spread(ghosts[2:4]), pltpu.roll(cell[v], count - 1, 1)))
@@ -252,57 +232,52 @@
 
 def local(state, new_slot, neighbours):
     count = lax.axis_size("curve")
-    along_x, along_z = (lax.axis_size(axis) for axis in SEG)
-    segs = along_x * along_z
+    segs = lax.axis_size("seg")
     f32 = jnp.float32
     sent, pick = pl.pallas_call(
         pack_kernel,
         out_shape=(jax.ShapeDtypeStruct((SLOT * count, LANES), f32), jax.ShapeDtypeStruct((8, LANES), f32)),
-        in_specs=[smem, smem, vmem],
+        in_specs=[hbm, hbm, hbm],
+        out_specs=(vmem, vmem),
+        scratch_shapes=[
+            pltpu.SMEM(new_slot.shape, jnp.int32),
+            pltpu.SMEM(neighbours.shape, jnp.int32),
+            pltpu.VMEM(state.shape, f32),
+            pltpu.SemaphoreType.DMA((3,)),
+        ],
+        name="pack",
+    )(new_slot, neighbours, state)
+    met = lax.all_to_all(sent.reshape(count, SLOT, LANES), "curve", 0, 0, tiled=True)
+    routed, best = pl.pallas_call(
+        route_kernel,
+        out_shape=(
+            jax.ShapeDtypeStruct((SLOT * count, LANES), f32),
+            jax.ShapeDtypeStruct((segs, 1, LANES), f32),
+        ),
+        in_specs=[vmem],
         out_specs=(vmem, vmem),
         compiler_params=params,
-        name="pack",
-    )(new_slot, neighbours, state)
+        name="route",
+    )(met.reshape(SLOT * count, LANES))
+    moved = lax.all_to_all(routed.reshape(count, SLOT, LANES), "curve", 0, 0, tiled=True)
     up = [(i, (i + 1) % segs) for i in range(segs)]
     down = [(j, i) for i, j in up]
-    met = lax.all_to_all(sent.reshape(count, SLOT, LANES), "curve", 0, 0, tiled=True)
-    before = lax.ppermute(sent[SLOT * (count - 1) :], SEG, up)
-    after = lax.ppermute(sent[:SLOT], SEG, down)
-    met = met.reshape(SLOT * count, LANES)
-    best = pl.pallas_call(
-        peak_kernel,
-        out_shape=jax.ShapeDtypeStruct((along_x, 1, LANES), f32),
-        in_specs=[vmem],
-        out_specs=vmem,
-        compiler_params=params,
-        name="peak",
-    )(met)
-    best = lax.all_to_all(best, SEG[0], 0, 0, tiled=True)
-    routed = pl.pallas_call(
-        route_kernel,
-        out_shape=jax.ShapeDtypeStruct((WIDE * count, LANES), f32),
-        in_specs=[vmem, vmem, vmem],
-        out_specs=vmem,
-        compiler_params=params,
-        name="route",
-    )(met, before, after)
-    moved = lax.all_to_all(routed.reshape(count, WIDE, LANES), "curve", 0, 0, tiled=True)
-    best = lax.all_gather(best, SEG[1], axis=0, tiled=True)
+    before = lax.ppermute(moved[count - 1], "seg", up)
+    after = lax.ppermute(moved[0], "seg", down)
+    best, before, after = lax.optimization_barrier((best, before, after))
+    best = lax.all_to_all(best, "seg", 0, 0, tiled=True)
     return pl.pallas_call(
         advance_kernel,
         out_shape=jax.ShapeDtypeStruct(state.shape, f32),
-        in_specs=[vmem, vmem, vmem],
+        in_specs=[vmem] * 5,
         out_specs=vmem,
         compiler_params=params,
         name="advance",
-    )(pick, moved.reshape(WIDE * count, LANES), best)
+    )(pick, moved.reshape(SLOT * count, LANES), before, after, best)
 
 
 def solution(mesh):
-    segs, count = mesh.devices.shape
-    side_x = math.isqrt(segs)
-    grid = Mesh(mesh.devices.reshape(side_x, segs // side_x, count), SEG + ("curve",))
-    placed = P(SEG + ("curve",))
+    placed = P(("seg", "curve"))
     return jax.shard_map(
-        local, mesh=grid, in_specs=(placed, placed, placed), out_specs=placed, check_vma=False
+        local, mesh=mesh, in_specs=(placed, placed, placed), out_specs=placed, check_vma=False
     )

time: 81.1 us -> 79.4 us (0.979)
  the two profiles are of different devices: /device:TPU:16 before, /device:TPU:1 now
where the time goes in v3:
time: 79.4 us; the launch traced here: 78.9 us
  blocking collectives  56.7 us (71%)
  starting transfers between devices  12.8 us (16%)
  waiting for transfers between devices  5.82 us (7%)
  Pallas kernels  3.42 us (4%)
    all_to_all x1, blocking collectives, local(): lax.all_to_all(sent.reshape(count, SLOT, LANES), 'curve', 0, 0, tiled=True)  27.8 us
    all_to_all x1, blocking collectives, local(): best = lax.all_to_all(best, 'seg', 0, 0, tiled=True)  15.9 us
    all_to_all x1, blocking collectives, local(): lax.all_to_all(routed.reshape(count, SLOT, LANES), 'curve', 0, 0, tiled=T...  13 us
    ppermute x1, starting transfers between devices, local(): after = lax.ppermute(moved[0], 'seg', down)  10.9 us
    ppermute x1, waiting for transfers between devices, local(): before = lax.ppermute(moved[count - 1], 'seg', up)  5.82 us
    ppermute x1, starting transfers between devices, local(): before = lax.ppermute(moved[count - 1], 'seg', up)  1.92 us
    pallas_call x1, Pallas kernels, local(): pl.pallas_call(pack_kernel, out_shape=(jax.ShapeDtypeStruct((SLOT * count...  1.76 us
  transfers between devices with their start and end apart: 2, of which 1 were waited for; matrix products, arithmetic and copies ran while one was open for 0% of the time, Pallas kernels for 0%

profile of v3, /device:TPU:1, one launch (start us, length us, event | category | flops | bytes accessed | tf_op | source)
XLA Modules:
  0.0 78.9 jit_solution(11503965163112204145)
XLA Ops:
  0.0 1.8 %pack.1 = (f32[384,128]{1,0:T(8,128)}, f32[8,128]{1,0:T(8,128)}) custom-call(s32[2]{0:T(128)} %slot_hbm.1, s32[2,6]{1,0:T(2,128)} %near_hbm.1, f32[2,5,16,256]{3,2,1,0:T(8,128)} %state_hbm.1), custom_call_target="tpu_custom_call" | custom-call | tf_op jit(solution)/shard_map/pack/pallas_call | solution.py:237
  1.8 27.8 %all_to_all.15 = f32[16,24,128]{2,1,0:T(8,128)S(1)} all-to-all(f32[16,24,128]{2,1,0:T(8,128)} %bitcast.11), channel_id=1, replica_groups=mesh['seg'=64,'curve'=16] {'curve'}, dimensions={0} | all-to-all | bytes 393216 | tf_op jit(solution)/shard_map/all_to_all | solution.py:250
  29.6 0.4 route.1
  30.0 13.0 %all_to_all.16 = f32[16,24,128]{2,1,0:T(8,128)S(1)} all-to-all(f32[16,24,128]{2,1,0:T(8,128)S(1)} %bitcast.10), channel_id=1, replica_groups=mesh['seg'=64,'curve'=16] {'curve'}, dimensions={0} | all-to-all | bytes 393216 | tf_op jit(solution)/shard_map/all_to_all | solution.py:262
  43.0 10.9 %collective-permute-start.1 = (f32[24,128]{1,0:T(8,128)S(1)}, f32[24,128]{1,0:T(8,128)S(1)}, u32[]{:S(2)}, u32[]{:S(2)}) collective-permute-start(f32[24,128]{1,0:T(8,128)S(1)} %get-tuple-element.19), channel_id=1, source_target_pairs={{16,0},{32,16},{48,32},{64,48},{80,64},{96,80},{112,96},{128,112},... | collective-permute-start | bytes 36872 | tf_op jit(solution)/shard_map/ppermute | solution.py:266
  53.9 1.9 %collective-permute-start = (f32[24,128]{1,0:T(8,128)S(1)}, f32[24,128]{1,0:T(8,128)S(1)}, u32[]{:S(2)}, u32[]{:S(2)}) collective-permute-start(f32[24,128]{1,0:T(8,128)S(1)} %get-tuple-element.20), channel_id=1, source_target_pairs={{0,16},{16,32},{32,48},{48,64},{64,80},{80,96},{96,112},{112,128},... | collective-permute-start | bytes 36872 | tf_op jit(solution)/shard_map/ppermute | solution.py:265
  55.8 0.0 collective-permute-done.1.after_ref
  55.8 5.8 %collective-permute-done.before_ref = f32[24,128]{1,0:T(8,128)S(1)} collective-permute-done((f32[24,128]{1,0:T(8,128)S(1)}, f32[24,128]{1,0:T(8,128)S(1)}, u32[]{:S(2)}, u32[]{:S(2)}) %collective-permute-start) | collective-permute-done | bytes 12320 | tf_op jit(solution)/shard_map/ppermute | solution.py:265
  61.6 0.0 copy-start
  61.6 15.9 %all_to_all.17.best_ref = f32[64,1,128]{2,1,0:T(1,128)S(1)} all-to-all(f32[64,1,128]{2,1,0:T(1,128)S(1)} %get-tuple-element.18), channel_id=1, replica_groups=mesh['seg'=64,'curve'=16] {'seg'}, dimensions={0} | all-to-all | bytes 65536 | tf_op jit(solution)/shard_map/all_to_all | solution.py:268
  77.6 0.0 copy-done
  77.6 1.3 %advance.1 = f32[2,5,16,256]{3,2,1,0:T(8,128)} custom-call(f32[8,128]{1,0:T(8,128)S(1)} %copy-done, f32[384,128]{1,0:T(8,128)S(1)} %bitcast.8, f32[24,128]{1,0:T(8,128)S(1)} %collective-permute-done.before_ref, f32[24,128]{1,0:T(8,128)S(1)} %collective-permute-done.1.after_ref, f32[64,1,128]{2,1,0:T(1,128)S(1)} %all_to_all.17.best_ref), custom_call_target="tpu_custom_call" | custom-call | tf_op jit(solution)/shard_map/advance/pallas_call | solution.py:269
  (1 shorter events, 0.0 us)
Async XLA Ops:
  43.0 12.9 %collective-permute-start.1 = (f32[24,128]{1,0:T(8,128)S(1)}, f32[24,128]{1,0:T(8,128)S(1)}, u32[]{:S(2)}, u32[]{:S(2)}) collective-permute-start(f32[24,128]{1,0:T(8,128)S(1)} %get-tuple-element.19), channel_id=1, source_target_pairs={{16,0},{32,16},{48,32},{64,48},{80,64},{96,80},{112,96},{128,112},... | collective-permute-start | bytes 36872 | tf_op jit(solution)/shard_map/ppermute | solution.py:266
  53.9 7.8 %collective-permute-start = (f32[24,128]{1,0:T(8,128)S(1)}, f32[24,128]{1,0:T(8,128)S(1)}, u32[]{:S(2)}, u32[]{:S(2)}) collective-permute-start(f32[24,128]{1,0:T(8,128)S(1)} %get-tuple-element.20), channel_id=1, source_target_pairs={{0,16},{16,32},{32,48},{48,64},{64,80},{80,96},{96,112},{112,128},... | collective-permute-start | bytes 36872 | tf_op jit(solution)/shard_map/ppermute | solution.py:265
  61.6 15.9 %copy-start = (f32[8,128]{1,0:T(8,128)S(1)}, f32[8,128]{1,0:T(8,128)}, u32[]{:S(2)}) copy-start(f32[8,128]{1,0:T(8,128)} %get-tuple-element.12.pick_ref) | copy-start | bytes 12292

commit v4 on v3

--- a/solution.py
+++ b/solution.py
@@ -57,17 +57,21 @@
     copies = [
         pltpu.make_async_copy(source, target, sems.at[i])
         for i, (source, target) in enumerate(
-            ((state_hbm, state_ref), (slot_hbm, slot_ref), (near_hbm, near_ref))
+            (
+                (state_hbm.at[0], state_ref.at[0]),
+                (state_hbm.at[1], state_ref.at[1]),
+                (slot_hbm, slot_ref),
+                (near_hbm, near_ref),
+            )
         )
     ]
     for copy in copies:
         copy.start()
-    for copy in copies:
-        copy.wait()
     count = out_ref.shape[0] // SLOT
     boxes = 2 * count
     best = None
     for box in range(2):
+        copies[box].wait()
         cell = [state_ref[box, v] for v in range(5)]
         for v in range(5):
             for half in range(2):
@@ -83,6 +87,8 @@
         local = lax.rem(index, boxes)
         return lax.rem(local, 2) * count + lax.div(local, 2)
 
+    copies[2].wait()
+    copies[3].wait()
     values = [place(slot_ref[0]), place(slot_ref[1])]
     for box in range(2):
         values += [place(near_ref[box, 2]), place(near_ref[box, 3])]
@@ -243,7 +249,7 @@
             pltpu.SMEM(new_slot.shape, jnp.int32),
             pltpu.SMEM(neighbours.shape, jnp.int32),
             pltpu.VMEM(state.shape, f32),
-            pltpu.SemaphoreType.DMA((3,)),
+            pltpu.SemaphoreType.DMA((4,)),
         ],
         name="pack",
     )(new_slot, neighbours, state)
@@ -264,7 +270,6 @@
     down = [(j, i) for i, j in up]
     before = lax.ppermute(moved[count - 1], "seg", up)
     after = lax.ppermute(moved[0], "seg", down)
-    best, before, after = lax.optimization_barrier((best, before, after))
     best = lax.all_to_all(best, "seg", 0, 0, tiled=True)
     return pl.pallas_call(
         advance_kernel,

time: 79.4 us -> 73.5 us (0.926)
  blocking collectives: 56.7 us -> 40.8 us
  starting transfers between devices: 12.8 us -> 22.4 us
    all_to_all x1 -> x0, blocking collectives: 15.9 us -> none  [local(): best = lax.all_to_all(best, 'seg', 0, 0, tiled=True)]
    all_to_all x0 -> x1, starting transfers between devices: none -> 13.9 us  [local(): best = lax.all_to_all(best, 'seg', 0, 0, tiled=True)]
    ppermute x1, starting transfers between devices: 10.9 us -> 6.55 us  [local(): after = lax.ppermute(moved[0], 'seg', down)]
    all_to_all x0 -> x1, waiting for transfers between devices: none -> 2.26 us  [local(): best = lax.all_to_all(best, 'seg', 0, 0, tiled=True)]
    ppermute x1, waiting for transfers between devices: 5.82 us -> 3.57 us  [local(): before = lax.ppermute(moved[count - 1], 'seg', up)]
  transfers between devices with their start and end apart: 2 -> 3, of which waited for: 1 -> 2; matrix products, arithmetic and copies ran while one was open for 0% -> 0% of each run, Pallas kernels for 0% -> 0%
where the time goes in v4:
time: 73.5 us; the launch traced here: 73.1 us
  blocking collectives  40.8 us (56%)
  starting transfers between devices  22.4 us (30%)
  waiting for transfers between devices  5.83 us (8%)
  Pallas kernels  4 us (5%)
    all_to_all x1, blocking collectives, local(): lax.all_to_all(sent.reshape(count, SLOT, LANES), 'curve', 0, 0, tiled=True)  27.8 us
    all_to_all x1, starting transfers between devices, local(): best = lax.all_to_all(best, 'seg', 0, 0, tiled=True)  13.9 us
    all_to_all x1, blocking collectives, local(): lax.all_to_all(routed.reshape(count, SLOT, LANES), 'curve', 0, 0, tiled=T...  13 us
    ppermute x1, starting transfers between devices, local(): after = lax.ppermute(moved[0], 'seg', down)  6.55 us
    ppermute x1, waiting for transfers between devices, local(): before = lax.ppermute(moved[count - 1], 'seg', up)  3.57 us
    all_to_all x1, waiting for transfers between devices, local(): best = lax.all_to_all(best, 'seg', 0, 0, tiled=True)  2.26 us
    ppermute x1, starting transfers between devices, local(): before = lax.ppermute(moved[count - 1], 'seg', up)  1.92 us
    pallas_call x1, Pallas kernels, local(): pl.pallas_call(pack_kernel, out_shape=(jax.ShapeDtypeStruct((SLOT * count...  1.82 us
  transfers between devices with their start and end apart: 3, of which 2 were waited for; matrix products, arithmetic and copies ran while one was open for 0% of the time, Pallas kernels for 0%

profile of v4, /device:TPU:1, one launch (start us, length us, event | category | flops | bytes accessed | tf_op | source)
XLA Modules:
  0.0 73.1 jit_solution(11851030696887496076)
XLA Ops:
  0.0 1.8 %pack.1 = (f32[384,128]{1,0:T(8,128)}, f32[8,128]{1,0:T(8,128)}) custom-call(s32[2]{0:T(128)} %slot_hbm.1, s32[2,6]{1,0:T(2,128)} %near_hbm.1, f32[2,5,16,256]{3,2,1,0:T(8,128)} %state_hbm.1), custom_call_target="tpu_custom_call" | custom-call | tf_op jit(solution)/shard_map/pack/pallas_call | solution.py:243
  1.8 27.8 %all_to_all.15 = f32[16,24,128]{2,1,0:T(8,128)S(1)} all-to-all(f32[16,24,128]{2,1,0:T(8,128)} %bitcast.11), channel_id=1, replica_groups=mesh['seg'=64,'curve'=16] {'curve'}, dimensions={0} | all-to-all | bytes 393216 | tf_op jit(solution)/shard_map/all_to_all | solution.py:256
  29.7 0.9 %route.1 = (f32[384,128]{1,0:T(8,128)S(1)}, f32[64,1,128]{2,1,0:T(1,128)}) custom-call(f32[384,128]{1,0:T(8,128)S(1)} %bitcast.9), custom_call_target="tpu_custom_call" | custom-call | tf_op jit(solution)/shard_map/route/pallas_call | solution.py:257
  30.6 13.0 %all_to_all.16 = f32[16,24,128]{2,1,0:T(8,128)S(1)} all-to-all(f32[16,24,128]{2,1,0:T(8,128)S(1)} %bitcast.10), channel_id=1, replica_groups=mesh['seg'=64,'curve'=16] {'curve'}, dimensions={0} | all-to-all | bytes 393216 | tf_op jit(solution)/shard_map/all_to_all | solution.py:268
  43.5 13.9 %all-to-all-start.2 = ((f32[64,1,128]{2,1,0:T(1,128)}), f32[64,1,128]{2,1,0:T(1,128)S(1)}, u32[]{:S(2)}, u32[]{:S(2)}) async-start(f32[64,1,128]{2,1,0:T(1,128)} %get-tuple-element.12), calls=%async_computation.2 | async-start | bytes 65536 | tf_op jit(solution)/shard_map/all_to_all | solution.py:273
  57.5 0.0 copy-start
  57.5 6.6 %collective-permute-start.1 = (f32[24,128]{1,0:T(8,128)S(1)}, f32[24,128]{1,0:T(8,128)S(1)}, u32[]{:S(2)}, u32[]{:S(2)}) collective-permute-start(f32[24,128]{1,0:T(8,128)S(1)} %get-tuple-element.13), channel_id=1, source_target_pairs={{16,0},{32,16},{48,32},{64,48},{80,64},{96,80},{112,96},{128,112},... | collective-permute-start | bytes 36872 | tf_op jit(solution)/shard_map/ppermute | solution.py:272
  64.0 1.9 %collective-permute-start = (f32[24,128]{1,0:T(8,128)S(1)}, f32[24,128]{1,0:T(8,128)S(1)}, u32[]{:S(2)}, u32[]{:S(2)}) collective-permute-start(f32[24,128]{1,0:T(8,128)S(1)} %get-tuple-element.14), channel_id=1, source_target_pairs={{0,16},{16,32},{32,48},{48,64},{64,80},{80,96},{96,112},{112,128},... | collective-permute-start | bytes 36872 | tf_op jit(solution)/shard_map/ppermute | solution.py:271
  66.0 2.3 %all-to-all-done.2.best_ref = f32[64,1,128]{2,1,0:T(1,128)S(1)} async-done(((f32[64,1,128]{2,1,0:T(1,128)}), f32[64,1,128]{2,1,0:T(1,128)S(1)}, u32[]{:S(2)}, u32[]{:S(2)}) %all-to-all-start.2) | async-done | bytes 32800 | tf_op jit(solution)/shard_map/all_to_all | solution.py:273
  68.2 0.0 collective-permute-done.1.after_ref
  68.2 3.6 %collective-permute-done.before_ref = f32[24,128]{1,0:T(8,128)S(1)} collective-permute-done((f32[24,128]{1,0:T(8,128)S(1)}, f32[24,128]{1,0:T(8,128)S(1)}, u32[]{:S(2)}, u32[]{:S(2)}) %collective-permute-start) | collective-permute-done | bytes 12320 | tf_op jit(solution)/shard_map/ppermute | solution.py:271
  71.8 0.0 copy-done
  71.8 1.3 %advance.1 = f32[2,5,16,256]{3,2,1,0:T(8,128)} custom-call(f32[8,128]{1,0:T(8,128)S(1)} %copy-done, f32[384,128]{1,0:T(8,128)S(1)} %bitcast.8, f32[24,128]{1,0:T(8,128)S(1)} %collective-permute-done.before_ref, f32[24,128]{1,0:T(8,128)S(1)} %collective-permute-done.1.after_ref, f32[64,1,128]{2,1,0:T(1,128)S(1)} %all-to-all-done.2.best_ref), custom_call_target="tpu_custom_call" | custom-call | tf_op jit(solution)/shard_map/advance/pallas_call | solution.py:274
  (1 shorter events, 0.0 us)
Async XLA Ops:
  43.5 24.7 %all-to-all-start.2 = ((f32[64,1,128]{2,1,0:T(1,128)}), f32[64,1,128]{2,1,0:T(1,128)S(1)}, u32[]{:S(2)}, u32[]{:S(2)}) async-start(f32[64,1,128]{2,1,0:T(1,128)} %get-tuple-element.12), calls=%async_computation.2 | async-start | bytes 65536 | tf_op jit(solution)/shard_map/all_to_all | solution.py:273
  57.5 14.3 %copy-start = (f32[8,128]{1,0:T(8,128)S(1)}, f32[8,128]{1,0:T(8,128)}, u32[]{:S(2)}) copy-start(f32[8,128]{1,0:T(8,128)} %get-tuple-element.9.pick_ref) | copy-start | bytes 12292
  57.5 10.8 %collective-permute-start.1 = (f32[24,128]{1,0:T(8,128)S(1)}, f32[24,128]{1,0:T(8,128)S(1)}, u32[]{:S(2)}, u32[]{:S(2)}) collective-permute-start(f32[24,128]{1,0:T(8,128)S(1)} %get-tuple-element.13), channel_id=1, source_target_pairs={{16,0},{32,16},{48,32},{64,48},{80,64},{96,80},{112,96},{128,112},... | collective-permute-start | bytes 36872 | tf_op jit(solution)/shard_map/ppermute | solution.py:272
  64.0 7.8 %collective-permute-start = (f32[24,128]{1,0:T(8,128)S(1)}, f32[24,128]{1,0:T(8,128)S(1)}, u32[]{:S(2)}, u32[]{:S(2)}) collective-permute-start(f32[24,128]{1,0:T(8,128)S(1)} %get-tuple-element.14), channel_id=1, source_target_pairs={{0,16},{16,32},{32,48},{48,64},{64,80},{80,96},{96,112},{112,128},... | collective-permute-start | bytes 36872 | tf_op jit(solution)/shard_map/ppermute | solution.py:271

commit v5 on v4

--- a/solution.py
+++ b/solution.py
@@ -1,14 +1,17 @@
+import math
+
 import jax
 import jax.numpy as jnp
 from jax import lax
 from jax.experimental import pallas as pl
 from jax.experimental.pallas import tpu as pltpu
-from jax.sharding import PartitionSpec as P
+from jax.sharding import Mesh, PartitionSpec as P
 
 gamma_ratio = 1.4
 courant = 0.3
 
 LANES = 128
+SEG = ("seg_x", "seg_z")
 ROWS = 10
 SLOT = 24
 
@@ -100,7 +103,7 @@
     for row in range(21, SLOT):
         out_ref[pl.ds(row, count, stride=SLOT), :] = jnp.zeros((count, LANES), jnp.float32)
 
-    segment = lax.axis_index("seg")
+    segment = lax.axis_index(SEG)
     lane = lane_index(pick_ref.shape)
     picks = jnp.zeros(pick_ref.shape, jnp.float32)
     for box in range(2):
@@ -166,7 +169,12 @@
         out_ref[pl.ds(22 + box, count, stride=SLOT), :] = above[rows]
 
 
-def advance_kernel(pick_ref, in_ref, before_ref, after_ref, best_ref, out_ref):
+def peak_kernel(in_ref, out_ref):
+    best = jnp.max(in_ref[...], axis=0, keepdims=True)
+    out_ref[...] = jnp.broadcast_to(best, out_ref.shape)
+
+
+def change_kernel(pick_ref, in_ref, before_ref, after_ref, out_ref):
     count = in_ref.shape[0] // SLOT
 
     def rows_of(row):
@@ -228,17 +236,25 @@
         above.append(jnp.where(deep == 15, edge, pltpu.roll(cell[v], LANES - 1, 2)))
     more = axis_change(cell, jnp.abs(velocity[2]) + sound, below, above, 2)
 
+    for v in range(5):
+        out_ref[v] = change[v] + more[v]
+
+
+def finish_kernel(in_ref, change_ref, best_ref, out_ref):
+    count = in_ref.shape[0] // SLOT
     step = courant / jnp.max(best_ref[...], axis=0)
-    for v in range(5):
-        result = cell[v] - step[None] * (change[v] + more[v])
-        for box in range(2):
+    for box in range(2):
+        for v in range(5):
             for half in range(2):
-                out_ref[box, v, :, LANES * half : LANES * (half + 1)] = result[2 * box + half]
+                cell = in_ref[pl.ds(ROWS * box + 2 * v + half, count, stride=SLOT), :]
+                columns = slice(LANES * half, LANES * (half + 1))
+                out_ref[box, v, :, columns] = cell - step * change_ref[v, 2 * box + half]
 
 
 def local(state, new_slot, neighbours):
     count = lax.axis_size("curve")
-    segs = lax.axis_size("seg")
+    along_x, along_z = (lax.axis_size(axis) for axis in SEG)
+    segs = along_x * along_z
     f32 = jnp.float32
     sent, pick = pl.pallas_call(
         pack_kernel,
@@ -258,7 +274,7 @@
         route_kernel,
         out_shape=(
             jax.ShapeDtypeStruct((SLOT * count, LANES), f32),
-            jax.ShapeDtypeStruct((segs, 1, LANES), f32),
+            jax.ShapeDtypeStruct((along_z, 1, LANES), f32),
         ),
         in_specs=[vmem],
         out_specs=(vmem, vmem),
@@ -268,21 +284,42 @@
     moved = lax.all_to_all(routed.reshape(count, SLOT, LANES), "curve", 0, 0, tiled=True)
     up = [(i, (i + 1) % segs) for i in range(segs)]
     down = [(j, i) for i, j in up]
-    before = lax.ppermute(moved[count - 1], "seg", up)
-    after = lax.ppermute(moved[0], "seg", down)
-    best = lax.all_to_all(best, "seg", 0, 0, tiled=True)
-    return pl.pallas_call(
-        advance_kernel,
-        out_shape=jax.ShapeDtypeStruct(state.shape, f32),
-        in_specs=[vmem] * 5,
+    best = lax.all_to_all(best, SEG[1], 0, 0, tiled=True)
+    before = lax.ppermute(moved[count - 1], SEG, up)
+    after = lax.ppermute(moved[0], SEG, down)
+    best = pl.pallas_call(
+        peak_kernel,
+        out_shape=jax.ShapeDtypeStruct((along_x, 1, LANES), f32),
+        in_specs=[vmem],
         out_specs=vmem,
         compiler_params=params,
-        name="advance",
-    )(pick, moved.reshape(SLOT * count, LANES), before, after, best)
+        name="peak",
+    )(best)
+    best = lax.all_to_all(best, SEG[0], 0, 0, tiled=True)
+    moved = moved.reshape(SLOT * count, LANES)
+    change = pl.pallas_call(
+        change_kernel,
+        out_shape=jax.ShapeDtypeStruct((5, 4, count, LANES), f32),
+        in_specs=[vmem] * 4,
+        out_specs=vmem,
+        compiler_params=params,
+        name="change",
+    )(pick, moved, before, after)
+    return pl.pallas_call(
+        finish_kernel,
+        out_shape=jax.ShapeDtypeStruct(state.shape, f32),
+        in_specs=[vmem] * 3,
+        out_specs=vmem,
+        compiler_params=params,
+        name="finish",
+    )(moved, change, best)
 
 
 def solution(mesh):
-    placed = P(("seg", "curve"))
+    segs, count = mesh.devices.shape
+    side_x = math.isqrt(segs)
+    grid = Mesh(mesh.devices.reshape(side_x, segs // side_x, count), SEG + ("curve",))
+    placed = P(SEG + ("curve",))
     return jax.shard_map(
-        local, mesh=mesh, in_specs=(placed, placed, placed), out_specs=placed, check_vma=False
+        local, mesh=grid, in_specs=(placed, placed, placed), out_specs=placed, check_vma=False
     )

time: 73.5 us -> 73 us (level)
  starting transfers between devices: 22.4 us -> 21.1 us
    all_to_all x1 -> x2, waiting for transfers between devices: 2.26 us -> 5.02 us  [the longest x1 5.01 us: local(): best = lax.all_to_all(best, SEG[0], 0, 0, tiled=True)]
    ppermute x2, waiting for transfers between devices: 3.57 us -> 0.91 us  [the longest x1 0.9 us: local(): before = lax.ppermute(moved[count - 1], SEG, up)]
    all_to_all x1 -> x2, starting transfers between devices: 13.9 us -> 12.3 us  [the longest x1 7.99 us: local(): best = lax.all_to_all(best, SEG[1], 0, 0, tiled=True)]
    pallas_call x1 -> x3, Pallas kernels: 1.29 us -> 1.89 us  [the longest x1 0.7 us: local(): pl.pallas_call(finish_kernel, out_shape=jax.ShapeDtypeStruct(state.shape,...]
  transfers between devices with their start and end apart: 3 -> 4, of which waited for: 2 -> 2; matrix products, arithmetic and copies ran while one was open for 0% -> 0% of each run, Pallas kernels for 0% -> 2%
where the time goes in v5:
time: 73 us; the launch traced here: 72.4 us
  blocking collectives  40.8 us (56%)
  starting transfers between devices  21.1 us (29%)
  waiting for transfers between devices  5.92 us (8%)
  Pallas kernels  4.57 us (6%)
    all_to_all x1, blocking collectives, local(): lax.all_to_all(sent.reshape(count, SLOT, LANES), 'curve', 0, 0, tiled=True)  27.8 us
    all_to_all x1, blocking collectives, local(): lax.all_to_all(routed.reshape(count, SLOT, LANES), 'curve', 0, 0, tiled=T...  13 us
    all_to_all x1, starting transfers between devices, local(): best = lax.all_to_all(best, SEG[1], 0, 0, tiled=True)  7.99 us
    ppermute x1, starting transfers between devices, local(): after = lax.ppermute(moved[0], SEG, down)  6.88 us
    all_to_all x1, waiting for transfers between devices, local(): best = lax.all_to_all(best, SEG[0], 0, 0, tiled=True)  5.01 us
    all_to_all x1, starting transfers between devices, local(): best = lax.all_to_all(best, SEG[0], 0, 0, tiled=True)  4.31 us
    ppermute x1, starting transfers between devices, local(): before = lax.ppermute(moved[count - 1], SEG, up)  1.92 us
    pallas_call x1, Pallas kernels, local(): pl.pallas_call(pack_kernel, out_shape=(jax.ShapeDtypeStruct((SLOT * count...  1.83 us
  transfers between devices with their start and end apart: 4, of which 2 were waited for; matrix products, arithmetic and copies ran while one was open for 0% of the time, Pallas kernels for 2%

profile of v5, /device:TPU:1, one launch (start us, length us, event | category | flops | bytes accessed | tf_op | source)
XLA Modules:
  0.0 72.4 jit_solution(2296032812239656671)
XLA Ops:
  0.0 1.8 %pack.1 = (f32[384,128]{1,0:T(8,128)}, f32[8,128]{1,0:T(8,128)}) custom-call(s32[2]{0:T(128)} %slot_hbm.1, s32[2,6]{1,0:T(2,128)} %near_hbm.1, f32[2,5,16,256]{3,2,1,0:T(8,128)} %state_hbm.1), custom_call_target="tpu_custom_call" | custom-call | tf_op jit(solution)/shard_map/pack/pallas_call | solution.py:259
  1.8 27.8 %all_to_all.20 = f32[16,24,128]{2,1,0:T(8,128)S(1)} all-to-all(f32[16,24,128]{2,1,0:T(8,128)} %bitcast.12), channel_id=1, replica_groups=mesh['seg_x'=8,'seg_z'=8,'curve'=16] {'curve'}, dimensions={0} | all-to-all | bytes 393216 | tf_op jit(solution)/shard_map/all_to_all | solution.py:272
  29.7 0.8 %route.1 = (f32[384,128]{1,0:T(8,128)S(1)}, f32[8,1,128]{2,1,0:T(1,128)}) custom-call(f32[384,128]{1,0:T(8,128)S(1)} %bitcast.10), custom_call_target="tpu_custom_call" | custom-call | tf_op jit(solution)/shard_map/route/pallas_call | solution.py:273
  30.5 13.0 %all_to_all.21 = f32[16,24,128]{2,1,0:T(8,128)S(1)} all-to-all(f32[16,24,128]{2,1,0:T(8,128)S(1)} %bitcast.11), channel_id=1, replica_groups=mesh['seg_x'=8,'seg_z'=8,'curve'=16] {'curve'}, dimensions={0} | all-to-all | bytes 393216 | tf_op jit(solution)/shard_map/all_to_all | solution.py:284
  43.5 8.0 %all-to-all-start.2 = ((f32[8,1,128]{2,1,0:T(1,128)}), f32[8,1,128]{2,1,0:T(1,128)S(1)}, u32[]{:S(2)}, u32[]{:S(2)}) async-start(f32[8,1,128]{2,1,0:T(1,128)} %get-tuple-element.12), calls=%async_computation.2 | async-start | bytes 8192 | tf_op jit(solution)/shard_map/all_to_all | solution.py:287
  51.5 6.9 %collective-permute-start.1 = (f32[24,128]{1,0:T(8,128)S(1)}, f32[24,128]{1,0:T(8,128)S(1)}, u32[]{:S(2)}, u32[]{:S(2)}) collective-permute-start(f32[24,128]{1,0:T(8,128)S(1)} %get-tuple-element.13), channel_id=1, source_target_pairs={{16,0},{32,16},{48,32},{64,48},{80,64},{96,80},{112,96},{128,112},... | collective-permute-start | bytes 36872 | tf_op jit(solution)/shard_map/ppermute | solution.py:289
  58.4 1.9 %collective-permute-start = (f32[24,128]{1,0:T(8,128)S(1)}, f32[24,128]{1,0:T(8,128)S(1)}, u32[]{:S(2)}, u32[]{:S(2)}) collective-permute-start(f32[24,128]{1,0:T(8,128)S(1)} %get-tuple-element.14), channel_id=1, source_target_pairs={{0,16},{16,32},{32,48},{48,64},{64,80},{80,96},{96,112},{112,128},... | collective-permute-start | bytes 36872 | tf_op jit(solution)/shard_map/ppermute | solution.py:288
  60.3 0.0 all-to-all-done.2.in_ref
  60.3 0.6 peak.1
  60.9 0.0 copy-start
  60.9 4.3 %all-to-all-start.3 = ((f32[8,1,128]{2,1,0:T(1,128)}), f32[8,1,128]{2,1,0:T(1,128)S(1)}, u32[]{:S(2)}, u32[]{:S(2)}) async-start(f32[8,1,128]{2,1,0:T(1,128)} %peak.1), calls=%async_computation.3 | async-start | bytes 8192 | tf_op jit(solution)/shard_map/all_to_all | solution.py:298
  65.2 0.0 collective-permute-done.1.after_ref
  65.2 0.9 %collective-permute-done.before_ref = f32[24,128]{1,0:T(8,128)S(1)} collective-permute-done((f32[24,128]{1,0:T(8,128)S(1)}, f32[24,128]{1,0:T(8,128)S(1)}, u32[]{:S(2)}, u32[]{:S(2)}) %collective-permute-start) | collective-permute-done | bytes 12320 | tf_op jit(solution)/shard_map/ppermute | solution.py:288
  66.1 0.0 copy-done
  66.1 0.6 change.1.change_ref
  66.7 5.0 %all-to-all-done.3.best_ref = f32[8,1,128]{2,1,0:T(1,128)S(1)} async-done(((f32[8,1,128]{2,1,0:T(1,128)}), f32[8,1,128]{2,1,0:T(1,128)S(1)}, u32[]{:S(2)}, u32[]{:S(2)}) %all-to-all-start.3) | async-done | bytes 4128 | tf_op jit(solution)/shard_map/all_to_all | solution.py:298
  71.7 0.7 finish.1
  (1 shorter events, 0.0 us)
Async XLA Ops:
  43.5 16.8 %all-to-all-start.2 = ((f32[8,1,128]{2,1,0:T(1,128)}), f32[8,1,128]{2,1,0:T(1,128)S(1)}, u32[]{:S(2)}, u32[]{:S(2)}) async-start(f32[8,1,128]{2,1,0:T(1,128)} %get-tuple-element.12), calls=%async_computation.2 | async-start | bytes 8192 | tf_op jit(solution)/shard_map/all_to_all | solution.py:287
  51.5 13.7 %collective-permute-start.1 = (f32[24,128]{1,0:T(8,128)S(1)}, f32[24,128]{1,0:T(8,128)S(1)}, u32[]{:S(2)}, u32[]{:S(2)}) collective-permute-start(f32[24,128]{1,0:T(8,128)S(1)} %get-tuple-element.13), channel_id=1, source_target_pairs={{16,0},{32,16},{48,32},{64,48},{80,64},{96,80},{112,96},{128,112},... | collective-permute-start | bytes 36872 | tf_op jit(solution)/shard_map/ppermute | solution.py:289
  58.4 7.8 %collective-permute-start = (f32[24,128]{1,0:T(8,128)S(1)}, f32[24,128]{1,0:T(8,128)S(1)}, u32[]{:S(2)}, u32[]{:S(2)}) collective-permute-start(f32[24,128]{1,0:T(8,128)S(1)} %get-tuple-element.14), channel_id=1, source_target_pairs={{0,16},{16,32},{32,48},{48,64},{64,80},{80,96},{96,112},{112,128},... | collective-permute-start | bytes 36872 | tf_op jit(solution)/shard_map/ppermute | solution.py:288
  60.9 5.2 %copy-start = (f32[8,128]{1,0:T(8,128)S(1)}, f32[8,128]{1,0:T(8,128)}, u32[]{:S(2)}) copy-start(f32[8,128]{1,0:T(8,128)} %get-tuple-element.11.pick_ref) | copy-start | bytes 12292
  60.9 10.8 %all-to-all-start.3 = ((f32[8,1,128]{2,1,0:T(1,128)}), f32[8,1,128]{2,1,0:T(1,128)S(1)}, u32[]{:S(2)}, u32[]{:S(2)}) async-start(f32[8,1,128]{2,1,0:T(1,128)} %peak.1), calls=%async_computation.3 | async-start | bytes 8192 | tf_op jit(solution)/shard_map/all_to_all | solution.py:298

commit v6 on v4

--- a/solution.py
+++ b/solution.py
@@ -11,6 +11,7 @@
 LANES = 128
 ROWS = 10
 SLOT = 24
+TOP = 96
 
 vmem = pl.BlockSpec(memory_space=pltpu.VMEM)
 hbm = pl.BlockSpec(memory_space=pltpu.HBM)
@@ -113,6 +114,13 @@
     pick_ref[...] = picks
 
 
+def peak_kernel(in_ref, out_ref):
+    count = in_ref.shape[0] // SLOT
+    header = in_ref[pl.ds(20, count, stride=SLOT), :]
+    best = jnp.max(jnp.where(lane_index(header.shape) == 6, header, 0.0), axis=0, keepdims=True)
+    out_ref[...] = jnp.broadcast_to(jnp.max(best, axis=1, keepdims=True), out_ref.shape)
+
+
 def three_parts(value):
     high = value.astype(jnp.bfloat16)
     rest = value - high.astype(jnp.float32)
@@ -126,13 +134,10 @@
     return jnp.dot(jnp.concatenate([chosen] * 3, axis=1), parts, preferred_element_type=jnp.float32)
 
 
-def route_kernel(in_ref, out_ref, best_ref):
+def route_kernel(in_ref, speed_ref, out_ref):
     count = in_ref.shape[0] // SLOT
     boxes = 2 * count
     header = in_ref[pl.ds(20, count, stride=SLOT), :]
-    best = jnp.max(jnp.where(lane_index(header.shape) == 6, header, 0.0), axis=0, keepdims=True)
-    best = jnp.max(best, axis=1, keepdims=True)
-    best_ref[...] = jnp.broadcast_to(best.reshape(1, 1, 1), best_ref.shape)
     both = jnp.concatenate([header, pltpu.roll(header, LANES - 1, 1)], axis=0)
     target = jnp.broadcast_to(jnp.transpose(both)[0:1, :], (boxes, boxes))
     index = lax.broadcasted_iota(jnp.int32, (boxes, boxes), 0).astype(jnp.float32)
@@ -158,6 +163,7 @@
     placed = gather_rows(index == target, three_parts(jnp.concatenate(columns, axis=1)))
     below = gather_rows(beside(2, 4) == target, three_parts(last))
     above = gather_rows(beside(3, 5) == target, three_parts(first))
+    below = jnp.where(lane2 >= TOP, speed_ref[0:1, :], below)
     for box in range(2):
         rows = slice(count * box, count * (box + 1))
         for row in range(ROWS):
@@ -166,43 +172,39 @@
         out_ref[pl.ds(22 + box, count, stride=SLOT), :] = above[rows]
 
 
-def advance_kernel(pick_ref, in_ref, before_ref, after_ref, best_ref, out_ref):
+def rows_of(ref, row):
+    return ref[pl.ds(row, ref.shape[0] // SLOT, stride=SLOT), :]
+
+
+def load_cells(ref):
+    return [
+        jnp.stack([rows_of(ref, ROWS * box + 2 * v + half) for box in range(2) for half in range(2)])
+        for v in range(5)
+    ]
+
+
+def pick(ref, box, face):
+    return ref[0:1, 6 * box + face : 6 * box + face + 1]
+
+
+def faces_kernel(in_ref, first_ref, last_ref, speed_ref):
     count = in_ref.shape[0] // SLOT
-
-    def rows_of(row):
-        return in_ref[pl.ds(row, count, stride=SLOT), :]
-
-    def pick(box, face):
-        return pick_ref[0:1, 6 * box + face : 6 * box + face + 1]
-
-    cell = [
-        jnp.stack([rows_of(ROWS * box + 2 * v + half) for box in range(2) for half in range(2)]) for v in range(5)
-    ]
+    speeds = rows_of(in_ref, 20)
+    best = jnp.max(jnp.where(lane_index(speeds.shape) >= TOP, speeds, 0.0), axis=0, keepdims=True)
+    best = jnp.max(best, axis=1, keepdims=True)
+    row = lax.broadcasted_iota(jnp.int32, first_ref.shape, 0)
+    first_ref[...] = jnp.where(row < 2 * ROWS, in_ref[0:SLOT, :], best)
+    last_ref[...] = jnp.where(row < 2 * ROWS, in_ref[SLOT * (count - 1) : SLOT * count, :], best)
+    speed_ref[...] = jnp.broadcast_to(best, speed_ref.shape)
+
+
+def planes_kernel(pick_ref, in_ref, out_ref):
+    cell = load_cells(in_ref)
     velocity, _, sound = primitives(cell)
     lane = lane_index(cell[0].shape)
 
-    own = (in_ref[SLOT * (count - 1) : SLOT * count, :], in_ref[0:SLOT, :])
-    other = (before_ref[...], after_ref[...])
-    ghosts = []
-    for face in range(2):
-        for box in range(2):
-            wanted = pick(box, face)
-            rows = jnp.where(wanted >= 2.0, own[face], other[face])
-            first = (wanted == 0.0) | (wanted == 2.0)
-            ghosts.append(jnp.where(first, rows[0:ROWS], rows[ROWS : 2 * ROWS]))
-    layer = lax.broadcasted_iota(jnp.int32, cell[0].shape, 1)
-    below, above = [], []
-    for v in range(5):
-
-        def spread(rows):
-            return jnp.stack([rows[box][2 * v + half : 2 * v + half + 1] for box in range(2) for half in range(2)])
-
-        below.append(jnp.where(layer == 0, spread(ghosts[0:2]), pltpu.roll(cell[v], 1, 1)))
-        above.append(jnp.where(layer == count - 1, spread(ghosts[2:4]), pltpu.roll(cell[v], count - 1, 1)))
-    change = axis_change(cell, jnp.abs(velocity[0]) + sound, below, above, 0)
-
-    ghost_low = [rows_of(20 + box) for box in range(2)]
-    ghost_high = [rows_of(22 + box) for box in range(2)]
+    ghost_low = [rows_of(in_ref, 20 + box) for box in range(2)]
+    ghost_high = [rows_of(in_ref, 22 + box) for box in range(2)]
     below, above = [], []
     for v in range(5):
         low = [pltpu.roll(g, LANES - 16 * v, 1) if v else g for g in ghost_low]
@@ -213,12 +215,11 @@
         rolled = pltpu.roll(cell[v], LANES - 16, 2)
         edge = jnp.stack([rolled[1], high[0], rolled[3], high[1]])
         above.append(jnp.where(lane >= LANES - 16, edge, rolled))
-    more = axis_change(cell, jnp.abs(velocity[1]) + sound, below, above, 1)
-    change = [change[v] + more[v] for v in range(5)]
+    change = axis_change(cell, jnp.abs(velocity[1]) + sound, below, above, 1)
 
     deep = lane & 15
     below, above = [], []
-    slots = [[pick(box, face) == 0.0 for box in range(2)] for face in (4, 5)]
+    slots = [[pick(pick_ref, box, face) == 0.0 for box in range(2)] for face in (4, 5)]
     for v in range(5):
         wrapped = pltpu.roll(cell[v], LANES - 15, 2)
         edge = jnp.concatenate([jnp.where(slots[0][box], wrapped[0:2], wrapped[2:4]) for box in range(2)], axis=0)
@@ -228,9 +229,40 @@
         above.append(jnp.where(deep == 15, edge, pltpu.roll(cell[v], LANES - 1, 2)))
     more = axis_change(cell, jnp.abs(velocity[2]) + sound, below, above, 2)
 
-    step = courant / jnp.max(best_ref[...], axis=0)
-    for v in range(5):
-        result = cell[v] - step[None] * (change[v] + more[v])
+    for v in range(5):
+        out_ref[v] = change[v] + more[v]
+
+
+def finish_kernel(pick_ref, in_ref, change_ref, before_ref, after_ref, speed_ref, beyond_ref, out_ref):
+    count = in_ref.shape[0] // SLOT
+    cell = load_cells(in_ref)
+    velocity, _, sound = primitives(cell)
+    own = (in_ref[SLOT * (count - 1) : SLOT * count, :], in_ref[0:SLOT, :])
+    other = (before_ref[...], after_ref[...])
+    ghosts = []
+    for face in range(2):
+        for box in range(2):
+            wanted = pick(pick_ref, box, face)
+            rows = jnp.where(wanted >= 2.0, own[face], other[face])
+            first = (wanted == 0.0) | (wanted == 2.0)
+            ghosts.append(jnp.where(first, rows[0:ROWS], rows[ROWS : 2 * ROWS]))
+    layer = lax.broadcasted_iota(jnp.int32, cell[0].shape, 1)
+    below, above = [], []
+    for v in range(5):
+
+        def spread(rows):
+            return jnp.stack([rows[box][2 * v + half : 2 * v + half + 1] for box in range(2) for half in range(2)])
+
+        below.append(jnp.where(layer == 0, spread(ghosts[0:2]), pltpu.roll(cell[v], 1, 1)))
+        above.append(jnp.where(layer == count - 1, spread(ghosts[2:4]), pltpu.roll(cell[v], count - 1, 1)))
+    change = axis_change(cell, jnp.abs(velocity[0]) + sound, below, above, 0)
+
+    row = 2 * ROWS
+    best = jnp.maximum(speed_ref[0:1, :], beyond_ref[0:1, :])
+    best = jnp.maximum(best, jnp.maximum(before_ref[row : row + 1, :], after_ref[row : row + 1, :]))
+    step = courant / best
+    for v in range(5):
+        result = cell[v] - step[None] * (change[v] + change_ref[v])
         for box in range(2):
             for half in range(2):
                 out_ref[box, v, :, LANES * half : LANES * (half + 1)] = result[2 * box + half]
@@ -239,6 +271,7 @@
 def local(state, new_slot, neighbours):
     count = lax.axis_size("curve")
     segs = lax.axis_size("seg")
+    assert segs % 4 == 0 and segs <= 4 * count
     f32 = jnp.float32
     sent, pick = pl.pallas_call(
         pack_kernel,
@@ -254,31 +287,58 @@
         name="pack",
     )(new_slot, neighbours, state)
     met = lax.all_to_all(sent.reshape(count, SLOT, LANES), "curve", 0, 0, tiled=True)
-    routed, best = pl.pallas_call(
+    met = met.reshape(SLOT * count, LANES)
+    speed = pl.pallas_call(
+        peak_kernel,
+        out_shape=jax.ShapeDtypeStruct((8, LANES), f32),
+        in_specs=[vmem],
+        out_specs=vmem,
+        compiler_params=params,
+        name="peak",
+    )(met)
+    spread = [((s + 4 * c) % segs * count + c, s * count + c) for s in range(segs) for c in range(count)]
+    speed = lax.ppermute(speed, ("seg", "curve"), spread)
+    routed = pl.pallas_call(
         route_kernel,
+        out_shape=jax.ShapeDtypeStruct((SLOT * count, LANES), f32),
+        in_specs=[vmem, vmem],
+        out_specs=vmem,
+        compiler_params=params,
+        name="route",
+    )(met, speed)
+    moved = lax.all_to_all(routed.reshape(count, SLOT, LANES), "curve", 0, 0, tiled=True)
+    moved = moved.reshape(SLOT * count, LANES)
+    first, last, speed = pl.pallas_call(
+        faces_kernel,
         out_shape=(
-            jax.ShapeDtypeStruct((SLOT * count, LANES), f32),
-            jax.ShapeDtypeStruct((segs, 1, LANES), f32),
+            jax.ShapeDtypeStruct((SLOT, LANES), f32),
+            jax.ShapeDtypeStruct((SLOT, LANES), f32),
+            jax.ShapeDtypeStruct((8, LANES), f32),
         ),
         in_specs=[vmem],
-        out_specs=(vmem, vmem),
-        compiler_params=params,
-        name="route",
-    )(met.reshape(SLOT * count, LANES))
-    moved = lax.all_to_all(routed.reshape(count, SLOT, LANES), "curve", 0, 0, tiled=True)
-    up = [(i, (i + 1) % segs) for i in range(segs)]
-    down = [(j, i) for i, j in up]
-    before = lax.ppermute(moved[count - 1], "seg", up)
-    after = lax.ppermute(moved[0], "seg", down)
-    best = lax.all_to_all(best, "seg", 0, 0, tiled=True)
+        out_specs=(vmem, vmem, vmem),
+        compiler_params=params,
+        name="faces",
+    )(moved)
+    before = lax.ppermute(last, "seg", [(i, (i + 1) % segs) for i in range(segs)])
+    after = lax.ppermute(first, "seg", [((i + 1) % segs, i) for i in range(segs)])
+    beyond = lax.ppermute(speed, "seg", [((i + 2) % segs, i) for i in range(segs)])
+    change = pl.pallas_call(
+        planes_kernel,
+        out_shape=jax.ShapeDtypeStruct((5, 4, count, LANES), f32),
+        in_specs=[vmem, vmem],
+        out_specs=vmem,
+        compiler_params=params,
+        name="planes",
+    )(pick, moved)
     return pl.pallas_call(
-        advance_kernel,
+        finish_kernel,
         out_shape=jax.ShapeDtypeStruct(state.shape, f32),
-        in_specs=[vmem] * 5,
+        in_specs=[vmem] * 7,
         out_specs=vmem,
         compiler_params=params,
-        name="advance",
-    )(pick, moved.reshape(SLOT * count, LANES), before, after, best)
+        name="finish",
+    )(pick, moved, change, before, after, speed, beyond)
 
 
 def solution(mesh):

time: 73.5 us -> 75.4 us (1.026)
  blocking collectives: 40.8 us -> 44.7 us
  waiting for transfers between devices: 5.83 us -> 2.39 us
  starting transfers between devices: 22.4 us -> 24.1 us
    ppermute x2 -> x4, starting transfers between devices: 8.47 us -> 24.1 us  [the longest x1 10 us: local(): lax.ppermute(first, 'seg', [((i + 1) % segs, i) for i in range(segs)])]
    all_to_all x1 -> x0, starting transfers between devices: 13.9 us -> none  [local(): best = lax.all_to_all(best, 'seg', 0, 0, tiled=True)]
    all_to_all x1, blocking collectives: 13 us -> 16.9 us  [local(): lax.all_to_all(routed.reshape(count, SLOT, LANES), 'curve', 0, 0, tiled=T...]
    all_to_all x1 -> x0, waiting for transfers between devices: 2.26 us -> none  [local(): best = lax.all_to_all(best, 'seg', 0, 0, tiled=True)]
    ppermute x2 -> x4, waiting for transfers between devices: 3.57 us -> 2.39 us  [the longest x1 1.65 us: local(): lax.ppermute(speed, 'seg', [((i + 2) % segs, i) for i in range(segs)])]
    pallas_call x2 -> x5, Pallas kernels: 2.18 us -> 1.94 us  [the longest x1 0.91 us: local(): pl.pallas_call(finish_kernel, out_shape=jax.ShapeDtypeStruct(state.shape,...]
  transfers between devices with their start and end apart: 3 -> 4, of which waited for: 2 -> 2; matrix products, arithmetic and copies ran while one was open for 0% -> 0% of each run, Pallas kernels for 0% -> 1%
where the time goes in v6:
time: 75.4 us; the launch traced here: 75 us
  blocking collectives  44.7 us (59%)
  starting transfers between devices  24.1 us (32%)
  Pallas kernels  3.76 us (5%)
  waiting for transfers between devices  2.39 us (3%)
    all_to_all x1, blocking collectives, local(): lax.all_to_all(sent.reshape(count, SLOT, LANES), 'curve', 0, 0, tiled=True)  27.8 us
    all_to_all x1, blocking collectives, local(): lax.all_to_all(routed.reshape(count, SLOT, LANES), 'curve', 0, 0, tiled=T...  16.9 us
    ppermute x1, starting transfers between devices, local(): lax.ppermute(first, 'seg', [((i + 1) % segs, i) for i in range(segs)])  10 us
    ppermute x1, starting transfers between devices, local(): speed = lax.ppermute(speed, ('seg', 'curve'), spread)  8.14 us
    ppermute x1, starting transfers between devices, local(): lax.ppermute(speed, 'seg', [((i + 2) % segs, i) for i in range(segs)])  3.09 us
    ppermute x1, starting transfers between devices, local(): lax.ppermute(last, 'seg', [(i, (i + 1) % segs) for i in range(segs)])  2.83 us
    pallas_call x1, Pallas kernels, local(): pl.pallas_call(pack_kernel, out_shape=(jax.ShapeDtypeStruct((SLOT * count...  1.82 us
    ppermute x1, waiting for transfers between devices, local(): lax.ppermute(speed, 'seg', [((i + 2) % segs, i) for i in range(segs)])  1.65 us
  transfers between devices with their start and end apart: 4, of which 2 were waited for; matrix products, arithmetic and copies ran while one was open for 0% of the time, Pallas kernels for 1%

profile of v6, /device:TPU:1, one launch (start us, length us, event | category | flops | bytes accessed | tf_op | source)
XLA Modules:
  0.0 75.0 jit_solution(13726264768446943666)
XLA Ops:
  0.0 1.8 %pack.1 = (f32[384,128]{1,0:T(8,128)}, f32[8,128]{1,0:T(8,128)}) custom-call(s32[2]{0:T(128)} %slot_hbm.1, s32[2,6]{1,0:T(2,128)} %near_hbm.1, f32[2,5,16,256]{3,2,1,0:T(8,128)} %state_hbm.1), custom_call_target="tpu_custom_call" | custom-call | tf_op jit(solution)/shard_map/pack/pallas_call | solution.py:276
  1.8 27.8 %all_to_all.10 = f32[16,24,128]{2,1,0:T(8,128)S(1)} all-to-all(f32[16,24,128]{2,1,0:T(8,128)} %bitcast.10), channel_id=1, replica_groups=mesh['seg'=64,'curve'=16] {'curve'}, dimensions={0} | all-to-all | bytes 393216 | tf_op jit(solution)/shard_map/all_to_all | solution.py:289
  29.7 0.1 peak.1
  29.8 8.1 %collective-permute-start = (f32[8,128]{1,0:T(8,128)S(1)}, f32[8,128]{1,0:T(8,128)S(1)}, u32[]{:S(2)}, u32[]{:S(2)}) collective-permute-start(f32[8,128]{1,0:T(8,128)S(1)} %peak.1), channel_id=1, source_target_pairs={{0,0},{65,1},{130,2},{195,3},{260,4},{325,5},{390,6},{455,7},{520,... | collective-permute-start | bytes 12296 | tf_op jit(solution)/shard_map/ppermute | solution.py:300
  37.9 0.7 collective-permute-done.speed_ref
  38.6 0.4 route.1
  39.0 16.9 %all_to_all.11 = f32[16,24,128]{2,1,0:T(8,128)S(1)} all-to-all(f32[16,24,128]{2,1,0:T(8,128)S(1)} %bitcast.9), channel_id=1, replica_groups=mesh['seg'=64,'curve'=16] {'curve'}, dimensions={0} | all-to-all | bytes 393216 | tf_op jit(solution)/shard_map/all_to_all | solution.py:309
  55.9 0.1 faces.1
  56.0 0.0 copy-start
  56.0 2.8 %collective-permute-start.1 = (f32[24,128]{1,0:T(8,128)S(1)}, f32[24,128]{1,0:T(8,128)S(1)}, u32[]{:S(2)}, u32[]{:S(2)}) collective-permute-start(f32[24,128]{1,0:T(8,128)S(1)} %get-tuple-element.12), channel_id=1, source_target_pairs={{0,16},{16,32},{32,48},{48,64},{64,80},{80,96},{96,112},{112,128},... | collective-permute-start | bytes 36872 | tf_op jit(solution)/shard_map/ppermute | solution.py:323
  58.8 10.0 %collective-permute-start.2 = (f32[24,128]{1,0:T(8,128)S(1)}, f32[24,128]{1,0:T(8,128)S(1)}, u32[]{:S(2)}, u32[]{:S(2)}) collective-permute-start(f32[24,128]{1,0:T(8,128)S(1)} %get-tuple-element.13), channel_id=1, source_target_pairs={{16,0},{32,16},{48,32},{64,48},{80,64},{96,80},{112,96},{128,112},... | collective-permute-start | bytes 36872 | tf_op jit(solution)/shard_map/ppermute | solution.py:324
  68.9 3.1 %collective-permute-start.3 = (f32[8,128]{1,0:T(8,128)S(1)}, f32[8,128]{1,0:T(8,128)S(1)}, u32[]{:S(2)}, u32[]{:S(2)}) collective-permute-start(f32[8,128]{1,0:T(8,128)S(1)} %get-tuple-element.14.speed_ref), channel_id=1, source_target_pairs={{32,0},{48,16},{64,32},{80,48},{96,64},{112,80},{128,96},{144,112}... | collective-permute-start | bytes 12296 | tf_op jit(solution)/shard_map/ppermute | solution.py:325
  72.0 0.0 copy-done
  72.0 0.5 planes.1.change_ref
  72.5 1.6 %collective-permute-done.3.beyond_ref = f32[8,128]{1,0:T(8,128)S(1)} collective-permute-done((f32[8,128]{1,0:T(8,128)S(1)}, f32[8,128]{1,0:T(8,128)S(1)}, u32[]{:S(2)}, u32[]{:S(2)}) %collective-permute-start.3) | collective-permute-done | bytes 4128 | tf_op jit(solution)/shard_map/ppermute | solution.py:325
  74.1 0.0 collective-permute-done.1.before_ref
  74.1 0.0 collective-permute-done.2.after_ref
  74.1 0.9 %finish.1 = f32[2,5,16,256]{3,2,1,0:T(8,128)} custom-call(f32[8,128]{1,0:T(8,128)S(1)} %copy-done, f32[384,128]{1,0:T(8,128)S(1)} %bitcast.6, f32[5,4,16,128]{3,2,1,0:T(8,128)S(1)} %planes.1.change_ref, f32[24,128]{1,0:T(8,128)S(1)} %collective-permute-done.1.before_ref, f32[24,128]{1,0:T(8,128)S(1)} %collective-permute-done.2.after_ref, ...), custom_call_target="tpu_custom_call" | custom-call | tf_op jit(solution)/shard_map/finish/pallas_call | solution.py:334
Async XLA Ops:
  29.8 8.9 %collective-permute-start = (f32[8,128]{1,0:T(8,128)S(1)}, f32[8,128]{1,0:T(8,128)S(1)}, u32[]{:S(2)}, u32[]{:S(2)}) collective-permute-start(f32[8,128]{1,0:T(8,128)S(1)} %peak.1), channel_id=1, source_target_pairs={{0,0},{65,1},{130,2},{195,3},{260,4},{325,5},{390,6},{455,7},{520,... | collective-permute-start | bytes 12296 | tf_op jit(solution)/shard_map/ppermute | solution.py:300
  56.0 16.0 %copy-start = (f32[8,128]{1,0:T(8,128)S(1)}, f32[8,128]{1,0:T(8,128)}, u32[]{:S(2)}) copy-start(f32[8,128]{1,0:T(8,128)} %get-tuple-element.10.pick_ref) | copy-start | bytes 12292
  56.0 18.1 %collective-permute-start.1 = (f32[24,128]{1,0:T(8,128)S(1)}, f32[24,128]{1,0:T(8,128)S(1)}, u32[]{:S(2)}, u32[]{:S(2)}) collective-permute-start(f32[24,128]{1,0:T(8,128)S(1)} %get-tuple-element.12), channel_id=1, source_target_pairs={{0,16},{16,32},{32,48},{48,64},{64,80},{80,96},{96,112},{112,128},... | collective-permute-start | bytes 36872 | tf_op jit(solution)/shard_map/ppermute | solution.py:323
  58.8 15.3 %collective-permute-start.2 = (f32[24,128]{1,0:T(8,128)S(1)}, f32[24,128]{1,0:T(8,128)S(1)}, u32[]{:S(2)}, u32[]{:S(2)}) collective-permute-start(f32[24,128]{1,0:T(8,128)S(1)} %get-tuple-element.13), channel_id=1, source_target_pairs={{16,0},{32,16},{48,32},{64,48},{80,64},{96,80},{112,96},{128,112},... | collective-permute-start | bytes 36872 | tf_op jit(solution)/shard_map/ppermute | solution.py:324
  68.9 5.3 %collective-permute-start.3 = (f32[8,128]{1,0:T(8,128)S(1)}, f32[8,128]{1,0:T(8,128)S(1)}, u32[]{:S(2)}, u32[]{:S(2)}) collective-permute-start(f32[8,128]{1,0:T(8,128)S(1)} %get-tuple-element.14.speed_ref), channel_id=1, source_target_pairs={{32,0},{48,16},{64,32},{80,48},{96,64},{112,80},{128,96},{144,112}... | collective-permute-start | bytes 12296 | tf_op jit(solution)/shard_map/ppermute | solution.py:325

commit v7 on v5

--- a/solution.py
+++ b/solution.py
@@ -274,7 +274,7 @@
         route_kernel,
         out_shape=(
             jax.ShapeDtypeStruct((SLOT * count, LANES), f32),
-            jax.ShapeDtypeStruct((along_z, 1, LANES), f32),
+            jax.ShapeDtypeStruct((along_x, 1, LANES), f32),
         ),
         in_specs=[vmem],
         out_specs=(vmem, vmem),
@@ -284,18 +284,18 @@
     moved = lax.all_to_all(routed.reshape(count, SLOT, LANES), "curve", 0, 0, tiled=True)
     up = [(i, (i + 1) % segs) for i in range(segs)]
     down = [(j, i) for i, j in up]
-    best = lax.all_to_all(best, SEG[1], 0, 0, tiled=True)
+    best = lax.all_to_all(best, SEG[0], 0, 0, tiled=True)
     before = lax.ppermute(moved[count - 1], SEG, up)
     after = lax.ppermute(moved[0], SEG, down)
     best = pl.pallas_call(
         peak_kernel,
-        out_shape=jax.ShapeDtypeStruct((along_x, 1, LANES), f32),
+        out_shape=jax.ShapeDtypeStruct((along_z, 1, LANES), f32),
         in_specs=[vmem],
         out_specs=vmem,
         compiler_params=params,
         name="peak",
     )(best)
-    best = lax.all_to_all(best, SEG[0], 0, 0, tiled=True)
+    best = lax.all_to_all(best, SEG[1], 0, 0, tiled=True)
     moved = moved.reshape(SLOT * count, LANES)
     change = pl.pallas_call(
         change_kernel,

time: 73 us -> 75.9 us (1.040)
  the two profiles are of different devices: /device:TPU:1 before, /device:TPU:6 now
where the time goes in v7:
time: 75.9 us; the launch traced here: 75.5 us
  starting transfers between devices  33.2 us (44%)
  blocking collectives  30.6 us (40%)
  waiting for transfers between devices  7.05 us (9%)
  Pallas kernels  4.57 us (6%)
    all_to_all x1, blocking collectives, local(): lax.all_to_all(sent.reshape(count, SLOT, LANES), 'curve', 0, 0, tiled=True)  17.6 us
    all_to_all x1, blocking collectives, local(): lax.all_to_all(routed.reshape(count, SLOT, LANES), 'curve', 0, 0, tiled=T...  13 us
    ppermute x1, starting transfers between devices, local(): after = lax.ppermute(moved[0], SEG, down)  12.4 us
    all_to_all x1, starting transfers between devices, local(): best = lax.all_to_all(best, SEG[0], 0, 0, tiled=True)  12.1 us
    all_to_all x1, waiting for transfers between devices, local(): best = lax.all_to_all(best, SEG[1], 0, 0, tiled=True)  7.04 us
    all_to_all x1, starting transfers between devices, local(): best = lax.all_to_all(best, SEG[1], 0, 0, tiled=True)  6.74 us
    ppermute x1, starting transfers between devices, local(): before = lax.ppermute(moved[count - 1], SEG, up)  1.92 us
    pallas_call x1, Pallas kernels, local(): pl.pallas_call(pack_kernel, out_shape=(jax.ShapeDtypeStruct((SLOT * count...  1.83 us
  transfers between devices with their start and end apart: 4, of which 1 were waited for; matrix products, arithmetic and copies ran while one was open for 0% of the time, Pallas kernels for 2%

profile of v7, /device:TPU:6, one launch (start us, length us, event | category | flops | bytes accessed | tf_op | source)
XLA Modules:
  0.0 75.5 jit_solution(13819101820127412282)
XLA Ops:
  0.0 1.8 %pack.1 = (f32[384,128]{1,0:T(8,128)}, f32[8,128]{1,0:T(8,128)}) custom-call(s32[2]{0:T(128)} %slot_hbm.1, s32[2,6]{1,0:T(2,128)} %near_hbm.1, f32[2,5,16,256]{3,2,1,0:T(8,128)} %state_hbm.1), custom_call_target="tpu_custom_call" | custom-call | tf_op jit(solution)/shard_map/pack/pallas_call | solution.py:259
  1.8 17.6 %all_to_all.20 = f32[16,24,128]{2,1,0:T(8,128)S(1)} all-to-all(f32[16,24,128]{2,1,0:T(8,128)} %bitcast.12), channel_id=1, replica_groups=mesh['seg_x'=8,'seg_z'=8,'curve'=16] {'curve'}, dimensions={0} | all-to-all | bytes 393216 | tf_op jit(solution)/shard_map/all_to_all | solution.py:272
  19.5 0.8 %route.1 = (f32[384,128]{1,0:T(8,128)S(1)}, f32[8,1,128]{2,1,0:T(1,128)}) custom-call(f32[384,128]{1,0:T(8,128)S(1)} %bitcast.10), custom_call_target="tpu_custom_call" | custom-call | tf_op jit(solution)/shard_map/route/pallas_call | solution.py:273
  20.3 13.0 %all_to_all.21 = f32[16,24,128]{2,1,0:T(8,128)S(1)} all-to-all(f32[16,24,128]{2,1,0:T(8,128)S(1)} %bitcast.11), channel_id=1, replica_groups=mesh['seg_x'=8,'seg_z'=8,'curve'=16] {'curve'}, dimensions={0} | all-to-all | bytes 393216 | tf_op jit(solution)/shard_map/all_to_all | solution.py:284
  33.3 12.1 %all-to-all-start.2 = ((f32[8,1,128]{2,1,0:T(1,128)}), f32[8,1,128]{2,1,0:T(1,128)S(1)}, u32[]{:S(2)}, u32[]{:S(2)}) async-start(f32[8,1,128]{2,1,0:T(1,128)} %get-tuple-element.12), calls=%async_computation.2 | async-start | bytes 8192 | tf_op jit(solution)/shard_map/all_to_all | solution.py:287
  45.4 12.4 %collective-permute-start.1 = (f32[24,128]{1,0:T(8,128)S(1)}, f32[24,128]{1,0:T(8,128)S(1)}, u32[]{:S(2)}, u32[]{:S(2)}) collective-permute-start(f32[24,128]{1,0:T(8,128)S(1)} %get-tuple-element.13), channel_id=1, source_target_pairs={{16,0},{32,16},{48,32},{64,48},{80,64},{96,80},{112,96},{128,112},... | collective-permute-start | bytes 36872 | tf_op jit(solution)/shard_map/ppermute | solution.py:289
  57.8 1.9 %collective-permute-start = (f32[24,128]{1,0:T(8,128)S(1)}, f32[24,128]{1,0:T(8,128)S(1)}, u32[]{:S(2)}, u32[]{:S(2)}) collective-permute-start(f32[24,128]{1,0:T(8,128)S(1)} %get-tuple-element.14), channel_id=1, source_target_pairs={{0,16},{16,32},{32,48},{48,64},{64,80},{80,96},{96,112},{112,128},... | collective-permute-start | bytes 36872 | tf_op jit(solution)/shard_map/ppermute | solution.py:288
  59.8 0.0 all-to-all-done.2.in_ref
  59.8 0.6 peak.1
  60.4 0.0 copy-start
  60.4 6.7 %all-to-all-start.3 = ((f32[8,1,128]{2,1,0:T(1,128)}), f32[8,1,128]{2,1,0:T(1,128)S(1)}, u32[]{:S(2)}, u32[]{:S(2)}) async-start(f32[8,1,128]{2,1,0:T(1,128)} %peak.1), calls=%async_computation.3 | async-start | bytes 8192 | tf_op jit(solution)/shard_map/all_to_all | solution.py:298
  67.1 0.0 collective-permute-done.1.after_ref
  67.1 0.0 collective-permute-done.before_ref
  67.1 0.0 copy-done
  67.2 0.6 change.1.change_ref
  67.8 7.0 %all-to-all-done.3.best_ref = f32[8,1,128]{2,1,0:T(1,128)S(1)} async-done(((f32[8,1,128]{2,1,0:T(1,128)}), f32[8,1,128]{2,1,0:T(1,128)S(1)}, u32[]{:S(2)}, u32[]{:S(2)}) %all-to-all-start.3) | async-done | bytes 4128 | tf_op jit(solution)/shard_map/all_to_all | solution.py:298
  74.8 0.7 finish.1
  (1 shorter events, 0.0 us)
Async XLA Ops:
  33.3 26.5 %all-to-all-start.2 = ((f32[8,1,128]{2,1,0:T(1,128)}), f32[8,1,128]{2,1,0:T(1,128)S(1)}, u32[]{:S(2)}, u32[]{:S(2)}) async-start(f32[8,1,128]{2,1,0:T(1,128)} %get-tuple-element.12), calls=%async_computation.2 | async-start | bytes 8192 | tf_op jit(solution)/shard_map/all_to_all | solution.py:287
  45.4 21.7 %collective-permute-start.1 = (f32[24,128]{1,0:T(8,128)S(1)}, f32[24,128]{1,0:T(8,128)S(1)}, u32[]{:S(2)}, u32[]{:S(2)}) collective-permute-start(f32[24,128]{1,0:T(8,128)S(1)} %get-tuple-element.13), channel_id=1, source_target_pairs={{16,0},{32,16},{48,32},{64,48},{80,64},{96,80},{112,96},{128,112},... | collective-permute-start | bytes 36872 | tf_op jit(solution)/shard_map/ppermute | solution.py:289
  57.8 9.3 %collective-permute-start = (f32[24,128]{1,0:T(8,128)S(1)}, f32[24,128]{1,0:T(8,128)S(1)}, u32[]{:S(2)}, u32[]{:S(2)}) collective-permute-start(f32[24,128]{1,0:T(8,128)S(1)} %get-tuple-element.14), channel_id=1, source_target_pairs={{0,16},{16,32},{32,48},{48,64},{64,80},{80,96},{96,112},{112,128},... | collective-permute-start | bytes 36872 | tf_op jit(solution)/shard_map/ppermute | solution.py:288
  60.4 6.8 %copy-start = (f32[8,128]{1,0:T(8,128)S(1)}, f32[8,128]{1,0:T(8,128)}, u32[]{:S(2)}) copy-start(f32[8,128]{1,0:T(8,128)} %get-tuple-element.11.pick_ref) | copy-start | bytes 12292
  60.4 14.4 %all-to-all-start.3 = ((f32[8,1,128]{2,1,0:T(1,128)}), f32[8,1,128]{2,1,0:T(1,128)S(1)}, u32[]{:S(2)}, u32[]{:S(2)}) async-start(f32[8,1,128]{2,1,0:T(1,128)} %peak.1), calls=%async_computation.3 | async-start | bytes 8192 | tf_op jit(solution)/shard_map/all_to_all | solution.py:298

commit v8 on v4

--- a/solution.py
+++ b/solution.py
@@ -11,6 +11,7 @@
 LANES = 128
 ROWS = 10
 SLOT = 24
+WIDE = 48
 
 vmem = pl.BlockSpec(memory_space=pltpu.VMEM)
 hbm = pl.BlockSpec(memory_space=pltpu.HBM)
@@ -53,7 +54,9 @@
     ]
 
 
-def pack_kernel(slot_hbm, near_hbm, state_hbm, out_ref, pick_ref, slot_ref, near_ref, state_ref, sems):
+def pack_kernel(
+    slot_hbm, near_hbm, state_hbm, out_ref, first_ref, last_ref, pick_ref, slot_ref, near_ref, state_ref, sems
+):
     copies = [
         pltpu.make_async_copy(source, target, sems.at[i])
         for i, (source, target) in enumerate(
@@ -76,7 +79,10 @@
         for v in range(5):
             for half in range(2):
                 row = ROWS * box + 2 * v + half
-                out_ref[pl.ds(row, count, stride=SLOT), :] = cell[v][:, LANES * half : LANES * (half + 1)]
+                part = cell[v][:, LANES * half : LANES * (half + 1)]
+                out_ref[pl.ds(row, count, stride=SLOT), :] = part
+                first_ref[row : row + 1, :] = part[0:1]
+                last_ref[row : row + 1, :] = part[count - 1 : count]
         velocity, _, sound = primitives(cell)
         largest = jnp.maximum(jnp.maximum(jnp.abs(velocity[0]), jnp.abs(velocity[1])), jnp.abs(velocity[2]))
         speed = largest + sound
@@ -97,6 +103,8 @@
     for position, value in enumerate(values):
         header = jnp.where(lane == position, value.astype(jnp.float32), header)
     out_ref[pl.ds(20, count, stride=SLOT), :] = header
+    first_ref[2 * ROWS : SLOT, :] = header[0 : SLOT - 2 * ROWS]
+    last_ref[2 * ROWS : SLOT, :] = header[0 : SLOT - 2 * ROWS]
     for row in range(21, SLOT):
         out_ref[pl.ds(row, count, stride=SLOT), :] = jnp.zeros((count, LANES), jnp.float32)
 
@@ -126,11 +134,12 @@
     return jnp.dot(jnp.concatenate([chosen] * 3, axis=1), parts, preferred_element_type=jnp.float32)
 
 
-def route_kernel(in_ref, out_ref, best_ref):
+def route_kernel(in_ref, before_ref, after_ref, out_ref, best_ref):
     count = in_ref.shape[0] // SLOT
     boxes = 2 * count
     header = in_ref[pl.ds(20, count, stride=SLOT), :]
-    best = jnp.max(jnp.where(lane_index(header.shape) == 6, header, 0.0), axis=0, keepdims=True)
+    lane = lane_index((count, LANES))
+    best = jnp.max(jnp.where(lane == 6, header, 0.0), axis=0, keepdims=True)
     best = jnp.max(best, axis=1, keepdims=True)
     best_ref[...] = jnp.broadcast_to(best.reshape(1, 1, 1), best_ref.shape)
     both = jnp.concatenate([header, pltpu.roll(header, LANES - 1, 1)], axis=0)
@@ -161,16 +170,31 @@
     for box in range(2):
         rows = slice(count * box, count * (box + 1))
         for row in range(ROWS):
-            out_ref[pl.ds(ROWS * box + row, count, stride=SLOT), :] = placed[rows, LANES * row : LANES * (row + 1)]
-        out_ref[pl.ds(20 + box, count, stride=SLOT), :] = below[rows]
-        out_ref[pl.ds(22 + box, count, stride=SLOT), :] = above[rows]
-
-
-def advance_kernel(pick_ref, in_ref, before_ref, after_ref, best_ref, out_ref):
-    count = in_ref.shape[0] // SLOT
+            out_ref[pl.ds(ROWS * box + row, count, stride=WIDE), :] = placed[rows, LANES * row : LANES * (row + 1)]
+        out_ref[pl.ds(20 + box, count, stride=WIDE), :] = below[rows]
+        out_ref[pl.ds(22 + box, count, stride=WIDE), :] = above[rows]
+
+    place = lax.broadcasted_iota(jnp.int32, (count, LANES), 0).astype(jnp.float32)
+    marks = jnp.zeros((count, LANES), jnp.float32)
+    for side_num, face_ref in enumerate((after_ref, before_ref)):
+        face = face_ref[...]
+        target = [jnp.broadcast_to(face[20:21, box : box + 1], place.shape) for box in range(2)]
+        slot = [jnp.where(t >= count, 1.0, 0.0) for t in target]
+        here = [place == target[box] - count * slot[box] for box in range(2)]
+        for row in range(ROWS):
+            value = jnp.where(here[0], face[row : row + 1], face[ROWS + row : ROWS + row + 1])
+            out_ref[pl.ds(24 + ROWS * side_num + row, count, stride=WIDE), :] = value
+        mark = jnp.where(here[0], slot[0], jnp.where(here[1], slot[1], -1.0))
+        marks = jnp.where(lane == side_num, mark, marks)
+    for row in range(44, WIDE):
+        out_ref[pl.ds(row, count, stride=WIDE), :] = marks
+
+
+def change_kernel(pick_ref, in_ref, out_ref):
+    count = in_ref.shape[0] // WIDE
 
     def rows_of(row):
-        return in_ref[pl.ds(row, count, stride=SLOT), :]
+        return in_ref[pl.ds(row, count, stride=WIDE), :]
 
     def pick(box, face):
         return pick_ref[0:1, 6 * box + face : 6 * box + face + 1]
@@ -181,21 +205,26 @@
     velocity, _, sound = primitives(cell)
     lane = lane_index(cell[0].shape)
 
-    own = (in_ref[SLOT * (count - 1) : SLOT * count, :], in_ref[0:SLOT, :])
-    other = (before_ref[...], after_ref[...])
+    marks = rows_of(44)
+    own = (in_ref[WIDE * (count - 1) : WIDE * (count - 1) + SLOT, :], in_ref[0:SLOT, :])
     ghosts = []
     for face in range(2):
+        start = 34 - ROWS * face
+        mark = jnp.broadcast_to(marks[:, 1 - face : 2 - face], (count, LANES))
+        strips = [rows_of(start + row) for row in range(ROWS)]
         for box in range(2):
             wanted = pick(box, face)
-            rows = jnp.where(wanted >= 2.0, own[face], other[face])
-            first = (wanted == 0.0) | (wanted == 2.0)
-            ghosts.append(jnp.where(first, rows[0:ROWS], rows[ROWS : 2 * ROWS]))
+            mine = mark == wanted
+            far = [jnp.sum(jnp.where(mine, strip, 0.0), axis=0, keepdims=True) for strip in strips]
+            near = jnp.where(wanted == 2.0, own[face][0:ROWS], own[face][ROWS : 2 * ROWS])
+            inside = wanted >= 2.0
+            ghosts.append([jnp.where(inside, near[row : row + 1], far[row]) for row in range(ROWS)])
     layer = lax.broadcasted_iota(jnp.int32, cell[0].shape, 1)
     below, above = [], []
     for v in range(5):
 
         def spread(rows):
-            return jnp.stack([rows[box][2 * v + half : 2 * v + half + 1] for box in range(2) for half in range(2)])
+            return jnp.stack([rows[box][2 * v + half] for box in range(2) for half in range(2)])
 
         below.append(jnp.where(layer == 0, spread(ghosts[0:2]), pltpu.roll(cell[v], 1, 1)))
         above.append(jnp.where(layer == count - 1, spread(ghosts[2:4]), pltpu.roll(cell[v], count - 1, 1)))
@@ -228,23 +257,35 @@
         above.append(jnp.where(deep == 15, edge, pltpu.roll(cell[v], LANES - 1, 2)))
     more = axis_change(cell, jnp.abs(velocity[2]) + sound, below, above, 2)
 
+    for v in range(5):
+        out_ref[v] = change[v] + more[v]
+
+
+def finish_kernel(in_ref, change_ref, best_ref, out_ref):
+    count = in_ref.shape[0] // WIDE
     step = courant / jnp.max(best_ref[...], axis=0)
-    for v in range(5):
-        result = cell[v] - step[None] * (change[v] + more[v])
-        for box in range(2):
+    for box in range(2):
+        for v in range(5):
             for half in range(2):
-                out_ref[box, v, :, LANES * half : LANES * (half + 1)] = result[2 * box + half]
+                cell = in_ref[pl.ds(ROWS * box + 2 * v + half, count, stride=WIDE), :]
+                columns = slice(LANES * half, LANES * (half + 1))
+                out_ref[box, v, :, columns] = cell - step * change_ref[v, 2 * box + half]
 
 
 def local(state, new_slot, neighbours):
     count = lax.axis_size("curve")
     segs = lax.axis_size("seg")
     f32 = jnp.float32
-    sent, pick = pl.pallas_call(
+    sent, first, last, pick = pl.pallas_call(
         pack_kernel,
-        out_shape=(jax.ShapeDtypeStruct((SLOT * count, LANES), f32), jax.ShapeDtypeStruct((8, LANES), f32)),
+        out_shape=(
+            jax.ShapeDtypeStruct((SLOT * count, LANES), f32),
+            jax.ShapeDtypeStruct((SLOT, LANES), f32),
+            jax.ShapeDtypeStruct((SLOT, LANES), f32),
+            jax.ShapeDtypeStruct((8, LANES), f32),
+        ),
         in_specs=[hbm, hbm, hbm],
-        out_specs=(vmem, vmem),
+        out_specs=(vmem, vmem, vmem, vmem),
         scratch_shapes=[
             pltpu.SMEM(new_slot.shape, jnp.int32),
             pltpu.SMEM(neighbours.shape, jnp.int32),
@@ -253,32 +294,42 @@
         ],
         name="pack",
     )(new_slot, neighbours, state)
+    up = [(i, (i + 1) % segs) for i in range(segs)]
+    down = [(j, i) for i, j in up]
     met = lax.all_to_all(sent.reshape(count, SLOT, LANES), "curve", 0, 0, tiled=True)
+    before = lax.ppermute(last, "seg", up)
+    after = lax.ppermute(first, "seg", down)
     routed, best = pl.pallas_call(
         route_kernel,
         out_shape=(
-            jax.ShapeDtypeStruct((SLOT * count, LANES), f32),
+            jax.ShapeDtypeStruct((WIDE * count, LANES), f32),
             jax.ShapeDtypeStruct((segs, 1, LANES), f32),
         ),
-        in_specs=[vmem],
+        in_specs=[vmem, vmem, vmem],
         out_specs=(vmem, vmem),
         compiler_params=params,
         name="route",
-    )(met.reshape(SLOT * count, LANES))
-    moved = lax.all_to_all(routed.reshape(count, SLOT, LANES), "curve", 0, 0, tiled=True)
-    up = [(i, (i + 1) % segs) for i in range(segs)]
-    down = [(j, i) for i, j in up]
-    before = lax.ppermute(moved[count - 1], "seg", up)
-    after = lax.ppermute(moved[0], "seg", down)
+    )(met.reshape(SLOT * count, LANES), before, after)
+    moved = lax.all_to_all(routed.reshape(count, WIDE, LANES), "curve", 0, 0, tiled=True)
+    moved, best = lax.optimization_barrier((moved, best))
     best = lax.all_to_all(best, "seg", 0, 0, tiled=True)
-    return pl.pallas_call(
-        advance_kernel,
-        out_shape=jax.ShapeDtypeStruct(state.shape, f32),
-        in_specs=[vmem] * 5,
+    moved = moved.reshape(WIDE * count, LANES)
+    change = pl.pallas_call(
+        change_kernel,
+        out_shape=jax.ShapeDtypeStruct((5, 4, count, LANES), f32),
+        in_specs=[vmem, vmem],
         out_specs=vmem,
         compiler_params=params,
-        name="advance",
-    )(pick, moved.reshape(SLOT * count, LANES), before, after, best)
+        name="change",
+    )(pick, moved)
+    return pl.pallas_call(
+        finish_kernel,
+        out_shape=jax.ShapeDtypeStruct(state.shape, f32),
+        in_specs=[vmem] * 3,
+        out_specs=vmem,
+        compiler_params=params,
+        name="finish",
+    )(moved, change, best)
 
 
 def solution(mesh):

time: 73.5 us -> 77.7 us (1.057)
  blocking collectives: 40.8 us -> 22.4 us
  starting transfers between devices: 22.4 us -> 39.5 us
  waiting for transfers between devices: 5.83 us -> 11.1 us
    all_to_all x2 -> x1, blocking collectives: 40.8 us -> 22.4 us  [local(): lax.all_to_all(routed.reshape(count, WIDE, LANES), 'curve', 0, 0, tiled=T...]
    all_to_all x0 -> x1, starting transfers between devices: none -> 17.5 us  [local(): lax.all_to_all(sent.reshape(count, SLOT, LANES), 'curve', 0, 0, tiled=True)]
    all_to_all x1, waiting for transfers between devices: 2.26 us -> 10.3 us  [local(): best = lax.all_to_all(best, 'seg', 0, 0, tiled=True)]
    all_to_all x1, starting transfers between devices: 13.9 us -> 9.15 us  [local(): best = lax.all_to_all(best, 'seg', 0, 0, tiled=True)]
    ppermute x2, starting transfers between devices: 8.47 us -> 12.9 us  [the longest x1 11 us: local(): after = lax.ppermute(first, 'seg', down)]
    ppermute x2, waiting for transfers between devices: 3.57 us -> 0.8 us  [the longest x1 0.8 us: local(): after = lax.ppermute(first, 'seg', down)]
    pallas_call x2 -> x3, Pallas kernels: 2.18 us -> 2.36 us  [the longest x1 0.92 us: local(): pl.pallas_call(route_kernel, out_shape=(jax.ShapeDtypeStruct((WIDE * coun...]
  transfers between devices with their start and end apart: 3 -> 4, of which waited for: 2 -> 2; matrix products, arithmetic and copies ran while one was open for 0% -> 0% of each run, Pallas kernels for 0% -> 1%
where the time goes in v8:
time: 77.7 us; the launch traced here: 77.3 us
  starting transfers between devices  39.5 us (51%)
  blocking collectives  22.4 us (29%)
  waiting for transfers between devices  11.1 us (14%)
  Pallas kernels  4.2 us (5%)
    all_to_all x1, blocking collectives, local(): lax.all_to_all(routed.reshape(count, WIDE, LANES), 'curve', 0, 0, tiled=T...  22.4 us
    all_to_all x1, starting transfers between devices, local(): lax.all_to_all(sent.reshape(count, SLOT, LANES), 'curve', 0, 0, tiled=True)  17.5 us
    ppermute x1, starting transfers between devices, local(): after = lax.ppermute(first, 'seg', down)  11 us
    all_to_all x1, waiting for transfers between devices, local(): best = lax.all_to_all(best, 'seg', 0, 0, tiled=True)  10.3 us
    all_to_all x1, starting transfers between devices, local(): best = lax.all_to_all(best, 'seg', 0, 0, tiled=True)  9.15 us
    ppermute x1, starting transfers between devices, local(): before = lax.ppermute(last, 'seg', up)  1.92 us
    pallas_call x1, Pallas kernels, local(): pl.pallas_call(pack_kernel, out_shape=(jax.ShapeDtypeStruct((SLOT * count...  1.84 us
  transfers between devices with their start and end apart: 4, of which 2 were waited for; matrix products, arithmetic and copies ran while one was open for 0% of the time, Pallas kernels for 1%

profile of v8, /device:TPU:1, one launch (start us, length us, event | category | flops | bytes accessed | tf_op | source)
XLA Modules:
  0.0 77.3 jit_solution(10272129500731126279)
XLA Ops:
  0.0 1.8 %pack.1 = (f32[384,128]{1,0:T(8,128)}, f32[24,128]{1,0:T(8,128)}, f32[24,128]{1,0:T(8,128)}, f32[8,128]{1,0:T(8,128)}) custom-call(s32[2]{0:T(128)} %slot_hbm.1, s32[2,6]{1,0:T(2,128)} %near_hbm.1, f32[2,5,16,256]{3,2,1,0:T(8,128)} %state_hbm.1), custom_call_target="tpu_custom_call" | custom-call | tf_op jit(solution)/shard_map/pack/pallas_call | solution.py:279
  1.8 0.0 copy-start.2
  1.9 0.0 copy-start.1
  1.9 17.5 %all-to-all-start = ((f32[16,24,128]{2,1,0:T(8,128)}), f32[16,24,128]{2,1,0:T(8,128)S(1)}, u32[]{:S(2)}, u32[]{:S(2)}) async-start(f32[16,24,128]{2,1,0:T(8,128)} %bitcast.8), calls=%async_computation | async-start | bytes 393216 | tf_op jit(solution)/shard_map/all_to_all | solution.py:299
  19.3 0.0 copy-done.2
  19.4 1.9 %collective-permute-start = (f32[24,128]{1,0:T(8,128)S(1)}, f32[24,128]{1,0:T(8,128)S(1)}, u32[]{:S(2)}, u32[]{:S(2)}) collective-permute-start(f32[24,128]{1,0:T(8,128)S(1)} %copy-done.2), channel_id=1, source_target_pairs={{0,16},{16,32},{32,48},{48,64},{64,80},{80,96},{96,112},{112,128},... | collective-permute-start | bytes 36872 | tf_op jit(solution)/shard_map/ppermute | solution.py:300
  21.3 0.0 copy-done.1
  21.3 11.0 %collective-permute-start.1 = (f32[24,128]{1,0:T(8,128)S(1)}, f32[24,128]{1,0:T(8,128)S(1)}, u32[]{:S(2)}, u32[]{:S(2)}) collective-permute-start(f32[24,128]{1,0:T(8,128)S(1)} %copy-done.1), channel_id=1, source_target_pairs={{16,0},{32,16},{48,32},{64,48},{80,64},{96,80},{112,96},{128,112},... | collective-permute-start | bytes 36872 | tf_op jit(solution)/shard_map/ppermute | solution.py:301
  32.3 0.0 collective-permute-done.before_ref
  32.3 0.8 %collective-permute-done.1.after_ref = f32[24,128]{1,0:T(8,128)S(1)} collective-permute-done((f32[24,128]{1,0:T(8,128)S(1)}, f32[24,128]{1,0:T(8,128)S(1)}, u32[]{:S(2)}, u32[]{:S(2)}) %collective-permute-start.1) | collective-permute-done | bytes 12320 | tf_op jit(solution)/shard_map/ppermute | solution.py:301
  33.1 0.0 all-to-all-done
  33.1 0.9 %route.1 = (f32[768,128]{1,0:T(8,128)S(1)}, f32[64,1,128]{2,1,0:T(1,128)}) custom-call(f32[384,128]{1,0:T(8,128)S(1)} %bitcast.6, f32[24,128]{1,0:T(8,128)S(1)} %collective-permute-done.before_ref, f32[24,128]{1,0:T(8,128)S(1)} %collective-permute-done.1.after_ref), custom_call_target="tpu_custom_call" | custom-call | tf_op jit(solution)/shard_map/route/pallas_call | solution.py:302
  34.0 22.4 %all_to_all.15 = f32[16,48,128]{2,1,0:T(8,128)S(1)} all-to-all(f32[16,48,128]{2,1,0:T(8,128)S(1)} %bitcast.7), channel_id=1, replica_groups=mesh['seg'=64,'curve'=16] {'curve'}, dimensions={0} | all-to-all | bytes 786432 | tf_op jit(solution)/shard_map/all_to_all | solution.py:313
  56.4 0.0 copy-start
  56.4 9.1 %all-to-all-start.2 = ((f32[64,1,128]{2,1,0:T(1,128)}), f32[64,1,128]{2,1,0:T(1,128)S(1)}, u32[]{:S(2)}, u32[]{:S(2)}) async-start(f32[64,1,128]{2,1,0:T(1,128)} %get-tuple-element.20), calls=%async_computation.2 | async-start | bytes 65536 | tf_op jit(solution)/shard_map/all_to_all | solution.py:315
  65.6 0.0 copy-done
  65.6 0.7 change.1.change_ref
  66.3 10.3 %all-to-all-done.2.best_ref = f32[64,1,128]{2,1,0:T(1,128)S(1)} async-done(((f32[64,1,128]{2,1,0:T(1,128)}), f32[64,1,128]{2,1,0:T(1,128)S(1)}, u32[]{:S(2)}, u32[]{:S(2)}) %all-to-all-start.2) | async-done | bytes 32800 | tf_op jit(solution)/shard_map/all_to_all | solution.py:315
  76.5 0.8 finish.1
Async XLA Ops:
  1.8 17.5 %copy-start.2 = (f32[24,128]{1,0:T(8,128)S(1)}, f32[24,128]{1,0:T(8,128)}, u32[]{:S(2)}) copy-start(f32[24,128]{1,0:T(8,128)} %get-tuple-element.14) | copy-start | bytes 36868
  1.9 19.4 %copy-start.1 = (f32[24,128]{1,0:T(8,128)S(1)}, f32[24,128]{1,0:T(8,128)}, u32[]{:S(2)}) copy-start(f32[24,128]{1,0:T(8,128)} %get-tuple-element.15) | copy-start | bytes 36868
  1.9 31.2 %all-to-all-start = ((f32[16,24,128]{2,1,0:T(8,128)}), f32[16,24,128]{2,1,0:T(8,128)S(1)}, u32[]{:S(2)}, u32[]{:S(2)}) async-start(f32[16,24,128]{2,1,0:T(8,128)} %bitcast.8), calls=%async_computation | async-start | bytes 393216 | tf_op jit(solution)/shard_map/all_to_all | solution.py:299
  19.4 12.9 %collective-permute-start = (f32[24,128]{1,0:T(8,128)S(1)}, f32[24,128]{1,0:T(8,128)S(1)}, u32[]{:S(2)}, u32[]{:S(2)}) collective-permute-start(f32[24,128]{1,0:T(8,128)S(1)} %copy-done.2), channel_id=1, source_target_pairs={{0,16},{16,32},{32,48},{48,64},{64,80},{80,96},{96,112},{112,128},... | collective-permute-start | bytes 36872 | tf_op jit(solution)/shard_map/ppermute | solution.py:300
  21.3 11.8 %collective-permute-start.1 = (f32[24,128]{1,0:T(8,128)S(1)}, f32[24,128]{1,0:T(8,128)S(1)}, u32[]{:S(2)}, u32[]{:S(2)}) collective-permute-start(f32[24,128]{1,0:T(8,128)S(1)} %copy-done.1), channel_id=1, source_target_pairs={{16,0},{32,16},{48,32},{64,48},{80,64},{96,80},{112,96},{128,112},... | collective-permute-start | bytes 36872 | tf_op jit(solution)/shard_map/ppermute | solution.py:301
  56.4 9.2 %copy-start = (f32[8,128]{1,0:T(8,128)S(1)}, f32[8,128]{1,0:T(8,128)}, u32[]{:S(2)}) copy-start(f32[8,128]{1,0:T(8,128)} %get-tuple-element.19.pick_ref) | copy-start | bytes 12292
  56.4 20.1 %all-to-all-start.2 = ((f32[64,1,128]{2,1,0:T(1,128)}), f32[64,1,128]{2,1,0:T(1,128)S(1)}, u32[]{:S(2)}, u32[]{:S(2)}) async-start(f32[64,1,128]{2,1,0:T(1,128)} %get-tuple-element.20), calls=%async_computation.2 | async-start | bytes 65536 | tf_op jit(solution)/shard_map/all_to_all | solution.py:315

commit v9 on v6

--- a/solution.py
+++ b/solution.py
@@ -1,17 +1,19 @@
+import math
+
 import jax
 import jax.numpy as jnp
 from jax import lax
 from jax.experimental import pallas as pl
 from jax.experimental.pallas import tpu as pltpu
-from jax.sharding import PartitionSpec as P
+from jax.sharding import Mesh, PartitionSpec as P
 
 gamma_ratio = 1.4
 courant = 0.3
 
 LANES = 128
+SEG = ("seg_x", "seg_z")
 ROWS = 10
 SLOT = 24
-TOP = 96
 
 vmem = pl.BlockSpec(memory_space=pltpu.VMEM)
 hbm = pl.BlockSpec(memory_space=pltpu.HBM)
@@ -101,7 +103,7 @@
     for row in range(21, SLOT):
         out_ref[pl.ds(row, count, stride=SLOT), :] = jnp.zeros((count, LANES), jnp.float32)
 
-    segment = lax.axis_index("seg")
+    segment = lax.axis_index(SEG)
     lane = lane_index(pick_ref.shape)
     picks = jnp.zeros(pick_ref.shape, jnp.float32)
     for box in range(2):
@@ -114,13 +116,6 @@
     pick_ref[...] = picks
 
 
-def peak_kernel(in_ref, out_ref):
-    count = in_ref.shape[0] // SLOT
-    header = in_ref[pl.ds(20, count, stride=SLOT), :]
-    best = jnp.max(jnp.where(lane_index(header.shape) == 6, header, 0.0), axis=0, keepdims=True)
-    out_ref[...] = jnp.broadcast_to(jnp.max(best, axis=1, keepdims=True), out_ref.shape)
-
-
 def three_parts(value):
     high = value.astype(jnp.bfloat16)
     rest = value - high.astype(jnp.float32)
@@ -134,10 +129,13 @@
     return jnp.dot(jnp.concatenate([chosen] * 3, axis=1), parts, preferred_element_type=jnp.float32)
 
 
-def route_kernel(in_ref, speed_ref, out_ref):
+def route_kernel(in_ref, out_ref, best_ref):
     count = in_ref.shape[0] // SLOT
     boxes = 2 * count
     header = in_ref[pl.ds(20, count, stride=SLOT), :]
+    best = jnp.max(jnp.where(lane_index(header.shape) == 6, header, 0.0), axis=0, keepdims=True)
+    best = jnp.max(best, axis=1, keepdims=True)
+    best_ref[...] = jnp.broadcast_to(best, best_ref.shape)
     both = jnp.concatenate([header, pltpu.roll(header, LANES - 1, 1)], axis=0)
     target = jnp.broadcast_to(jnp.transpose(both)[0:1, :], (boxes, boxes))
     index = lax.broadcasted_iota(jnp.int32, (boxes, boxes), 0).astype(jnp.float32)
@@ -163,7 +161,6 @@
     placed = gather_rows(index == target, three_parts(jnp.concatenate(columns, axis=1)))
     below = gather_rows(beside(2, 4) == target, three_parts(last))
     above = gather_rows(beside(3, 5) == target, three_parts(first))
-    below = jnp.where(lane2 >= TOP, speed_ref[0:1, :], below)
     for box in range(2):
         rows = slice(count * box, count * (box + 1))
         for row in range(ROWS):
@@ -187,15 +184,42 @@
     return ref[0:1, 6 * box + face : 6 * box + face + 1]
 
 
-def faces_kernel(in_ref, first_ref, last_ref, speed_ref):
-    count = in_ref.shape[0] // SLOT
-    speeds = rows_of(in_ref, 20)
-    best = jnp.max(jnp.where(lane_index(speeds.shape) >= TOP, speeds, 0.0), axis=0, keepdims=True)
-    best = jnp.max(best, axis=1, keepdims=True)
-    row = lax.broadcasted_iota(jnp.int32, first_ref.shape, 0)
-    first_ref[...] = jnp.where(row < 2 * ROWS, in_ref[0:SLOT, :], best)
-    last_ref[...] = jnp.where(row < 2 * ROWS, in_ref[SLOT * (count - 1) : SLOT * count, :], best)
-    speed_ref[...] = jnp.broadcast_to(best, speed_ref.shape)
+def edge_layers(ref):
+    end = ref.shape[0]
+    return ref[0:SLOT, :], ref[end - SLOT : end, :]
+
+
+def with_speed(rows, speed):
+    return jnp.where(lax.broadcasted_iota(jnp.int32, rows.shape, 0) < 2 * ROWS, rows, speed)
+
+
+def slot_of(ref, place, step):
+    count = ref.shape[0] // SLOT
+    index = lax.rem(place + step + count, count)
+    return ref[pl.ds(pl.multiple_of(index * SLOT, SLOT), SLOT), :]
+
+
+def fill_slots(ref, place, to_next, to_previous):
+    count = ref.shape[0] // SLOT
+    following = lax.rem(place + 1, count)
+    for slot in range(count):
+        ref[SLOT * slot : SLOT * (slot + 1), :] = jnp.where(following == slot, to_next, to_previous)
+
+
+def along_x_kernel(in_ref, best_ref, out_ref):
+    first, last = edge_layers(in_ref)
+    best = best_ref[0:1, :]
+    fill_slots(out_ref, lax.axis_index(SEG[0]), with_speed(last, best), with_speed(first, best))
+
+
+def along_z_kernel(in_ref, met_ref, out_ref):
+    first, last = edge_layers(in_ref)
+    best = jnp.max(rows_of(met_ref, 2 * ROWS), axis=0, keepdims=True)
+    place_x, place_z = (lax.axis_index(axis) for axis in SEG)
+    end = out_ref.shape[0] // SLOT - 1
+    last = jnp.where(place_z == end, slot_of(met_ref, place_x, -1), last)
+    first = jnp.where(place_z == 0, slot_of(met_ref, place_x, 1), first)
+    fill_slots(out_ref, place_z, with_speed(last, best), with_speed(first, best))
 
 
 def planes_kernel(pick_ref, in_ref, out_ref):
@@ -233,12 +257,13 @@
         out_ref[v] = change[v] + more[v]
 
 
-def finish_kernel(pick_ref, in_ref, change_ref, before_ref, after_ref, speed_ref, beyond_ref, out_ref):
+def finish_kernel(pick_ref, in_ref, change_ref, met_ref, out_ref):
     count = in_ref.shape[0] // SLOT
     cell = load_cells(in_ref)
     velocity, _, sound = primitives(cell)
     own = (in_ref[SLOT * (count - 1) : SLOT * count, :], in_ref[0:SLOT, :])
-    other = (before_ref[...], after_ref[...])
+    place = lax.axis_index(SEG[1])
+    other = (slot_of(met_ref, place, -1), slot_of(met_ref, place, 1))
     ghosts = []
     for face in range(2):
         for box in range(2):
@@ -257,10 +282,7 @@
         above.append(jnp.where(layer == count - 1, spread(ghosts[2:4]), pltpu.roll(cell[v], count - 1, 1)))
     change = axis_change(cell, jnp.abs(velocity[0]) + sound, below, above, 0)
 
-    row = 2 * ROWS
-    best = jnp.maximum(speed_ref[0:1, :], beyond_ref[0:1, :])
-    best = jnp.maximum(best, jnp.maximum(before_ref[row : row + 1, :], after_ref[row : row + 1, :]))
-    step = courant / best
+    step = courant / jnp.max(rows_of(met_ref, 2 * ROWS), axis=0, keepdims=True)
     for v in range(5):
         result = cell[v] - step[None] * (change[v] + change_ref[v])
         for box in range(2):
@@ -270,8 +292,7 @@
 
 def local(state, new_slot, neighbours):
     count = lax.axis_size("curve")
-    segs = lax.axis_size("seg")
-    assert segs % 4 == 0 and segs <= 4 * count
+    along_x, along_z = (lax.axis_size(axis) for axis in SEG)
     f32 = jnp.float32
     sent, pick = pl.pallas_call(
         pack_kernel,
@@ -287,46 +308,41 @@
         name="pack",
     )(new_slot, neighbours, state)
     met = lax.all_to_all(sent.reshape(count, SLOT, LANES), "curve", 0, 0, tiled=True)
-    met = met.reshape(SLOT * count, LANES)
-    speed = pl.pallas_call(
-        peak_kernel,
-        out_shape=jax.ShapeDtypeStruct((8, LANES), f32),
-        in_specs=[vmem],
-        out_specs=vmem,
-        compiler_params=params,
-        name="peak",
-    )(met)
-    spread = [((s + 4 * c) % segs * count + c, s * count + c) for s in range(segs) for c in range(count)]
-    speed = lax.ppermute(speed, ("seg", "curve"), spread)
-    routed = pl.pallas_call(
+    routed, best = pl.pallas_call(
         route_kernel,
-        out_shape=jax.ShapeDtypeStruct((SLOT * count, LANES), f32),
-        in_specs=[vmem, vmem],
-        out_specs=vmem,
-        compiler_params=params,
-        name="route",
-    )(met, speed)
-    moved = lax.all_to_all(routed.reshape(count, SLOT, LANES), "curve", 0, 0, tiled=True)
-    moved = moved.reshape(SLOT * count, LANES)
-    first, last, speed = pl.pallas_call(
-        faces_kernel,
         out_shape=(
-            jax.ShapeDtypeStruct((SLOT, LANES), f32),
-            jax.ShapeDtypeStruct((SLOT, LANES), f32),
+            jax.ShapeDtypeStruct((SLOT * count, LANES), f32),
             jax.ShapeDtypeStruct((8, LANES), f32),
         ),
         in_specs=[vmem],
-        out_specs=(vmem, vmem, vmem),
-        compiler_params=params,
-        name="faces",
-    )(moved)
-    before = lax.ppermute(last, "seg", [(i, (i + 1) % segs) for i in range(segs)])
-    after = lax.ppermute(first, "seg", [((i + 1) % segs, i) for i in range(segs)])
-    beyond = lax.ppermute(speed, "seg", [((i + 2) % segs, i) for i in range(segs)])
+        out_specs=(vmem, vmem),
+        compiler_params=params,
+        name="route",
+    )(met.reshape(SLOT * count, LANES))
+    moved = lax.all_to_all(routed.reshape(count, SLOT, LANES), "curve", 0, 0, tiled=True)
+    moved = moved.reshape(SLOT * count, LANES)
+    along = pl.pallas_call(
+        along_x_kernel,
+        out_shape=jax.ShapeDtypeStruct((SLOT * along_x, LANES), f32),
+        in_specs=[vmem] * 2,
+        out_specs=vmem,
+        compiler_params=params,
+        name="along_x",
+    )(moved, best)
+    along = lax.all_to_all(along.reshape(along_x, SLOT, LANES), SEG[0], 0, 0, tiled=True)
+    along = pl.pallas_call(
+        along_z_kernel,
+        out_shape=jax.ShapeDtypeStruct((SLOT * along_z, LANES), f32),
+        in_specs=[vmem] * 2,
+        out_specs=vmem,
+        compiler_params=params,
+        name="along_z",
+    )(moved, along.reshape(SLOT * along_x, LANES))
+    along = lax.all_to_all(along.reshape(along_z, SLOT, LANES), SEG[1], 0, 0, tiled=True)
     change = pl.pallas_call(
         planes_kernel,
         out_shape=jax.ShapeDtypeStruct((5, 4, count, LANES), f32),
-        in_specs=[vmem, vmem],
+        in_specs=[vmem] * 2,
         out_specs=vmem,
         compiler_params=params,
         name="planes",
@@ -334,15 +350,18 @@
     return pl.pallas_call(
         finish_kernel,
         out_shape=jax.ShapeDtypeStruct(state.shape, f32),
-        in_specs=[vmem] * 7,
+        in_specs=[vmem] * 4,
         out_specs=vmem,
         compiler_params=params,
         name="finish",
-    )(pick, moved, change, before, after, speed, beyond)
+    )(pick, moved, change, along.reshape(SLOT * along_z, LANES))
 
 
 def solution(mesh):
-    placed = P(("seg", "curve"))
+    segs, count = mesh.devices.shape
+    side_x = math.isqrt(segs)
+    grid = Mesh(mesh.devices.reshape(side_x, segs // side_x, count), SEG + ("curve",))
+    placed = P(SEG + ("curve",))
     return jax.shard_map(
-        local, mesh=mesh, in_specs=(placed, placed, placed), out_specs=placed, check_vma=False
+        local, mesh=grid, in_specs=(placed, placed, placed), out_specs=placed, check_vma=False
     )

time: 75.4 us -> 75.2 us (level)
  starting transfers between devices: 24.1 us -> 11.2 us
  blocking collectives: 44.7 us -> 52.1 us
  waiting for transfers between devices: 2.39 us -> 7.08 us
    ppermute x4 -> x0, starting transfers between devices: 24.1 us -> none  [the longest x1 10 us: local(): lax.ppermute(first, 'seg', [((i + 1) % segs, i) for i in range(segs)])]
    all_to_all x0 -> x1, blocking collectives: none -> 11.3 us  [local(): lax.all_to_all(along.reshape(along_x, SLOT, LANES), SEG[0], 0, 0, tiled=T...]
    all_to_all x0 -> x1, starting transfers between devices: none -> 11.2 us  [local(): lax.all_to_all(along.reshape(along_z, SLOT, LANES), SEG[1], 0, 0, tiled=T...]
    all_to_all x0 -> x1, waiting for transfers between devices: none -> 7.08 us  [local(): lax.all_to_all(along.reshape(along_z, SLOT, LANES), SEG[1], 0, 0, tiled=T...]
    all_to_all x1, blocking collectives: 16.9 us -> 13 us  [local(): lax.all_to_all(routed.reshape(count, SLOT, LANES), 'curve', 0, 0, tiled=T...]
    ppermute x4 -> x0, waiting for transfers between devices: 2.39 us -> none  [the longest x1 1.65 us: local(): lax.ppermute(speed, 'seg', [((i + 2) % segs, i) for i in range(segs)])]
  transfers between devices with their start and end apart: 4 -> 1, of which waited for: 2 -> 1; matrix products, arithmetic and copies ran while one was open for 0% -> 0% of each run, Pallas kernels for 1% -> 1%
where the time goes in v9:
time: 75.2 us; the launch traced here: 74.7 us
  blocking collectives  52.1 us (69%)
  starting transfers between devices  11.2 us (15%)
  waiting for transfers between devices  7.08 us (9%)
  Pallas kernels  4.27 us (6%)
    all_to_all x1, blocking collectives, local(): lax.all_to_all(sent.reshape(count, SLOT, LANES), 'curve', 0, 0, tiled=True)  27.8 us
    all_to_all x1, blocking collectives, local(): lax.all_to_all(routed.reshape(count, SLOT, LANES), 'curve', 0, 0, tiled=T...  13 us
    all_to_all x1, blocking collectives, local(): lax.all_to_all(along.reshape(along_x, SLOT, LANES), SEG[0], 0, 0, tiled=T...  11.3 us
    all_to_all x1, starting transfers between devices, local(): lax.all_to_all(along.reshape(along_z, SLOT, LANES), SEG[1], 0, 0, tiled=T...  11.2 us
    all_to_all x1, waiting for transfers between devices, local(): lax.all_to_all(along.reshape(along_z, SLOT, LANES), SEG[1], 0, 0, tiled=T...  7.08 us
    pallas_call x1, Pallas kernels, local(): pl.pallas_call(pack_kernel, out_shape=(jax.ShapeDtypeStruct((SLOT * count...  1.83 us
  transfers between devices with their start and end apart: 1, of which 1 were waited for; matrix products, arithmetic and copies ran while one was open for 0% of the time, Pallas kernels for 1%

profile of v9, /device:TPU:1, one launch (start us, length us, event | category | flops | bytes accessed | tf_op | source)
XLA Modules:
  0.0 74.7 jit_solution(5640601359994140634)
XLA Ops:
  0.0 1.8 %pack.1 = (f32[384,128]{1,0:T(8,128)}, f32[8,128]{1,0:T(8,128)}) custom-call(s32[2]{0:T(128)} %slot_hbm.1, s32[2,6]{1,0:T(2,128)} %near_hbm.1, f32[2,5,16,256]{3,2,1,0:T(8,128)} %state_hbm.1), custom_call_target="tpu_custom_call" | custom-call | tf_op jit(solution)/shard_map/pack/pallas_call | solution.py:297
  1.8 27.8 %all_to_all.20 = f32[16,24,128]{2,1,0:T(8,128)S(1)} all-to-all(f32[16,24,128]{2,1,0:T(8,128)} %bitcast.17), channel_id=1, replica_groups=mesh['seg_x'=8,'seg_z'=8,'curve'=16] {'curve'}, dimensions={0} | all-to-all | bytes 393216 | tf_op jit(solution)/shard_map/all_to_all | solution.py:310
  29.7 0.4 route.1
  30.0 13.0 %all_to_all.21 = f32[16,24,128]{2,1,0:T(8,128)S(1)} all-to-all(f32[16,24,128]{2,1,0:T(8,128)S(1)} %bitcast.16), channel_id=1, replica_groups=mesh['seg_x'=8,'seg_z'=8,'curve'=16] {'curve'}, dimensions={0} | all-to-all | bytes 393216 | tf_op jit(solution)/shard_map/all_to_all | solution.py:322
  43.0 11.3 %all_to_all.22 = f32[8,24,128]{2,1,0:T(8,128)S(1)} all-to-all(f32[8,24,128]{2,1,0:T(8,128)S(1)} %bitcast.14), channel_id=1, replica_groups=mesh['seg_x'=8,'seg_z'=8,'curve'=16] {'seg_x'}, dimensions={0} | all-to-all | bytes 196608 | tf_op jit(solution)/shard_map/all_to_all | solution.py:332
  54.3 0.7 along_z.1
  55.0 0.0 copy-start
  55.0 11.2 %all-to-all-start.3 = ((f32[8,24,128]{2,1,0:T(8,128)}), f32[8,24,128]{2,1,0:T(8,128)S(1)}, u32[]{:S(2)}, u32[]{:S(2)}) async-start(f32[8,24,128]{2,1,0:T(8,128)} %bitcast.6), calls=%async_computation.3 | async-start | bytes 196608 | tf_op jit(solution)/shard_map/all_to_all | solution.py:341
  66.2 0.0 copy-done
  66.2 0.5 planes.1.change_ref
  66.7 7.1 %all-to-all-done.3 = f32[8,24,128]{2,1,0:T(8,128)S(1)} async-done(((f32[8,24,128]{2,1,0:T(8,128)}), f32[8,24,128]{2,1,0:T(8,128)S(1)}, u32[]{:S(2)}, u32[]{:S(2)}) %all-to-all-start.3) | async-done | bytes 98336 | tf_op jit(solution)/shard_map/all_to_all | solution.py:341
  73.8 0.9 %finish.1 = f32[2,5,16,256]{3,2,1,0:T(8,128)} custom-call(f32[8,128]{1,0:T(8,128)S(1)} %copy-done, f32[384,128]{1,0:T(8,128)S(1)} %bitcast.11, f32[5,4,16,128]{3,2,1,0:T(8,128)S(1)} %planes.1.change_ref, f32[192,128]{1,0:T(8,128)S(1)} %bitcast.13), custom_call_target="tpu_custom_call" | custom-call | tf_op jit(solution)/shard_map/finish/pallas_call | solution.py:350
  (1 shorter events, 0.0 us)
Async XLA Ops:
  55.0 11.2 %copy-start = (f32[8,128]{1,0:T(8,128)S(1)}, f32[8,128]{1,0:T(8,128)}, u32[]{:S(2)}) copy-start(f32[8,128]{1,0:T(8,128)} %get-tuple-element.9.pick_ref) | copy-start | bytes 12292
  55.0 18.8 %all-to-all-start.3 = ((f32[8,24,128]{2,1,0:T(8,128)}), f32[8,24,128]{2,1,0:T(8,128)S(1)}, u32[]{:S(2)}, u32[]{:S(2)}) async-start(f32[8,24,128]{2,1,0:T(8,128)} %bitcast.6), calls=%async_computation.3 | async-start | bytes 196608 | tf_op jit(solution)/shard_map/all_to_all | solution.py:341

commit v10 on v5

--- a/solution.py
+++ b/solution.py
@@ -167,11 +167,6 @@
             out_ref[pl.ds(ROWS * box + row, count, stride=SLOT), :] = placed[rows, LANES * row : LANES * (row + 1)]
         out_ref[pl.ds(20 + box, count, stride=SLOT), :] = below[rows]
         out_ref[pl.ds(22 + box, count, stride=SLOT), :] = above[rows]
-
-
-def peak_kernel(in_ref, out_ref):
-    best = jnp.max(in_ref[...], axis=0, keepdims=True)
-    out_ref[...] = jnp.broadcast_to(best, out_ref.shape)
 
 
 def change_kernel(pick_ref, in_ref, before_ref, after_ref, out_ref):
@@ -287,15 +282,7 @@
     best = lax.all_to_all(best, SEG[1], 0, 0, tiled=True)
     before = lax.ppermute(moved[count - 1], SEG, up)
     after = lax.ppermute(moved[0], SEG, down)
-    best = pl.pallas_call(
-        peak_kernel,
-        out_shape=jax.ShapeDtypeStruct((along_x, 1, LANES), f32),
-        in_specs=[vmem],
-        out_specs=vmem,
-        compiler_params=params,
-        name="peak",
-    )(best)
-    best = lax.all_to_all(best, SEG[0], 0, 0, tiled=True)
+    best = lax.all_gather(best, SEG[0], axis=0, tiled=True)
     moved = moved.reshape(SLOT * count, LANES)
     change = pl.pallas_call(
         change_kernel,

time: 73 us -> 85 us (1.16)
  the two profiles are of different devices: /device:TPU:1 before, /device:TPU:4 now
where the time goes in v10:
time: 85 us; the launch traced here: 84.6 us
  blocking collectives  56.2 us (66%)
  starting transfers between devices  23.7 us (28%)
  Pallas kernels  4 us (5%)
    all_gather x1, blocking collectives, local(): best = lax.all_gather(best, SEG[0], axis=0, tiled=True)  25.6 us
    all_to_all x1, blocking collectives, local(): lax.all_to_all(sent.reshape(count, SLOT, LANES), 'curve', 0, 0, tiled=True)  17.6 us
    all_to_all x1, starting transfers between devices, local(): best = lax.all_to_all(best, SEG[1], 0, 0, tiled=True)  16.7 us
    all_to_all x1, blocking collectives, local(): lax.all_to_all(routed.reshape(count, SLOT, LANES), 'curve', 0, 0, tiled=T...  13 us
    ppermute x1, starting transfers between devices, local(): after = lax.ppermute(moved[0], SEG, down)  5.1 us
    ppermute x1, starting transfers between devices, local(): before = lax.ppermute(moved[count - 1], SEG, up)  1.92 us
    pallas_call x1, Pallas kernels, local(): pl.pallas_call(pack_kernel, out_shape=(jax.ShapeDtypeStruct((SLOT * count...  1.83 us
  transfers between devices with their start and end apart: 3, of which 1 were waited for; matrix products, arithmetic and copies ran while one was open for 0% of the time, Pallas kernels for 0%

profile of v10, /device:TPU:4, one launch (start us, length us, event | category | flops | bytes accessed | tf_op | source)
XLA Modules:
  0.0 84.6 jit_solution(9112930496623115417)
XLA Ops:
  0.0 1.8 %pack.1 = (f32[384,128]{1,0:T(8,128)}, f32[8,128]{1,0:T(8,128)}) custom-call(s32[2]{0:T(128)} %slot_hbm.1, s32[2,6]{1,0:T(2,128)} %near_hbm.1, f32[2,5,16,256]{3,2,1,0:T(8,128)} %state_hbm.1), custom_call_target="tpu_custom_call" | custom-call | tf_op jit(solution)/shard_map/pack/pallas_call | solution.py:254
  1.8 17.6 %all_to_all.15 = f32[16,24,128]{2,1,0:T(8,128)S(1)} all-to-all(f32[16,24,128]{2,1,0:T(8,128)} %bitcast.12), channel_id=1, replica_groups=mesh['seg_x'=8,'seg_z'=8,'curve'=16] {'curve'}, dimensions={0} | all-to-all | bytes 393216 | tf_op jit(solution)/shard_map/all_to_all | solution.py:267
  19.5 0.8 %route.1 = (f32[384,128]{1,0:T(8,128)S(1)}, f32[8,1,128]{2,1,0:T(1,128)}) custom-call(f32[384,128]{1,0:T(8,128)S(1)} %bitcast.10), custom_call_target="tpu_custom_call" | custom-call | tf_op jit(solution)/shard_map/route/pallas_call | solution.py:268
  20.3 13.0 %all_to_all.16 = f32[16,24,128]{2,1,0:T(8,128)S(1)} all-to-all(f32[16,24,128]{2,1,0:T(8,128)S(1)} %bitcast.11), channel_id=1, replica_groups=mesh['seg_x'=8,'seg_z'=8,'curve'=16] {'curve'}, dimensions={0} | all-to-all | bytes 393216 | tf_op jit(solution)/shard_map/all_to_all | solution.py:279
  33.3 16.7 %all-to-all-start.2 = ((f32[8,1,128]{2,1,0:T(1,128)}), f32[8,1,128]{2,1,0:T(1,128)S(1)}, u32[]{:S(2)}, u32[]{:S(2)}) async-start(f32[8,1,128]{2,1,0:T(1,128)} %get-tuple-element.12), calls=%async_computation.2 | async-start | bytes 8192 | tf_op jit(solution)/shard_map/all_to_all | solution.py:282
  50.0 5.1 %collective-permute-start.1 = (f32[24,128]{1,0:T(8,128)S(1)}, f32[24,128]{1,0:T(8,128)S(1)}, u32[]{:S(2)}, u32[]{:S(2)}) collective-permute-start(f32[24,128]{1,0:T(8,128)S(1)} %get-tuple-element.13), channel_id=1, source_target_pairs={{16,0},{32,16},{48,32},{64,48},{80,64},{96,80},{112,96},{128,112},... | collective-permute-start | bytes 36872 | tf_op jit(solution)/shard_map/ppermute | solution.py:284
  55.1 1.9 %collective-permute-start = (f32[24,128]{1,0:T(8,128)S(1)}, f32[24,128]{1,0:T(8,128)S(1)}, u32[]{:S(2)}, u32[]{:S(2)}) collective-permute-start(f32[24,128]{1,0:T(8,128)S(1)} %get-tuple-element.14), channel_id=1, source_target_pairs={{0,16},{16,32},{32,48},{48,64},{64,80},{80,96},{96,112},{112,128},... | collective-permute-start | bytes 36872 | tf_op jit(solution)/shard_map/ppermute | solution.py:283
  57.0 0.6 all-to-all-done.2
  57.7 0.0 copy-start
  57.7 25.6 %all_gather.3.best_ref = f32[64,1,128]{2,1,0:T(1,128)S(1)} all-gather(f32[8,1,128]{2,1,0:T(1,128)S(1)} %all-to-all-done.2), channel_id=1, replica_groups=mesh['seg_x'=8,'seg_z'=8,'curve'=16] {'seg_x'}, dimensions={0}, use_global_device_ids=true | all-gather | bytes 36864 | tf_op jit(solution)/shard_map/all_gather | solution.py:285
  83.2 0.0 collective-permute-done.1.after_ref
  83.2 0.0 collective-permute-done.before_ref
  83.2 0.0 copy-done
  83.2 0.6 change.1.change_ref
  83.8 0.7 finish.1
  (1 shorter events, 0.0 us)
Async XLA Ops:
  33.3 24.4 %all-to-all-start.2 = ((f32[8,1,128]{2,1,0:T(1,128)}), f32[8,1,128]{2,1,0:T(1,128)S(1)}, u32[]{:S(2)}, u32[]{:S(2)}) async-start(f32[8,1,128]{2,1,0:T(1,128)} %get-tuple-element.12), calls=%async_computation.2 | async-start | bytes 8192 | tf_op jit(solution)/shard_map/all_to_all | solution.py:282
  50.0 33.2 %collective-permute-start.1 = (f32[24,128]{1,0:T(8,128)S(1)}, f32[24,128]{1,0:T(8,128)S(1)}, u32[]{:S(2)}, u32[]{:S(2)}) collective-permute-start(f32[24,128]{1,0:T(8,128)S(1)} %get-tuple-element.13), channel_id=1, source_target_pairs={{16,0},{32,16},{48,32},{64,48},{80,64},{96,80},{112,96},{128,112},... | collective-permute-start | bytes 36872 | tf_op jit(solution)/shard_map/ppermute | solution.py:284
  55.1 28.1 %collective-permute-start = (f32[24,128]{1,0:T(8,128)S(1)}, f32[24,128]{1,0:T(8,128)S(1)}, u32[]{:S(2)}, u32[]{:S(2)}) collective-permute-start(f32[24,128]{1,0:T(8,128)S(1)} %get-tuple-element.14), channel_id=1, source_target_pairs={{0,16},{16,32},{32,48},{48,64},{64,80},{80,96},{96,112},{112,128},... | collective-permute-start | bytes 36872 | tf_op jit(solution)/shard_map/ppermute | solution.py:283
  57.7 25.6 %copy-start = (f32[8,128]{1,0:T(8,128)S(1)}, f32[8,128]{1,0:T(8,128)}, u32[]{:S(2)}) copy-start(f32[8,128]{1,0:T(8,128)} %get-tuple-element.11.pick_ref) | copy-start | bytes 12292

commit v11 on v5

--- a/solution.py
+++ b/solution.py
@@ -129,13 +129,15 @@
     return jnp.dot(jnp.concatenate([chosen] * 3, axis=1), parts, preferred_element_type=jnp.float32)
 
 
-def route_kernel(in_ref, out_ref, best_ref):
+def route_kernel(in_ref, out_ref, best_hbm, best_ref, sem):
     count = in_ref.shape[0] // SLOT
     boxes = 2 * count
     header = in_ref[pl.ds(20, count, stride=SLOT), :]
     best = jnp.max(jnp.where(lane_index(header.shape) == 6, header, 0.0), axis=0, keepdims=True)
     best = jnp.max(best, axis=1, keepdims=True)
     best_ref[...] = jnp.broadcast_to(best.reshape(1, 1, 1), best_ref.shape)
+    copy = pltpu.make_async_copy(best_ref, best_hbm, sem)
+    copy.start()
     both = jnp.concatenate([header, pltpu.roll(header, LANES - 1, 1)], axis=0)
     target = jnp.broadcast_to(jnp.transpose(both)[0:1, :], (boxes, boxes))
     index = lax.broadcasted_iota(jnp.int32, (boxes, boxes), 0).astype(jnp.float32)
@@ -167,6 +169,7 @@
             out_ref[pl.ds(ROWS * box + row, count, stride=SLOT), :] = placed[rows, LANES * row : LANES * (row + 1)]
         out_ref[pl.ds(20 + box, count, stride=SLOT), :] = below[rows]
         out_ref[pl.ds(22 + box, count, stride=SLOT), :] = above[rows]
+    copy.wait()
 
 
 def peak_kernel(in_ref, out_ref):
@@ -240,7 +243,7 @@
         out_ref[v] = change[v] + more[v]
 
 
-def finish_kernel(in_ref, change_ref, best_ref, out_ref):
+def finish_kernel(in_ref, change_ref, best_ref, out_hbm, out_ref, sems):
     count = in_ref.shape[0] // SLOT
     step = courant / jnp.max(best_ref[...], axis=0)
     for box in range(2):
@@ -249,6 +252,9 @@
                 cell = in_ref[pl.ds(ROWS * box + 2 * v + half, count, stride=SLOT), :]
                 columns = slice(LANES * half, LANES * (half + 1))
                 out_ref[box, v, :, columns] = cell - step * change_ref[v, 2 * box + half]
+        pltpu.make_async_copy(out_ref.at[box], out_hbm.at[box], sems.at[box]).start()
+    for box in range(2):
+        pltpu.make_async_copy(out_ref.at[box], out_hbm.at[box], sems.at[box]).wait()
 
 
 def local(state, new_slot, neighbours):
@@ -277,7 +283,8 @@
             jax.ShapeDtypeStruct((along_z, 1, LANES), f32),
         ),
         in_specs=[vmem],
-        out_specs=(vmem, vmem),
+        out_specs=(vmem, hbm),
+        scratch_shapes=[pltpu.VMEM((along_z, 1, LANES), f32), pltpu.SemaphoreType.DMA],
         compiler_params=params,
         name="route",
     )(met.reshape(SLOT * count, LANES))
@@ -309,7 +316,8 @@
         finish_kernel,
         out_shape=jax.ShapeDtypeStruct(state.shape, f32),
         in_specs=[vmem] * 3,
-        out_specs=vmem,
+        out_specs=hbm,
+        scratch_shapes=[pltpu.VMEM(state.shape, f32), pltpu.SemaphoreType.DMA((2,))],
         compiler_params=params,
         name="finish",
     )(moved, change, best)

time: 73 us -> 73.1 us (level)
  no operation moved by 1% of the time
where the time goes in v11:
time: 73.1 us; the launch traced here: 72.5 us
  blocking collectives  40.8 us (56%)
  starting transfers between devices  21.1 us (29%)
  waiting for transfers between devices  5.92 us (8%)
  Pallas kernels  4.58 us (6%)
    all_to_all x1, blocking collectives, local(): lax.all_to_all(sent.reshape(count, SLOT, LANES), 'curve', 0, 0, tiled=True)  27.8 us
    all_to_all x1, blocking collectives, local(): lax.all_to_all(routed.reshape(count, SLOT, LANES), 'curve', 0, 0, tiled=T...  13 us
    all_to_all x1, starting transfers between devices, local(): best = lax.all_to_all(best, SEG[1], 0, 0, tiled=True)  7.99 us
    ppermute x1, starting transfers between devices, local(): after = lax.ppermute(moved[0], SEG, down)  6.88 us
    all_to_all x1, waiting for transfers between devices, local(): best = lax.all_to_all(best, SEG[0], 0, 0, tiled=True)  5.01 us
    all_to_all x1, starting transfers between devices, local(): best = lax.all_to_all(best, SEG[0], 0, 0, tiled=True)  4.31 us
    ppermute x1, starting transfers between devices, local(): before = lax.ppermute(moved[count - 1], SEG, up)  1.92 us
    pallas_call x1, Pallas kernels, local(): pl.pallas_call(pack_kernel, out_shape=(jax.ShapeDtypeStruct((SLOT * count...  1.83 us
  transfers between devices with their start and end apart: 4, of which 2 were waited for; matrix products, arithmetic and copies ran while one was open for 0% of the time, Pallas kernels for 2%

profile of v11, /device:TPU:1, one launch (start us, length us, event | category | flops | bytes accessed | tf_op | source)
XLA Modules:
  0.0 72.5 jit_solution(4977752330738924552)
XLA Ops:
  0.0 1.8 %pack.1 = (f32[384,128]{1,0:T(8,128)}, f32[8,128]{1,0:T(8,128)}) custom-call(s32[2]{0:T(128)} %slot_hbm.1, s32[2,6]{1,0:T(2,128)} %near_hbm.1, f32[2,5,16,256]{3,2,1,0:T(8,128)} %state_hbm.1), custom_call_target="tpu_custom_call" | custom-call | tf_op jit(solution)/shard_map/pack/pallas_call | solution.py:265
  1.8 27.8 %all_to_all.20 = f32[16,24,128]{2,1,0:T(8,128)S(1)} all-to-all(f32[16,24,128]{2,1,0:T(8,128)} %bitcast.12), channel_id=1, replica_groups=mesh['seg_x'=8,'seg_z'=8,'curve'=16] {'curve'}, dimensions={0} | all-to-all | bytes 393216 | tf_op jit(solution)/shard_map/all_to_all | solution.py:278
  29.7 0.9 %route.1 = (f32[384,128]{1,0:T(8,128)S(1)}, f32[8,1,128]{2,1,0:T(1,128)}) custom-call(f32[384,128]{1,0:T(8,128)S(1)} %bitcast.10), custom_call_target="tpu_custom_call" | custom-call | tf_op jit(solution)/shard_map/route/pallas_call | solution.py:279
  30.5 13.0 %all_to_all.21 = f32[16,24,128]{2,1,0:T(8,128)S(1)} all-to-all(f32[16,24,128]{2,1,0:T(8,128)S(1)} %bitcast.11), channel_id=1, replica_groups=mesh['seg_x'=8,'seg_z'=8,'curve'=16] {'curve'}, dimensions={0} | all-to-all | bytes 393216 | tf_op jit(solution)/shard_map/all_to_all | solution.py:291
  43.5 8.0 %all-to-all-start.2 = ((f32[8,1,128]{2,1,0:T(1,128)}), f32[8,1,128]{2,1,0:T(1,128)S(1)}, u32[]{:S(2)}, u32[]{:S(2)}) async-start(f32[8,1,128]{2,1,0:T(1,128)} %get-tuple-element.12), calls=%async_computation.2 | async-start | bytes 8192 | tf_op jit(solution)/shard_map/all_to_all | solution.py:294
  51.5 6.9 %collective-permute-start.1 = (f32[24,128]{1,0:T(8,128)S(1)}, f32[24,128]{1,0:T(8,128)S(1)}, u32[]{:S(2)}, u32[]{:S(2)}) collective-permute-start(f32[24,128]{1,0:T(8,128)S(1)} %get-tuple-element.13), channel_id=1, source_target_pairs={{16,0},{32,16},{48,32},{64,48},{80,64},{96,80},{112,96},{128,112},... | collective-permute-start | bytes 36872 | tf_op jit(solution)/shard_map/ppermute | solution.py:296
  58.4 1.9 %collective-permute-start = (f32[24,128]{1,0:T(8,128)S(1)}, f32[24,128]{1,0:T(8,128)S(1)}, u32[]{:S(2)}, u32[]{:S(2)}) collective-permute-start(f32[24,128]{1,0:T(8,128)S(1)} %get-tuple-element.14), channel_id=1, source_target_pairs={{0,16},{16,32},{32,48},{48,64},{64,80},{80,96},{96,112},{112,128},... | collective-permute-start | bytes 36872 | tf_op jit(solution)/shard_map/ppermute | solution.py:295
  60.3 0.0 all-to-all-done.2.in_ref
  60.3 0.6 peak.1
  60.9 0.0 copy-start
  60.9 4.3 %all-to-all-start.3 = ((f32[8,1,128]{2,1,0:T(1,128)}), f32[8,1,128]{2,1,0:T(1,128)S(1)}, u32[]{:S(2)}, u32[]{:S(2)}) async-start(f32[8,1,128]{2,1,0:T(1,128)} %peak.1), calls=%async_computation.3 | async-start | bytes 8192 | tf_op jit(solution)/shard_map/all_to_all | solution.py:305
  65.2 0.0 collective-permute-done.1.after_ref
  65.2 0.9 %collective-permute-done.before_ref = f32[24,128]{1,0:T(8,128)S(1)} collective-permute-done((f32[24,128]{1,0:T(8,128)S(1)}, f32[24,128]{1,0:T(8,128)S(1)}, u32[]{:S(2)}, u32[]{:S(2)}) %collective-permute-start) | collective-permute-done | bytes 12320 | tf_op jit(solution)/shard_map/ppermute | solution.py:295
  66.2 0.0 copy-done
  66.2 0.6 change.1.change_ref
  66.8 5.0 %all-to-all-done.3.best_ref = f32[8,1,128]{2,1,0:T(1,128)S(1)} async-done(((f32[8,1,128]{2,1,0:T(1,128)}), f32[8,1,128]{2,1,0:T(1,128)S(1)}, u32[]{:S(2)}, u32[]{:S(2)}) %all-to-all-start.3) | async-done | bytes 4128 | tf_op jit(solution)/shard_map/all_to_all | solution.py:305
  71.8 0.7 finish.1
  (1 shorter events, 0.0 us)
Async XLA Ops:
  43.5 16.8 %all-to-all-start.2 = ((f32[8,1,128]{2,1,0:T(1,128)}), f32[8,1,128]{2,1,0:T(1,128)S(1)}, u32[]{:S(2)}, u32[]{:S(2)}) async-start(f32[8,1,128]{2,1,0:T(1,128)} %get-tuple-element.12), calls=%async_computation.2 | async-start | bytes 8192 | tf_op jit(solution)/shard_map/all_to_all | solution.py:294
  51.5 13.7 %collective-permute-start.1 = (f32[24,128]{1,0:T(8,128)S(1)}, f32[24,128]{1,0:T(8,128)S(1)}, u32[]{:S(2)}, u32[]{:S(2)}) collective-permute-start(f32[24,128]{1,0:T(8,128)S(1)} %get-tuple-element.13), channel_id=1, source_target_pairs={{16,0},{32,16},{48,32},{64,48},{80,64},{96,80},{112,96},{128,112},... | collective-permute-start | bytes 36872 | tf_op jit(solution)/shard_map/ppermute | solution.py:296
  58.4 7.8 %collective-permute-start = (f32[24,128]{1,0:T(8,128)S(1)}, f32[24,128]{1,0:T(8,128)S(1)}, u32[]{:S(2)}, u32[]{:S(2)}) collective-permute-start(f32[24,128]{1,0:T(8,128)S(1)} %get-tuple-element.14), channel_id=1, source_target_pairs={{0,16},{16,32},{32,48},{48,64},{64,80},{80,96},{96,112},{112,128},... | collective-permute-start | bytes 36872 | tf_op jit(solution)/shard_map/ppermute | solution.py:295
  60.9 5.2 %copy-start = (f32[8,128]{1,0:T(8,128)S(1)}, f32[8,128]{1,0:T(8,128)}, u32[]{:S(2)}) copy-start(f32[8,128]{1,0:T(8,128)} %get-tuple-element.11.pick_ref) | copy-start | bytes 12292
  60.9 10.8 %all-to-all-start.3 = ((f32[8,1,128]{2,1,0:T(1,128)}), f32[8,1,128]{2,1,0:T(1,128)S(1)}, u32[]{:S(2)}, u32[]{:S(2)}) async-start(f32[8,1,128]{2,1,0:T(1,128)} %peak.1), calls=%async_computation.3 | async-start | bytes 8192 | tf_op jit(solution)/shard_map/all_to_all | solution.py:305

commit v12 on v5

--- a/solution.py
+++ b/solution.py
@@ -284,9 +284,9 @@
     moved = lax.all_to_all(routed.reshape(count, SLOT, LANES), "curve", 0, 0, tiled=True)
     up = [(i, (i + 1) % segs) for i in range(segs)]
     down = [(j, i) for i, j in up]
+    moved, best = lax.optimization_barrier((moved, best))
     best = lax.all_to_all(best, SEG[1], 0, 0, tiled=True)
     before = lax.ppermute(moved[count - 1], SEG, up)
-    after = lax.ppermute(moved[0], SEG, down)
     best = pl.pallas_call(
         peak_kernel,
         out_shape=jax.ShapeDtypeStruct((along_x, 1, LANES), f32),
@@ -295,6 +295,8 @@
         compiler_params=params,
         name="peak",
     )(best)
+    best, first = lax.optimization_barrier((best, moved[0]))
+    after = lax.ppermute(first, SEG, down)
     best = lax.all_to_all(best, SEG[0], 0, 0, tiled=True)
     moved = moved.reshape(SLOT * count, LANES)
     change = pl.pallas_call(

time: 73 us -> 75.5 us (1.034)
  waiting for transfers between devices: 5.92 us -> 9.06 us
  starting transfers between devices: 21.1 us -> 20.1 us
    all_to_all x1, waiting for transfers between devices: 0.01 us -> 3.16 us  [local(): best = lax.all_to_all(best, SEG[1], 0, 0, tiled=True)]
    ppermute x1, starting transfers between devices: 6.88 us -> 4.6 us  [local(): after = lax.ppermute(first, SEG, down)]
    ppermute x1, starting transfers between devices: 1.92 us -> 3.35 us  [local(): before = lax.ppermute(moved[count - 1], SEG, up)]
    ppermute x1, waiting for transfers between devices: 0.9 us -> 0.01 us  [local(): before = lax.ppermute(moved[count - 1], SEG, up)]
    all_to_all x1, waiting for transfers between devices: 5.01 us -> 5.9 us  [local(): best = lax.all_to_all(best, SEG[0], 0, 0, tiled=True)]
where the time goes in v12:
time: 75.5 us; the launch traced here: 74.6 us
  blocking collectives  40.8 us (54%)
  starting transfers between devices  20.1 us (27%)
  waiting for transfers between devices  9.06 us (12%)
  Pallas kernels  4.57 us (6%)
    all_to_all x1, blocking collectives, local(): lax.all_to_all(sent.reshape(count, SLOT, LANES), 'curve', 0, 0, tiled=True)  27.8 us
    all_to_all x1, blocking collectives, local(): lax.all_to_all(routed.reshape(count, SLOT, LANES), 'curve', 0, 0, tiled=T...  13 us
    all_to_all x1, starting transfers between devices, local(): best = lax.all_to_all(best, SEG[1], 0, 0, tiled=True)  7.99 us
    all_to_all x1, waiting for transfers between devices, local(): best = lax.all_to_all(best, SEG[0], 0, 0, tiled=True)  5.9 us
    ppermute x1, starting transfers between devices, local(): after = lax.ppermute(first, SEG, down)  4.6 us
    all_to_all x1, starting transfers between devices, local(): best = lax.all_to_all(best, SEG[0], 0, 0, tiled=True)  4.18 us
    ppermute x1, starting transfers between devices, local(): before = lax.ppermute(moved[count - 1], SEG, up)  3.35 us
    all_to_all x1, waiting for transfers between devices, local(): best = lax.all_to_all(best, SEG[1], 0, 0, tiled=True)  3.16 us
  transfers between devices with their start and end apart: 4, of which 2 were waited for; matrix products, arithmetic and copies ran while one was open for 0% of the time, Pallas kernels for 2%

profile of v12, /device:TPU:1, one launch (start us, length us, event | category | flops | bytes accessed | tf_op | source)
XLA Modules:
  0.0 74.6 jit_solution(10585939987000452213)
XLA Ops:
  0.0 1.8 %pack.1 = (f32[384,128]{1,0:T(8,128)}, f32[8,128]{1,0:T(8,128)}) custom-call(s32[2]{0:T(128)} %slot_hbm.1, s32[2,6]{1,0:T(2,128)} %near_hbm.1, f32[2,5,16,256]{3,2,1,0:T(8,128)} %state_hbm.1), custom_call_target="tpu_custom_call" | custom-call | tf_op jit(solution)/shard_map/pack/pallas_call | solution.py:259
  1.8 27.8 %all_to_all.20 = f32[16,24,128]{2,1,0:T(8,128)S(1)} all-to-all(f32[16,24,128]{2,1,0:T(8,128)} %bitcast.12), channel_id=1, replica_groups=mesh['seg_x'=8,'seg_z'=8,'curve'=16] {'curve'}, dimensions={0} | all-to-all | bytes 393216 | tf_op jit(solution)/shard_map/all_to_all | solution.py:272
  29.7 0.8 %route.1 = (f32[384,128]{1,0:T(8,128)S(1)}, f32[8,1,128]{2,1,0:T(1,128)}) custom-call(f32[384,128]{1,0:T(8,128)S(1)} %bitcast.10), custom_call_target="tpu_custom_call" | custom-call | tf_op jit(solution)/shard_map/route/pallas_call | solution.py:273
  30.5 13.0 %all_to_all.21 = f32[16,24,128]{2,1,0:T(8,128)S(1)} all-to-all(f32[16,24,128]{2,1,0:T(8,128)S(1)} %bitcast.11), channel_id=1, replica_groups=mesh['seg_x'=8,'seg_z'=8,'curve'=16] {'curve'}, dimensions={0} | all-to-all | bytes 393216 | tf_op jit(solution)/shard_map/all_to_all | solution.py:284
  43.5 8.0 %all-to-all-start.2 = ((f32[8,1,128]{2,1,0:T(1,128)}), f32[8,1,128]{2,1,0:T(1,128)S(1)}, u32[]{:S(2)}, u32[]{:S(2)}) async-start(f32[8,1,128]{2,1,0:T(1,128)} %get-tuple-element.18), calls=%async_computation.2 | async-start | bytes 8192 | tf_op jit(solution)/shard_map/all_to_all | solution.py:288
  51.5 3.4 %collective-permute-start = (f32[24,128]{1,0:T(8,128)S(1)}, f32[24,128]{1,0:T(8,128)S(1)}, u32[]{:S(2)}, u32[]{:S(2)}) collective-permute-start(f32[24,128]{1,0:T(8,128)S(1)} %get-tuple-element.22), channel_id=1, source_target_pairs={{0,16},{16,32},{32,48},{48,64},{64,80},{80,96},{96,112},{112,128},... | collective-permute-start | bytes 36872 | tf_op jit(solution)/shard_map/ppermute | solution.py:289
  54.8 3.2 %all-to-all-done.2.in_ref = f32[8,1,128]{2,1,0:T(1,128)S(1)} async-done(((f32[8,1,128]{2,1,0:T(1,128)}), f32[8,1,128]{2,1,0:T(1,128)S(1)}, u32[]{:S(2)}, u32[]{:S(2)}) %all-to-all-start.2) | async-done | bytes 4128 | tf_op jit(solution)/shard_map/all_to_all | solution.py:288
  58.0 0.6 peak.1
  58.6 0.0 copy-start
  58.6 4.6 %collective-permute-start.1 = (f32[24,128]{1,0:T(8,128)S(1)}, f32[24,128]{1,0:T(8,128)S(1)}, u32[]{:S(2)}, u32[]{:S(2)}) collective-permute-start(f32[24,128]{1,0:T(8,128)S(1)} %get-tuple-element.19), channel_id=1, source_target_pairs={{16,0},{32,16},{48,32},{64,48},{80,64},{96,80},{112,96},{128,112},... | collective-permute-start | bytes 36872 | tf_op jit(solution)/shard_map/ppermute | solution.py:299
  63.2 4.2 %all-to-all-start.3 = ((f32[8,1,128]{2,1,0:T(1,128)}), f32[8,1,128]{2,1,0:T(1,128)S(1)}, u32[]{:S(2)}, u32[]{:S(2)}) async-start(f32[8,1,128]{2,1,0:T(1,128)} %peak.1), calls=%async_computation.3 | async-start | bytes 8192 | tf_op jit(solution)/shard_map/all_to_all | solution.py:300
  67.4 0.0 collective-permute-done.before_ref
  67.4 0.0 collective-permute-done.1.after_ref
  67.4 0.0 copy-done
  67.4 0.6 change.1.change_ref
  68.0 5.9 %all-to-all-done.3.best_ref = f32[8,1,128]{2,1,0:T(1,128)S(1)} async-done(((f32[8,1,128]{2,1,0:T(1,128)}), f32[8,1,128]{2,1,0:T(1,128)S(1)}, u32[]{:S(2)}, u32[]{:S(2)}) %all-to-all-start.3) | async-done | bytes 4128 | tf_op jit(solution)/shard_map/all_to_all | solution.py:300
  73.9 0.7 finish.1
  (1 shorter events, 0.0 us)
Async XLA Ops:
  43.5 14.5 %all-to-all-start.2 = ((f32[8,1,128]{2,1,0:T(1,128)}), f32[8,1,128]{2,1,0:T(1,128)S(1)}, u32[]{:S(2)}, u32[]{:S(2)}) async-start(f32[8,1,128]{2,1,0:T(1,128)} %get-tuple-element.18), calls=%async_computation.2 | async-start | bytes 8192 | tf_op jit(solution)/shard_map/all_to_all | solution.py:288
  51.5 15.9 %collective-permute-start = (f32[24,128]{1,0:T(8,128)S(1)}, f32[24,128]{1,0:T(8,128)S(1)}, u32[]{:S(2)}, u32[]{:S(2)}) collective-permute-start(f32[24,128]{1,0:T(8,128)S(1)} %get-tuple-element.22), channel_id=1, source_target_pairs={{0,16},{16,32},{32,48},{48,64},{64,80},{80,96},{96,112},{112,128},... | collective-permute-start | bytes 36872 | tf_op jit(solution)/shard_map/ppermute | solution.py:289
  58.6 8.8 %copy-start = (f32[8,128]{1,0:T(8,128)S(1)}, f32[8,128]{1,0:T(8,128)}, u32[]{:S(2)}) copy-start(f32[8,128]{1,0:T(8,128)} %get-tuple-element.17.pick_ref) | copy-start | bytes 12292
  58.6 8.8 %collective-permute-start.1 = (f32[24,128]{1,0:T(8,128)S(1)}, f32[24,128]{1,0:T(8,128)S(1)}, u32[]{:S(2)}, u32[]{:S(2)}) collective-permute-start(f32[24,128]{1,0:T(8,128)S(1)} %get-tuple-element.19), channel_id=1, source_target_pairs={{16,0},{32,16},{48,32},{64,48},{80,64},{96,80},{112,96},{128,112},... | collective-permute-start | bytes 36872 | tf_op jit(solution)/shard_map/ppermute | solution.py:299
  63.2 10.7 %all-to-all-start.3 = ((f32[8,1,128]{2,1,0:T(1,128)}), f32[8,1,128]{2,1,0:T(1,128)S(1)}, u32[]{:S(2)}, u32[]{:S(2)}) async-start(f32[8,1,128]{2,1,0:T(1,128)} %peak.1), calls=%async_computation.3 | async-start | bytes 8192 | tf_op jit(solution)/shard_map/all_to_all | solution.py:300

commit v13 on v5

--- a/solution.py
+++ b/solution.py
@@ -174,7 +174,7 @@
     out_ref[...] = jnp.broadcast_to(best, out_ref.shape)
 
 
-def change_kernel(pick_ref, in_ref, before_ref, after_ref, out_ref):
+def change_kernel(pick_ref, in_ref, after_ref, before_ref, out_ref):
     count = in_ref.shape[0] // SLOT
 
     def rows_of(row):
@@ -285,8 +285,8 @@
     up = [(i, (i + 1) % segs) for i in range(segs)]
     down = [(j, i) for i, j in up]
     best = lax.all_to_all(best, SEG[1], 0, 0, tiled=True)
+    after = lax.ppermute(moved[0], SEG, down)
     before = lax.ppermute(moved[count - 1], SEG, up)
-    after = lax.ppermute(moved[0], SEG, down)
     best = pl.pallas_call(
         peak_kernel,
         out_shape=jax.ShapeDtypeStruct((along_x, 1, LANES), f32),
@@ -304,7 +304,7 @@
         out_specs=vmem,
         compiler_params=params,
         name="change",
-    )(pick, moved, before, after)
+    )(pick, moved, after, before)
     return pl.pallas_call(
         finish_kernel,
         out_shape=jax.ShapeDtypeStruct(state.shape, f32),

time: 73 us -> 75 us (1.027)
  starting transfers between devices: 21.1 us -> 23.2 us
    all_to_all x1, starting transfers between devices: 4.31 us -> 6.42 us  [local(): best = lax.all_to_all(best, SEG[0], 0, 0, tiled=True)]
    ppermute x1, starting transfers between devices: 6.88 us -> 5.44 us  [local(): after = lax.ppermute(moved[0], SEG, down)]
    ppermute x1, starting transfers between devices: 1.92 us -> 3.35 us  [local(): before = lax.ppermute(moved[count - 1], SEG, up)]
    ppermute x1, waiting for transfers between devices: 0.9 us -> 0.01 us  [local(): before = lax.ppermute(moved[count - 1], SEG, up)]
    all_to_all x1, waiting for transfers between devices: 5.01 us -> 5.9 us  [local(): best = lax.all_to_all(best, SEG[0], 0, 0, tiled=True)]
  transfers between devices with their start and end apart: 4 -> 4, of which waited for: 2 -> 1; matrix products, arithmetic and copies ran while one was open for 0% -> 0% of each run, Pallas kernels for 2% -> 2%
where the time goes in v13:
time: 75 us; the launch traced here: 74.6 us
  blocking collectives  40.8 us (54%)
  starting transfers between devices  23.2 us (31%)
  waiting for transfers between devices  5.91 us (8%)
  Pallas kernels  4.57 us (6%)
    all_to_all x1, blocking collectives, local(): lax.all_to_all(sent.reshape(count, SLOT, LANES), 'curve', 0, 0, tiled=True)  27.8 us
    all_to_all x1, blocking collectives, local(): lax.all_to_all(routed.reshape(count, SLOT, LANES), 'curve', 0, 0, tiled=T...  13 us
    all_to_all x1, starting transfers between devices, local(): best = lax.all_to_all(best, SEG[1], 0, 0, tiled=True)  7.99 us
    all_to_all x1, starting transfers between devices, local(): best = lax.all_to_all(best, SEG[0], 0, 0, tiled=True)  6.42 us
    all_to_all x1, waiting for transfers between devices, local(): best = lax.all_to_all(best, SEG[0], 0, 0, tiled=True)  5.9 us
    ppermute x1, starting transfers between devices, local(): after = lax.ppermute(moved[0], SEG, down)  5.44 us
    ppermute x1, starting transfers between devices, local(): before = lax.ppermute(moved[count - 1], SEG, up)  3.35 us
    pallas_call x1, Pallas kernels, local(): pl.pallas_call(pack_kernel, out_shape=(jax.ShapeDtypeStruct((SLOT * count...  1.83 us
  transfers between devices with their start and end apart: 4, of which 1 were waited for; matrix products, arithmetic and copies ran while one was open for 0% of the time, Pallas kernels for 2%

profile of v13, /device:TPU:1, one launch (start us, length us, event | category | flops | bytes accessed | tf_op | source)
XLA Modules:
  0.0 74.6 jit_solution(11947494515171977254)
XLA Ops:
  0.0 1.8 %pack.1 = (f32[384,128]{1,0:T(8,128)}, f32[8,128]{1,0:T(8,128)}) custom-call(s32[2]{0:T(128)} %slot_hbm.1, s32[2,6]{1,0:T(2,128)} %near_hbm.1, f32[2,5,16,256]{3,2,1,0:T(8,128)} %state_hbm.1), custom_call_target="tpu_custom_call" | custom-call | tf_op jit(solution)/shard_map/pack/pallas_call | solution.py:259
  1.8 27.8 %all_to_all.20 = f32[16,24,128]{2,1,0:T(8,128)S(1)} all-to-all(f32[16,24,128]{2,1,0:T(8,128)} %bitcast.12), channel_id=1, replica_groups=mesh['seg_x'=8,'seg_z'=8,'curve'=16] {'curve'}, dimensions={0} | all-to-all | bytes 393216 | tf_op jit(solution)/shard_map/all_to_all | solution.py:272
  29.7 0.8 %route.1 = (f32[384,128]{1,0:T(8,128)S(1)}, f32[8,1,128]{2,1,0:T(1,128)}) custom-call(f32[384,128]{1,0:T(8,128)S(1)} %bitcast.10), custom_call_target="tpu_custom_call" | custom-call | tf_op jit(solution)/shard_map/route/pallas_call | solution.py:273
  30.5 13.0 %all_to_all.21 = f32[16,24,128]{2,1,0:T(8,128)S(1)} all-to-all(f32[16,24,128]{2,1,0:T(8,128)S(1)} %bitcast.11), channel_id=1, replica_groups=mesh['seg_x'=8,'seg_z'=8,'curve'=16] {'curve'}, dimensions={0} | all-to-all | bytes 393216 | tf_op jit(solution)/shard_map/all_to_all | solution.py:284
  43.5 8.0 %all-to-all-start.2 = ((f32[8,1,128]{2,1,0:T(1,128)}), f32[8,1,128]{2,1,0:T(1,128)S(1)}, u32[]{:S(2)}, u32[]{:S(2)}) async-start(f32[8,1,128]{2,1,0:T(1,128)} %get-tuple-element.12), calls=%async_computation.2 | async-start | bytes 8192 | tf_op jit(solution)/shard_map/all_to_all | solution.py:287
  51.5 3.4 %collective-permute-start.1 = (f32[24,128]{1,0:T(8,128)S(1)}, f32[24,128]{1,0:T(8,128)S(1)}, u32[]{:S(2)}, u32[]{:S(2)}) collective-permute-start(f32[24,128]{1,0:T(8,128)S(1)} %get-tuple-element.13), channel_id=1, source_target_pairs={{0,16},{16,32},{32,48},{48,64},{64,80},{80,96},{96,112},{112,128},... | collective-permute-start | bytes 36872 | tf_op jit(solution)/shard_map/ppermute | solution.py:289
  54.8 5.4 %collective-permute-start = (f32[24,128]{1,0:T(8,128)S(1)}, f32[24,128]{1,0:T(8,128)S(1)}, u32[]{:S(2)}, u32[]{:S(2)}) collective-permute-start(f32[24,128]{1,0:T(8,128)S(1)} %get-tuple-element.14), channel_id=1, source_target_pairs={{16,0},{32,16},{48,32},{64,48},{80,64},{96,80},{112,96},{128,112},... | collective-permute-start | bytes 36872 | tf_op jit(solution)/shard_map/ppermute | solution.py:288
  60.3 0.0 all-to-all-done.2.in_ref
  60.3 0.6 peak.1
  60.9 0.0 copy-start
  60.9 6.4 %all-to-all-start.3 = ((f32[8,1,128]{2,1,0:T(1,128)}), f32[8,1,128]{2,1,0:T(1,128)S(1)}, u32[]{:S(2)}, u32[]{:S(2)}) async-start(f32[8,1,128]{2,1,0:T(1,128)} %peak.1), calls=%async_computation.3 | async-start | bytes 8192 | tf_op jit(solution)/shard_map/all_to_all | solution.py:298
  67.3 0.0 collective-permute-done.1.before_ref
  67.3 0.0 collective-permute-done.after_ref
  67.3 0.0 copy-done
  67.3 0.6 change.1.change_ref
  68.0 5.9 %all-to-all-done.3.best_ref = f32[8,1,128]{2,1,0:T(1,128)S(1)} async-done(((f32[8,1,128]{2,1,0:T(1,128)}), f32[8,1,128]{2,1,0:T(1,128)S(1)}, u32[]{:S(2)}, u32[]{:S(2)}) %all-to-all-start.3) | async-done | bytes 4128 | tf_op jit(solution)/shard_map/all_to_all | solution.py:298
  73.8 0.7 finish.1
  (1 shorter events, 0.0 us)
Async XLA Ops:
  43.5 16.8 %all-to-all-start.2 = ((f32[8,1,128]{2,1,0:T(1,128)}), f32[8,1,128]{2,1,0:T(1,128)S(1)}, u32[]{:S(2)}, u32[]{:S(2)}) async-start(f32[8,1,128]{2,1,0:T(1,128)} %get-tuple-element.12), calls=%async_computation.2 | async-start | bytes 8192 | tf_op jit(solution)/shard_map/all_to_all | solution.py:287
  51.5 15.8 %collective-permute-start.1 = (f32[24,128]{1,0:T(8,128)S(1)}, f32[24,128]{1,0:T(8,128)S(1)}, u32[]{:S(2)}, u32[]{:S(2)}) collective-permute-start(f32[24,128]{1,0:T(8,128)S(1)} %get-tuple-element.13), channel_id=1, source_target_pairs={{0,16},{16,32},{32,48},{48,64},{64,80},{80,96},{96,112},{112,128},... | collective-permute-start | bytes 36872 | tf_op jit(solution)/shard_map/ppermute | solution.py:289
  54.8 12.5 %collective-permute-start = (f32[24,128]{1,0:T(8,128)S(1)}, f32[24,128]{1,0:T(8,128)S(1)}, u32[]{:S(2)}, u32[]{:S(2)}) collective-permute-start(f32[24,128]{1,0:T(8,128)S(1)} %get-tuple-element.14), channel_id=1, source_target_pairs={{16,0},{32,16},{48,32},{64,48},{80,64},{96,80},{112,96},{128,112},... | collective-permute-start | bytes 36872 | tf_op jit(solution)/shard_map/ppermute | solution.py:288
  60.9 6.4 %copy-start = (f32[8,128]{1,0:T(8,128)S(1)}, f32[8,128]{1,0:T(8,128)}, u32[]{:S(2)}) copy-start(f32[8,128]{1,0:T(8,128)} %get-tuple-element.11.pick_ref) | copy-start | bytes 12292
  60.9 12.9 %all-to-all-start.3 = ((f32[8,1,128]{2,1,0:T(1,128)}), f32[8,1,128]{2,1,0:T(1,128)S(1)}, u32[]{:S(2)}, u32[]{:S(2)}) async-start(f32[8,1,128]{2,1,0:T(1,128)} %peak.1), calls=%async_computation.3 | async-start | bytes 8192 | tf_op jit(solution)/shard_map/all_to_all | solution.py:298
